TPU v7x, 128 devices: a whole 4x4x4 slice. The times are simulated.
128 devices in a mesh: lon: 16 (over y, z_hi, core), lat: 8 (over z_lo, x).
Axes of the slice: x: 4, y: 4, z: 4 (z_hi: 2, z_lo: 2; z = z_hi * 2 + z_lo), core: 2. Of those that a mesh axis runs over, the one named last changes fastest.
Arguments:
- tracers: float32 [2, 4, 512, 4096], P(None, None, 'lat', 'lon'), may hold values from -6 to 6
- velocity: float32 [3, 4, 512, 4096], P(None, None, 'lat', 'lon'), may hold values from -0.15 to 0.15
- slopes: float32 [2, 4, 512, 4096], P(None, None, 'lat', 'lon'), may hold values from -1 to 1
- diffusivity: float32 [4, 512, 4096], P(None, 'lat', 'lon'), may hold values from 0.02 to 0.1
- sea_mask: int32 [4, 512, 4096], P(None, 'lat', 'lon'), may hold values from 0 to 1, as said below
Outputs:
- tracers_next: float32 [2, 4, 512, 4096], P(None, None, 'lat', 'lon')
Inputs may be any that keep to these rules, and one draw needn't show every extreme that they name: `sea_mask`: 1 marks sea and 0 land; the sea cells of each column are its top levels.
All inputs are finite; a program needn't handle non-finite values.
Results may differ from a plain program's by a relative error of at most 0.0003.
Values sent between devices are 32-bit elements; how exact they have to be, the bound alone decides.
No kernel may reach another device: no remote copies, remote signals or barrier semaphores. Data moves between devices by JAX's collectives and lax.ppermute only.
A program may use at most 64 MiB of HBM per device.

v0:
```python
import jax
import jax.numpy as jnp
from jax import lax
from jax.sharding import PartitionSpec as P


def with_halo(cells, sides, width, closed):
    for axis, dim in sides:
        count = lax.axis_size(axis)
        ends = count if closed else count - 1
        head = lax.slice_in_dim(cells, 0, width, axis=dim)
        tail = lax.slice_in_dim(cells, cells.shape[dim] - width, cells.shape[dim], axis=dim)
        cells = jnp.concatenate(
            [
                lax.ppermute(tail, axis, [(i, (i + 1) % count) for i in range(ends)]),
                cells,
                lax.ppermute(head, axis, [((i + 1) % count, i) for i in range(ends)]),
            ],
            axis=dim,
        )
    return cells


def from_partner(block, axis, apart):
    count = lax.axis_size(axis)
    route = []
    for low in range(count):
        high = low | 1 << apart
        if high != low and high < count:
            route += [(low, high), (high, low)]
    return lax.ppermute(block, axis, route)


def minmod(first, second):
    smaller = jnp.minimum(jnp.abs(first), jnp.abs(second))
    agreeing = first * second > 0.0
    return jnp.where(agreeing, jnp.where(first > 0.0, smaller, -smaller), 0.0)


def take(array, start, count, direction):
    return lax.slice_in_dim(array, start, start + count, axis=direction)


def face_flux(tracer, marker, speed_cells, direction):
    length = tracer.shape[direction]
    open_face = take(marker, 0, length - 1, direction) * take(marker, 1, length - 1, direction)
    steps = (
        take(tracer, 1, length - 1, direction) - take(tracer, 0, length - 1, direction)
    ) * open_face
    speeds = (
        0.5
        * (
            take(speed_cells, 0, length - 1, direction)
            + take(speed_cells, 1, length - 1, direction)
        )
        * open_face
    )
    speed = take(speeds, 1, length - 3, direction)
    centre = take(steps, 1, length - 3, direction)
    upwind = jnp.where(
        speed >= 0.0, take(steps, 0, length - 3, direction), take(steps, 2, length - 3, direction)
    )
    flux = (
        jnp.maximum(speed, 0.0) * take(tracer, 1, length - 3, direction)
        + jnp.minimum(speed, 0.0) * take(tracer, 2, length - 3, direction)
        + 0.5 * jnp.abs(speed) * (1.0 - jnp.abs(speed)) * minmod(upwind, centre)
    )
    return take(flux, 1, length - 4, direction) - take(flux, 0, length - 4, direction)


def trimmed(array, margin):
    return array[:, margin : array.shape[1] - margin, margin : array.shape[2] - margin]


def advect(tracer, marker, eastward, northward, downward):
    across_x = face_flux(tracer, marker, eastward, 2)[:, 2:-2, :]
    across_y = face_flux(tracer, marker, northward, 1)[:, :, 2:-2]
    levels = ((2, 2), (0, 0), (0, 0))
    across_z = face_flux(
        jnp.pad(trimmed(tracer, 2), levels),
        jnp.pad(trimmed(marker, 2), levels),
        jnp.pad(downward, levels),
        0,
    )
    return (trimmed(tracer, 2) - across_x - across_y - across_z) * trimmed(marker, 2)


def diffuse(tracer, slope_east, slope_north, diffusivity, marker):
    levels = ((1, 1), (0, 0), (0, 0))
    padded = jnp.pad(tracer, levels)
    padded_marker = jnp.pad(marker, levels)
    step_z = (padded[1:] - padded[:-1]) * padded_marker[1:] * padded_marker[:-1]
    centre_z = 0.5 * (step_z[:-1] + step_z[1:])
    open_x = marker[:, :, 1:] * marker[:, :, :-1]
    step_x = (tracer[:, :, 1:] - tracer[:, :, :-1]) * open_x
    centre_x = 0.5 * (step_x[:, :, :-1] + step_x[:, :, 1:])
    open_y = marker[:, 1:, :] * marker[:, :-1, :]
    step_y = (tracer[:, 1:, :] - tracer[:, :-1, :]) * open_y
    centre_y = 0.5 * (step_y[:, :-1, :] + step_y[:, 1:, :])
    flux_x = (
        -0.5
        * (diffusivity[:, :, 1:] + diffusivity[:, :, :-1])
        * (
            step_x
            + 0.5
            * (slope_east[:, :, 1:] + slope_east[:, :, :-1])
            * 0.5
            * (centre_z[:, :, 1:] + centre_z[:, :, :-1])
        )
        * open_x
    )
    flux_y = (
        -0.5
        * (diffusivity[:, 1:, :] + diffusivity[:, :-1, :])
        * (
            step_y
            + 0.5
            * (slope_north[:, 1:, :] + slope_north[:, :-1, :])
            * 0.5
            * (centre_z[:, 1:, :] + centre_z[:, :-1, :])
        )
        * open_y
    )
    across_x = flux_x[:, 1:-1, 1:] - flux_x[:, 1:-1, :-1]
    across_y = flux_y[:, 1:, 1:-1] - flux_y[:, :-1, 1:-1]
    inner_x = centre_x[:, 1:-1, :]
    inner_y = centre_y[:, :, 1:-1]
    east_in = trimmed(slope_east, 1)
    north_in = trimmed(slope_north, 1)
    kappa_in = trimmed(diffusivity, 1)
    marker_in = trimmed(marker, 1)
    east_face = 0.5 * (east_in[1:] + east_in[:-1])
    north_face = 0.5 * (north_in[1:] + north_in[:-1])
    flux_z = (
        -0.5
        * (kappa_in[1:] + kappa_in[:-1])
        * (
            east_face * 0.5 * (inner_x[1:] + inner_x[:-1])
            + north_face * 0.5 * (inner_y[1:] + inner_y[:-1])
            + (east_face * east_face + north_face * north_face) * step_z[1:-1, 1:-1, 1:-1]
        )
        * marker_in[1:]
        * marker_in[:-1]
    )
    flux_z = jnp.pad(flux_z, levels)
    across_z = flux_z[1:] - flux_z[:-1]
    return (trimmed(tracer, 1) - across_x - across_y - across_z) * marker_in


def extend(stacked, margin, signs):
    lon_side = with_halo(stacked, (("lon", 3),), margin, True)
    both = with_halo(lon_side, (("lat", 2),), margin, False)
    rows = stacked.shape[2]
    partner = lon_side[:, :, rows - margin :, :]
    for swap_bit in range(lax.axis_size("lon").bit_length() - 1):
        partner = from_partner(partner, "lon", swap_bit)
    partner = jnp.flip(partner, (2, 3))
    folded = partner * signs[:, None, None, None]
    at_top = lax.axis_index("lat") == lax.axis_size("lat") - 1
    upper = jnp.where(at_top, folded, both[:, :, rows + margin :, :])
    return jnp.concatenate([both[:, :, : rows + margin, :], upper], axis=2)


def shards(tracers, velocity, slopes, diffusivity, sea_mask):
    marker = sea_mask.astype(jnp.float32)
    five_signs = jnp.array([1.0, 1.0, -1.0, -1.0, 1.0], jnp.float32)
    first = jnp.concatenate([tracers, velocity[:2], marker[None]], axis=0)
    wide = extend(first, 2, five_signs)
    advected = jnp.stack(
        [advect(wide[member], wide[4], wide[2], wide[3], velocity[2]) for member in range(2)]
    )
    second = jnp.concatenate([advected, slopes, diffusivity[None]], axis=0)
    narrow = extend(second, 1, five_signs)
    marker_rim = trimmed(wide[4], 1)
    result = [
        diffuse(narrow[member], narrow[2], narrow[3], narrow[4], marker_rim) for member in range(2)
    ]
    return jnp.stack(result)


def solution(mesh):
    return jax.shard_map(
        shards,
        mesh=mesh,
        in_specs=(
            P(None, None, "lat", "lon"),
            P(None, None, "lat", "lon"),
            P(None, None, "lat", "lon"),
            P(None, "lat", "lon"),
            P(None, "lat", "lon"),
        ),
        out_specs=P(None, None, "lat", "lon"),
        check_vma=False,
    )
```

profile of v0, /device:TPU:30, one launch (start us, length us, event | category | flops | bytes accessed | tf_op | source)
XLA Modules:
  0.0 81.9 jit_solution(1584564009322124099)
XLA Ops:
  0.0 1.0 %convert_bitcast_fusion = f32[1,4,64,256]{3,2,1,0:T(8,128)S(1)} fusion(s32[4,64,256]{2,1,0:T(8,128)} %param.10), kind=kLoop, calls=%fused_computation.207 | loop fusion | flops 65536 | bytes 524288 | tf_op jit(solution)/shard_map/broadcast_in_dim | solution.py:167
  1.0 1.1 %slice.610 = f32[2,4,64,256]{3,2,1,0:T(8,128)S(1)} slice(f32[3,4,64,256]{3,2,1,0:T(8,128)} %param.7), slice={[0:2], [0:4], [0:64], [0:256]} | slice | bytes 1048576 | tf_op jit(solution)/shard_map/slice | solution.py:167
  2.1 1.2 %pad_maximum_fusion.2 = f32[5,4,64,256]{3,2,1,0:T(8,128)S(1)} fusion(f32[1,4,64,256]{3,2,1,0:T(8,128)S(1)} %convert_bitcast_fusion, f32[2,4,64,256]{3,2,1,0:T(8,128)S(1)} %slice.610, f32[2,4,64,256]{3,2,1,0:T(8,128)} %param.6), kind=kLoop, calls=%fused_computation.2 | loop fusion | flops 655360 | bytes 2621440 | tf_op jit(solution)/shard_map/concatenate | solution.py:167
  3.7 3.5 %collective-permute-start.1 = (f32[5,4,64,2]{2,1,3,0:T(4,128)S(1)}, f32[5,4,64,2]{2,1,3,0:T(4,128)S(1)}, u32[]{:S(2)}, u32[]{:S(2)}) collective-permute-start(f32[5,4,64,2]{2,1,3,0:T(4,128)S(1)} %copy.38), channel_id=1, source_target_pairs={{8,0},{16,8},{24,16},{32,24},{40,32},{48,40},{56,48},{64,56},{72,6... | collective-permute-start | bytes 30728 | tf_op jit(solution)/shard_map/ppermute | solution.py:17
  7.6 1.2 %collective-permute-done.1 = f32[5,4,64,2]{2,1,3,0:T(4,128)S(1)} collective-permute-done((f32[5,4,64,2]{2,1,3,0:T(4,128)S(1)}, f32[5,4,64,2]{2,1,3,0:T(4,128)S(1)}, u32[]{:S(2)}, u32[]{:S(2)}) %collective-permute-start.1) | collective-permute-done | bytes 10272 | tf_op jit(solution)/shard_map/ppermute | solution.py:17
  9.0 4.1 %collective-permute-done = f32[5,4,64,2]{2,1,3,0:T(4,128)S(1)} collective-permute-done((f32[5,4,64,2]{2,1,3,0:T(4,128)S(1)}, f32[5,4,64,2]{2,1,3,0:T(4,128)S(1)}, u32[]{:S(2)}, u32[]{:S(2)}) %collective-permute-start) | collective-permute-done | bytes 10272 | tf_op jit(solution)/shard_map/ppermute | solution.py:15
  13.8 1.2 %collective-permute-done.3 = f32[5,4,2,260]{3,1,2,0:T(4,128)S(1)} collective-permute-done((f32[5,4,2,260]{3,1,2,0:T(4,128)S(1)}, f32[5,4,2,260]{3,1,2,0:T(4,128)S(1)}, u32[]{:S(2)}, u32[]{:S(2)}) %collective-permute-start.3) | collective-permute-done | bytes 41632 | tf_op jit(solution)/shard_map/ppermute | solution.py:31
  15.1 1.1 %collective-permute-start.4 = (f32[5,4,2,260]{3,1,2,0:T(4,128)S(1)}, f32[5,4,2,260]{3,1,2,0:T(4,128)S(1)}, u32[]{:S(2)}, u32[]{:S(2)}) collective-permute-start(f32[5,4,2,260]{3,1,2,0:T(4,128)S(1)} %collective-permute-done.3), channel_id=1, source_target_pairs={{0,16},{16,0},{8,24},{24,8},{32,48},{48,32},{40,56},{56,40},{64,80... | collective-permute-start | bytes 124808 | tf_op jit(solution)/shard_map/ppermute | solution.py:31
  16.2 4.6 %collective-permute-done.4 = f32[5,4,2,260]{3,1,2,0:T(4,128)S(1)} collective-permute-done((f32[5,4,2,260]{3,1,2,0:T(4,128)S(1)}, f32[5,4,2,260]{3,1,2,0:T(4,128)S(1)}, u32[]{:S(2)}, u32[]{:S(2)}) %collective-permute-start.4) | collective-permute-done | bytes 41632 | tf_op jit(solution)/shard_map/ppermute | solution.py:31
  21.2 2.8 %collective-permute-start.2 = (f32[5,4,2,260]{3,1,2,0:T(4,128)S(1)}, f32[5,4,2,260]{3,1,2,0:T(4,128)S(1)}, u32[]{:S(2)}, u32[]{:S(2)}) collective-permute-start(f32[5,4,2,260]{3,1,2,0:T(4,128)S(1)} %copy.41), channel_id=1, source_target_pairs={{0,1},{1,2},{2,3},{3,4},{4,5},{5,6},{6,7},{8,9},{9,10},{10,11},{11... | collective-permute-start | bytes 124808 | tf_op jit(solution)/shard_map/ppermute | solution.py:15
  24.1 3.0 %collective-permute-start.7 = (f32[5,4,2,260]{3,1,2,0:T(4,128)S(1)}, f32[5,4,2,260]{3,1,2,0:T(4,128)S(1)}, u32[]{:S(2)}, u32[]{:S(2)}) collective-permute-start(f32[5,4,2,260]{3,1,2,0:T(4,128)S(1)} %copy.43), channel_id=1, source_target_pairs={{1,0},{2,1},{3,2},{4,3},{5,4},{6,5},{7,6},{9,8},{10,9},{11,10},{12... | collective-permute-start | bytes 124808 | tf_op jit(solution)/shard_map/ppermute | solution.py:17
  27.1 4.8 %collective-permute-start.6 = (f32[5,4,2,260]{3,1,2,0:T(4,128)S(1)}, f32[5,4,2,260]{3,1,2,0:T(4,128)S(1)}, u32[]{:S(2)}, u32[]{:S(2)}) collective-permute-start(f32[5,4,2,260]{3,1,2,0:T(4,128)S(1)} %collective-permute-done.5), channel_id=1, source_target_pairs={{0,64},{64,0},{8,72},{72,8},{16,80},{80,16},{24,88},{88,24},{32,96... | collective-permute-start | bytes 124808 | tf_op jit(solution)/shard_map/ppermute | solution.py:31
  31.9 1.0 %slice_bitcast_fusion.10 = f32[4,64,256]{2,1,0:T(8,128)S(1)} fusion(f32[3,4,64,256]{3,2,1,0:T(8,128)} %param.7), kind=kLoop, calls=%fused_computation.206 | loop fusion | bytes 524288 | tf_op jit(solution)/shard_map/squeeze | solution.py:170
  33.0 1.2 %collective-permute-done.6 = f32[5,4,2,260]{3,1,2,0:T(4,128)S(1)} collective-permute-done((f32[5,4,2,260]{3,1,2,0:T(4,128)S(1)}, f32[5,4,2,260]{3,1,2,0:T(4,128)S(1)}, u32[]{:S(2)}, u32[]{:S(2)}) %collective-permute-start.6) | collective-permute-done | bytes 41632 | tf_op jit(solution)/shard_map/ppermute | solution.py:31
  34.6 0.9 %pad_maximum_fusion = f32[5,4,68,260]{3,2,1,0:T(8,128)S(1)} fusion(f32[5,4,2,260]{3,2,1,0:T(2,128)S(1)} %copy.45, f32[5,4,64,2]{3,2,1,0:T(8,128)S(1)} %copy.40, f32[1,4,64,256]{3,2,1,0:T(8,128)S(1)} %convert_bitcast_fusion, f32[2,4,64,256]{3,2,1,0:T(8,128)S(1)} %slice.610, f32[2,4,64,256]{3,2,1,0:T(8,128)S(1)} %copy-done, f32[5,4,64,2]{3,2,1,0:T(8,128)S(1)} %copy.39, ...), kind=kLoop, calls=%fused_computation | loop fusion | flops 2121600 | bytes 2828800 | tf_op jit(solution)/shard_map/concatenate | solution.py:161
  36.6 0.9 %fusion.16 = (f32[4,65,260]{2,1,0:T(8,128)S(1)}, f32[4,65,260]{2,1,0:T(8,128)S(1)}) fusion(f32[4,68,260]{2,1,0:T(8,128)S(1)} %get-tuple-element.34, f32[4,67,260]{2,1,0:T(8,128)S(1)} %get-tuple-element.17, f32[4,67,260]{2,1,0:T(8,128)S(1)} %get-tuple-element.18, f32[4,67,260]{2,1,0:T(8,128)S(1)} %get-tuple-element.62, ...), kind=kLoop, calls=%fused_computation.45 | loop fusion | flops 2704000 | bytes 4056000 | tf_op jit(solution)/shard_map/add | solution.py:64
  37.9 1.3 %fusion.13 = (f32[4,68,257]{2,1,0:T(8,128)S(1)}, f32[4,68,257]{2,1,0:T(8,128)S(1)}) fusion(f32[4,68,260]{2,1,0:T(8,128)S(1)} %get-tuple-element.34, f32[4,68,259]{2,1,0:T(8,128)S(1)} %get-tuple-element.15, f32[4,68,259]{2,1,0:T(8,128)S(1)} %get-tuple-element.16, f32[4,68,259]{2,1,0:T(8,128)S(1)} %get-tuple-element.58, ...), kind=kLoop, calls=%fused_computation.42 | loop fusion | flops 2796160 | bytes 4194240 | tf_op jit(solution)/shard_map/add | solution.py:64
  43.7 4.1 %collective-permute-done.8 = f32[5,4,64,1]{2,1,3,0:T(4,128)S(1)} collective-permute-done((f32[5,4,64,1]{2,1,3,0:T(4,128)S(1)}, f32[5,4,64,1]{2,1,3,0:T(4,128)S(1)}, u32[]{:S(2)}, u32[]{:S(2)}) %collective-permute-start.8) | collective-permute-done | bytes 5152 | tf_op jit(solution)/shard_map/ppermute | solution.py:15
  48.4 1.2 %collective-permute-done.11 = f32[5,4,1,258]{3,1,2,0:T(4,128)S(1)} collective-permute-done((f32[5,4,1,258]{3,1,2,0:T(4,128)S(1)}, f32[5,4,1,258]{3,1,2,0:T(4,128)S(1)}, u32[]{:S(2)}, u32[]{:S(2)}) %collective-permute-start.11) | collective-permute-done | bytes 20672 | tf_op jit(solution)/shard_map/ppermute | solution.py:31
  50.3 4.8 %collective-permute-done.12 = f32[5,4,1,258]{3,1,2,0:T(4,128)S(1)} collective-permute-done((f32[5,4,1,258]{3,1,2,0:T(4,128)S(1)}, f32[5,4,1,258]{3,1,2,0:T(4,128)S(1)}, u32[]{:S(2)}, u32[]{:S(2)}) %collective-permute-start.12) | collective-permute-done | bytes 20672 | tf_op jit(solution)/shard_map/ppermute | solution.py:31
  55.4 4.9 %collective-permute-start.10 = (f32[5,4,1,258]{3,1,2,0:T(4,128)S(1)}, f32[5,4,1,258]{3,1,2,0:T(4,128)S(1)}, u32[]{:S(2)}, u32[]{:S(2)}) collective-permute-start(f32[5,4,1,258]{3,1,2,0:T(4,128)S(1)} %copy.50), channel_id=1, source_target_pairs={{0,1},{1,2},{2,3},{3,4},{4,5},{5,6},{6,7},{8,9},{9,10},{10,11},{11... | collective-permute-start | bytes 61928 | tf_op jit(solution)/shard_map/ppermute | solution.py:15
  60.4 4.4 %collective-permute-start.14 = (f32[5,4,1,258]{3,1,2,0:T(4,128)S(1)}, f32[5,4,1,258]{3,1,2,0:T(4,128)S(1)}, u32[]{:S(2)}, u32[]{:S(2)}) collective-permute-start(f32[5,4,1,258]{3,1,2,0:T(4,128)S(1)} %collective-permute-done.13), channel_id=1, source_target_pairs={{0,64},{64,0},{8,72},{72,8},{16,80},{80,16},{24,88},{88,24},{32,96... | collective-permute-start | bytes 61928 | tf_op jit(solution)/shard_map/ppermute | solution.py:31
  65.4 1.9 %collective-permute-start.15 = (f32[5,4,1,258]{3,1,2,0:T(4,128)}, f32[5,4,1,258]{3,1,2,0:T(4,128)}, u32[]{:S(2)}, u32[]{:S(2)}) collective-permute-start(f32[5,4,1,258]{3,1,2,0:T(4,128)} %copy.52), channel_id=1, source_target_pairs={{1,0},{2,1},{3,2},{4,3},{5,4},{6,5},{7,6},{9,8},{10,9},{11,10},{12... | collective-permute-start | bytes 61928 | tf_op jit(solution)/shard_map/ppermute | solution.py:17
  68.8 1.6 %reverse.1 = f32[5,4,1,384]{3,1,2,0:T(4,128)S(1)} reverse(f32[5,4,1,384]{3,1,2,0:T(4,128)} %bitcast.39), dimensions={2,3} | reverse | bytes 61440
  70.4 3.3 %collective-permute-done.15 = f32[5,4,1,258]{3,1,2,0:T(4,128)} collective-permute-done((f32[5,4,1,258]{3,1,2,0:T(4,128)}, f32[5,4,1,258]{3,1,2,0:T(4,128)}, u32[]{:S(2)}, u32[]{:S(2)}) %collective-permute-start.15) | collective-permute-done | bytes 20672 | tf_op jit(solution)/shard_map/ppermute | solution.py:17
  73.6 0.8 %multiply_select_fusion.1 = f32[5,4,1,258]{3,1,2,0:T(4,128)S(1)} fusion(f32[5,4,1,258]{3,1,2,0:T(4,128)} %collective-permute-done.15, f32[5]{0:T(128)S(1)} %copy-done.4, pred[]{:T(512)S(6)} %eq.4, f32[5,4,1,384]{3,1,2,0:T(4,128)S(1)} %reverse.1), kind=kLoop, calls=%fused_computation.248 | loop fusion | flops 10320 | bytes 61941 | tf_op jit(solution)/shard_map/jit(_where)/select_n | solution.py:160
  74.5 1.6 %pad_maximum_fusion.1 = f32[5,4,66,258]{3,2,1,0:T(8,128)S(1)} fusion(f32[5,4,1,258]{3,2,1,0:T(1,128)S(1)} %copy.54, f32[5,4,64,1]{3,2,1,0:T(8,128)S(1)} %copy.49, f32[1,4,64,256]{3,2,1,0:T(8,128)S(1)} %bitcast.37, f32[2,4,64,256]{3,2,1,0:T(8,128)S(1)} %copy-done.1, f32[1,4,64,256]{3,2,1,0:T(8,128)S(1)} %get-tuple-element.50, ...), kind=kLoop, calls=%fused_computation.1 | loop fusion | flops 2383920 | bytes 2724480 | tf_op jit(solution)/shard_map/concatenate | solution.py:161
  77.0 0.8 fusion.44
  79.0 0.7 fusion.108
  79.7 0.7 fusion.101
  80.4 0.8 fusion.79
  81.1 0.8 %pad_maximum_fusion.4 = f32[2,4,64,256]{3,2,1,0:T(8,128)} fusion(f32[1,4,64,256]{3,2,1,0:T(8,128)S(1)} %get-tuple-element.46, f32[1,4,64,256]{3,2,1,0:T(8,128)S(1)} %get-tuple-element.45), kind=kLoop, calls=%fused_computation.32 | loop fusion | flops 131072 | bytes 1048576 | tf_op jit(solution)/shard_map/stack | solution.py:178
  (76 shorter events, 14.2 us)
Async XLA Ops:
  3.2 10.3 %copy-start = (f32[2,4,64,256]{3,2,1,0:T(8,128)S(1)}, f32[2,4,64,256]{3,2,1,0:T(8,128)}, u32[]{:S(2)}) copy-start(f32[2,4,64,256]{3,2,1,0:T(8,128)} %param.6) | copy-start | bytes 1572868
  3.7 5.0 %collective-permute-start.1 = (f32[5,4,64,2]{2,1,3,0:T(4,128)S(1)}, f32[5,4,64,2]{2,1,3,0:T(4,128)S(1)}, u32[]{:S(2)}, u32[]{:S(2)}) collective-permute-start(f32[5,4,64,2]{2,1,3,0:T(4,128)S(1)} %copy.38), channel_id=1, source_target_pairs={{8,0},{16,8},{24,16},{32,24},{40,32},{48,40},{56,48},{64,56},{72,6... | collective-permute-start | bytes 30728 | tf_op jit(solution)/shard_map/ppermute | solution.py:17
  7.5 5.7 %collective-permute-start = (f32[5,4,64,2]{2,1,3,0:T(4,128)S(1)}, f32[5,4,64,2]{2,1,3,0:T(4,128)S(1)}, u32[]{:S(2)}, u32[]{:S(2)}) collective-permute-start(f32[5,4,64,2]{2,1,3,0:T(4,128)S(1)} %copy.37), channel_id=1, source_target_pairs={{0,8},{8,16},{16,24},{24,32},{32,40},{40,48},{48,56},{56,64},{64,7... | collective-permute-start | bytes 30728 | tf_op jit(solution)/shard_map/ppermute | solution.py:15
  9.0 25.4 %copy-start.4 = (f32[5]{0:T(128)S(1)}, f32[5]{0:T(128)}, u32[]{:S(2)}) copy-start(f32[5]{0:T(128)} %constant.15.clone) | copy-start | bytes 64
  13.7 1.3 %collective-permute-start.3 = (f32[5,4,2,260]{3,1,2,0:T(4,128)S(1)}, f32[5,4,2,260]{3,1,2,0:T(4,128)S(1)}, u32[]{:S(2)}, u32[]{:S(2)}) collective-permute-start(f32[5,4,2,260]{3,1,2,0:T(4,128)S(1)} %copy.41), channel_id=1, source_target_pairs={{0,8},{8,0},{16,24},{24,16},{32,40},{40,32},{48,56},{56,48},{64,72... | collective-permute-start | bytes 124808 | tf_op jit(solution)/shard_map/ppermute | solution.py:31
  15.1 5.7 %collective-permute-start.4 = (f32[5,4,2,260]{3,1,2,0:T(4,128)S(1)}, f32[5,4,2,260]{3,1,2,0:T(4,128)S(1)}, u32[]{:S(2)}, u32[]{:S(2)}) collective-permute-start(f32[5,4,2,260]{3,1,2,0:T(4,128)S(1)} %collective-permute-done.3), channel_id=1, source_target_pairs={{0,16},{16,0},{8,24},{24,8},{32,48},{48,32},{40,56},{56,40},{64,80... | collective-permute-start | bytes 124808 | tf_op jit(solution)/shard_map/ppermute | solution.py:31
  20.8 6.3 %collective-permute-start.5 = (f32[5,4,2,260]{3,1,2,0:T(4,128)S(1)}, f32[5,4,2,260]{3,1,2,0:T(4,128)S(1)}, u32[]{:S(2)}, u32[]{:S(2)}) collective-permute-start(f32[5,4,2,260]{3,1,2,0:T(4,128)S(1)} %collective-permute-done.4), channel_id=1, source_target_pairs={{0,32},{32,0},{8,40},{40,8},{16,48},{48,16},{24,56},{56,24},{64,96... | collective-permute-start | bytes 124808 | tf_op jit(solution)/shard_map/ppermute | solution.py:31
  21.2 11.7 %collective-permute-start.2 = (f32[5,4,2,260]{3,1,2,0:T(4,128)S(1)}, f32[5,4,2,260]{3,1,2,0:T(4,128)S(1)}, u32[]{:S(2)}, u32[]{:S(2)}) collective-permute-start(f32[5,4,2,260]{3,1,2,0:T(4,128)S(1)} %copy.41), channel_id=1, source_target_pairs={{0,1},{1,2},{2,3},{3,4},{4,5},{5,6},{6,7},{8,9},{9,10},{10,11},{11... | collective-permute-start | bytes 124808 | tf_op jit(solution)/shard_map/ppermute | solution.py:15
  24.1 10.4 %collective-permute-start.7 = (f32[5,4,2,260]{3,1,2,0:T(4,128)S(1)}, f32[5,4,2,260]{3,1,2,0:T(4,128)S(1)}, u32[]{:S(2)}, u32[]{:S(2)}) collective-permute-start(f32[5,4,2,260]{3,1,2,0:T(4,128)S(1)} %copy.43), channel_id=1, source_target_pairs={{1,0},{2,1},{3,2},{4,3},{5,4},{6,5},{7,6},{9,8},{10,9},{11,10},{12... | collective-permute-start | bytes 124808 | tf_op jit(solution)/shard_map/ppermute | solution.py:17
  27.1 7.0 %collective-permute-start.6 = (f32[5,4,2,260]{3,1,2,0:T(4,128)S(1)}, f32[5,4,2,260]{3,1,2,0:T(4,128)S(1)}, u32[]{:S(2)}, u32[]{:S(2)}) collective-permute-start(f32[5,4,2,260]{3,1,2,0:T(4,128)S(1)} %collective-permute-done.5), channel_id=1, source_target_pairs={{0,64},{64,0},{8,72},{72,8},{16,80},{80,16},{24,88},{88,24},{32,96... | collective-permute-start | bytes 124808 | tf_op jit(solution)/shard_map/ppermute | solution.py:31
  40.2 1.0 %copy-start.1 = (f32[2,4,64,256]{3,2,1,0:T(8,128)S(1)}, f32[2,4,64,256]{3,2,1,0:T(8,128)}, u32[]{:S(2)}) copy-start(f32[2,4,64,256]{3,2,1,0:T(8,128)} %param.8) | copy-start | bytes 1572868
  40.2 1.1 %copy-start.2 = (f32[4,64,256]{2,1,0:T(8,128)S(1)}, f32[4,64,256]{2,1,0:T(8,128)}, u32[]{:S(2)}) copy-start(f32[4,64,256]{2,1,0:T(8,128)} %param.9) | copy-start | bytes 786436
  41.9 1.4 %collective-permute-start.9 = (f32[5,4,64,1]{2,1,3,0:T(4,128)S(1)}, f32[5,4,64,1]{2,1,3,0:T(4,128)S(1)}, u32[]{:S(2)}, u32[]{:S(2)}) collective-permute-start(f32[5,4,64,1]{2,1,3,0:T(4,128)S(1)} %copy.47), channel_id=1, source_target_pairs={{8,0},{16,8},{24,16},{32,24},{40,32},{48,40},{56,48},{64,56},{72,6... | collective-permute-start | bytes 15368 | tf_op jit(solution)/shard_map/ppermute | solution.py:17
  42.2 5.6 %collective-permute-start.8 = (f32[5,4,64,1]{2,1,3,0:T(4,128)S(1)}, f32[5,4,64,1]{2,1,3,0:T(4,128)S(1)}, u32[]{:S(2)}, u32[]{:S(2)}) collective-permute-start(f32[5,4,64,1]{2,1,3,0:T(4,128)S(1)} %copy.46), channel_id=1, source_target_pairs={{0,8},{8,16},{16,24},{24,32},{32,40},{40,48},{48,56},{56,64},{64,7... | collective-permute-start | bytes 15368 | tf_op jit(solution)/shard_map/ppermute | solution.py:15
  48.3 1.3 %collective-permute-start.11 = (f32[5,4,1,258]{3,1,2,0:T(4,128)S(1)}, f32[5,4,1,258]{3,1,2,0:T(4,128)S(1)}, u32[]{:S(2)}, u32[]{:S(2)}) collective-permute-start(f32[5,4,1,258]{3,1,2,0:T(4,128)S(1)} %copy.50), channel_id=1, source_target_pairs={{0,8},{8,0},{16,24},{24,16},{32,40},{40,32},{48,56},{56,48},{64,72... | collective-permute-start | bytes 61928 | tf_op jit(solution)/shard_map/ppermute | solution.py:31
  49.6 5.4 %collective-permute-start.12 = (f32[5,4,1,258]{3,1,2,0:T(4,128)S(1)}, f32[5,4,1,258]{3,1,2,0:T(4,128)S(1)}, u32[]{:S(2)}, u32[]{:S(2)}) collective-permute-start(f32[5,4,1,258]{3,1,2,0:T(4,128)S(1)} %collective-permute-done.11), channel_id=1, source_target_pairs={{0,16},{16,0},{8,24},{24,8},{32,48},{48,32},{40,56},{56,40},{64,80... | collective-permute-start | bytes 61928 | tf_op jit(solution)/shard_map/ppermute | solution.py:31
  55.0 5.3 %collective-permute-start.13 = (f32[5,4,1,258]{3,1,2,0:T(4,128)S(1)}, f32[5,4,1,258]{3,1,2,0:T(4,128)S(1)}, u32[]{:S(2)}, u32[]{:S(2)}) collective-permute-start(f32[5,4,1,258]{3,1,2,0:T(4,128)S(1)} %collective-permute-done.12), channel_id=1, source_target_pairs={{0,32},{32,0},{8,40},{40,8},{16,48},{48,16},{24,56},{56,24},{64,96... | collective-permute-start | bytes 61928 | tf_op jit(solution)/shard_map/ppermute | solution.py:31
  55.4 12.1 %collective-permute-start.10 = (f32[5,4,1,258]{3,1,2,0:T(4,128)S(1)}, f32[5,4,1,258]{3,1,2,0:T(4,128)S(1)}, u32[]{:S(2)}, u32[]{:S(2)}) collective-permute-start(f32[5,4,1,258]{3,1,2,0:T(4,128)S(1)} %copy.50), channel_id=1, source_target_pairs={{0,1},{1,2},{2,3},{3,4},{4,5},{5,6},{6,7},{8,9},{9,10},{10,11},{11... | collective-permute-start | bytes 61928 | tf_op jit(solution)/shard_map/ppermute | solution.py:15
  60.4 7.8 %collective-permute-start.14 = (f32[5,4,1,258]{3,1,2,0:T(4,128)S(1)}, f32[5,4,1,258]{3,1,2,0:T(4,128)S(1)}, u32[]{:S(2)}, u32[]{:S(2)}) collective-permute-start(f32[5,4,1,258]{3,1,2,0:T(4,128)S(1)} %collective-permute-done.13), channel_id=1, source_target_pairs={{0,64},{64,0},{8,72},{72,8},{16,80},{80,16},{24,88},{88,24},{32,96... | collective-permute-start | bytes 61928 | tf_op jit(solution)/shard_map/ppermute | solution.py:31
  65.4 8.2 %collective-permute-start.15 = (f32[5,4,1,258]{3,1,2,0:T(4,128)}, f32[5,4,1,258]{3,1,2,0:T(4,128)}, u32[]{:S(2)}, u32[]{:S(2)}) collective-permute-start(f32[5,4,1,258]{3,1,2,0:T(4,128)} %copy.52), channel_id=1, source_target_pairs={{1,0},{2,1},{3,2},{4,3},{5,4},{6,5},{7,6},{9,8},{10,9},{11,10},{12... | collective-permute-start | bytes 61928 | tf_op jit(solution)/shard_map/ppermute | solution.py:17
  68.2 0.6 copy-start.3
where the time goes:
time: 82.5 us; the launch traced here: 81.9 us
  starting transfers between devices  28.9 us (35%)
  waiting for transfers between devices  26.3 us (32%)
  other arithmetic  16 us (19%)
  local copies, waits for them, and re-layouts  10.3 us (12%)
    ppermute x8, waiting for transfers between devices, from_partner(): return lax.ppermute(block, axis, route)  13 us
    ppermute x8, starting transfers between devices, from_partner(): return lax.ppermute(block, axis, route)  12 us
    ppermute x4, starting transfers between devices, with_halo(): lax.ppermute(head, axis, [((i + 1) % count, i) for i in range(ends)])  8.52 us
    ppermute x4, starting transfers between devices, with_halo(): lax.ppermute(tail, axis, [(i, (i + 1) % count) for i in range(ends)])  8.37 us
    ppermute x4, waiting for transfers between devices, with_halo(): lax.ppermute(tail, axis, [(i, (i + 1) % count) for i in range(ends)])  8.28 us
    ppermute x4, waiting for transfers between devices, with_halo(): lax.ppermute(head, axis, [((i + 1) % count, i) for i in range(ends)])  5.02 us
    unnamed x12, local copies, waits for them, and re-layouts  3 us
    add x3, other arithmetic, face_flux(): jnp.maximum(speed, 0.0) * take(tracer, 1, length - 3, direction)  2.64 us
  transfers between devices with their start and end apart: 16, of which 10 were waited for; matrix products, arithmetic and copies ran while one was open for 7% of the time, Pallas kernels for 0%

commit v1 on v0

v1 whole, which is shorter than its diff:
```python
import jax
import jax.numpy as jnp
from jax import lax
from jax.experimental import pallas as pl
from jax.experimental.pallas import tpu as pltpu
from jax.sharding import PartitionSpec as P


ROWS = 64
LANES = 128
F32 = jnp.float32
VMEM = pl.BlockSpec(memory_space=pltpu.VMEM)
LIMIT = 48 * 1024 * 1024
FIELDS = ("c", "m", "u", "v", "w", "sx", "k", "sy")
SIDE = FIELDS[:7]


def lane_of():
    return lax.broadcasted_iota(jnp.int32, (8, LANES), 1)


def low_of():
    return lax.broadcasted_iota(jnp.int32, (8, LANES), 0) < 4


def twice_low(x):
    return jnp.where(low_of(), x, pltpu.roll(x, 4, 0))


def twice_high(x):
    return jnp.where(low_of(), pltpu.roll(x, 4, 0), x)


def load_rows(halves, row):
    out = []
    for tracer, velocity, slope, kappa, mask in halves:
        eight = lambda ref, start: ref.reshape(ref.shape[0] * ROWS, LANES)[pl.ds(start + row, 8, stride=ROWS), :]
        four = lambda ref: ref.reshape(ref.shape[0] * ROWS, LANES)[pl.ds(row, 4, stride=ROWS), :]
        out.append(
            {
                "c": eight(tracer, 0),
                "uv": eight(velocity, 0),
                "vw": eight(velocity, 4 * ROWS),
                "s": eight(slope, 0),
                "k": four(kappa),
                "m": four(mask).astype(F32),
            }
        )
    return out


def halves_of(refs):
    return [refs[0::2], refs[1::2]]


def pack_kernel(*refs):
    halves, packed = halves_of(refs[:10]), refs[10]
    lane, low = lane_of(), low_of()
    second = jnp.logical_or(lane == 1, lane == 126)

    def group(g, carry):
        total = jnp.zeros((8, LANES), F32)
        for part in range(8):
            left, right = load_rows(halves, part * 8 + g)
            rim = {n: jnp.where(lane[: left[n].shape[0]] < 64, left[n], right[n]) for n in left}
            mk = jnp.concatenate([rim["m"], rim["k"]], axis=0)
            mku = jnp.where(jnp.logical_and(second, jnp.logical_not(low)), pltpu.roll(rim["uv"], 4, 0), mk)
            sw = jnp.where(low, rim["s"], rim["vw"])
            slots = jnp.where(lane < 14, pltpu.roll(rim["uv"], 13, 1), pltpu.roll(sw, 15, 1))
            slots = jnp.where(lane < 12, pltpu.roll(mku, 9, 1), slots)
            slots = jnp.where(lane < 6, pltpu.roll(rim["c"], 3, 1), slots)
            if part:
                slots = pltpu.roll(slots, 16 * part, 1)
                total = jnp.where(lane < 16 * part, total, slots)
            else:
                total = slots
        packed[g] = total
        return carry

    lax.fori_loop(0, 8, group, 0)


def rows_kernel(*refs):
    halves, outs = halves_of(refs[:10]), dict(zip(FIELDS, refs[10:]))

    def row_group(block, carry):
        for inner in range(4):
            row = block * 4 + inner
            for half, values in enumerate(load_rows(halves, row)):
                full = {
                    "c": values["c"],
                    "m": jnp.concatenate([values["m"]] * 2, axis=0),
                    "u": twice_low(values["uv"]),
                    "v": twice_low(values["vw"]),
                    "w": twice_high(values["vw"]),
                    "sx": twice_low(values["s"]),
                    "sy": twice_high(values["s"]),
                    "k": jnp.concatenate([values["k"]] * 2, axis=0),
                }
                for name in FIELDS:
                    outs[name][row, :, half * LANES : (half + 1) * LANES] = full[name]
        return carry

    lax.fori_loop(0, ROWS // 4, row_group, 0)


def edge_kernel(*refs):
    from_far, from_near = refs[0], refs[1]
    fields = dict(zip(FIELDS, refs[2:10]))
    rim, send_a, send_b = refs[10:]
    lane, low = lane_of(), low_of()
    lon, lat = lax.axis_index("lon"), lax.axis_index("lat")
    slot = lane % 16
    west = (slot < 3) | ((slot >= 6) & (slot < 9)) | (slot == 12) | (slot == 14)
    far_is_west = jnp.broadcast_to(lon % 2, (8, LANES)) == 0
    take_far = west == far_is_west
    for g in range(8):
        rim[g] = jnp.where(take_far, from_far[g], from_near[g])

    def message(top):
        row = lambda q: jnp.where(top, ROWS - 1 - q, q)
        part = lambda name, q, h: fields[name][row(q), :, h * LANES : (h + 1) * LANES]
        pair = lambda n1, q1, n2, q2: [jnp.where(low, part(n1, q1, h), part(n2, q2, h)) for h in range(2)]
        tiles = [[part("c", q, h) for h in range(2)] for q in range(3)]
        tiles += [pair("m", 0, "v", 0), pair("m", 1, "v", 1), pair("m", 2, "u", 0), pair("w", 0, "sy", 0)]
        corners = [pltpu.roll(rim[jnp.where(top, 7 - q, q)], jnp.where(top, 16, 0), 1) for q in range(3)]
        return tiles, [part("k", 0, h) for h in range(2)], corners

    def store(ref, tiles, kappa, corners):
        for i, tile in enumerate(tiles):
            for h in range(2):
                ref[i, :, h * LANES : (h + 1) * LANES] = tile[h]
        packed = corners[0]
        for q in (1, 2):
            packed = jnp.where(lane < 16 * q, packed, pltpu.roll(corners[q], 16 * q, 1))
        ref[7, :, :LANES] = jnp.where(low, kappa[0], pltpu.roll(packed, 4, 0))
        ref[7, :, LANES:] = jnp.where(low, kappa[1], packed)

    even = lat % 2 == 0
    store(send_a, *message(even))
    folds = lat == lax.axis_size("lat") - 1

    @pl.when(jnp.logical_not(folds))
    def _():
        store(send_b, *message(jnp.logical_not(even)))

    @pl.when(folds)
    def _():
        tiles, kappa, corners = message(True)
        backward = LANES - 1 - lane
        flip = lambda x, index: jnp.take_along_axis(x, index, axis=1, mode="promise_in_bounds")
        flip_tile = lambda tile: [flip(tile[1], backward), flip(tile[0], backward)]
        sign = jnp.where(low, 1.0, -1.0)
        turned = [flip_tile(tile) for tile in tiles]
        turned = turned[:3] + [[sign * x for x in tile] for tile in turned[3:]]
        index = jnp.where(lane < 6, 5 - lane, jnp.where(lane < 12, 17 - lane, jnp.where(lane < 14, 25 - lane, 29 - lane)))
        index = jnp.where(lane < 16, index, lane)
        uv = (lane == 12) | (lane == 13) | (((lane == 7) | (lane == 10)) & jnp.logical_not(low))
        corner_sign = jnp.where(uv, -1.0, 1.0)
        store(send_b, turned, flip_tile(kappa), [corner_sign * flip(x, index) for x in corners])


def decode_rim(vector, part):
    lane = lane_of()
    at = lambda first: pltpu.roll(vector, lax.rem(2 * LANES - 16 * part - first, LANES), 1)
    mku, uv, sw = at(9), at(13), at(15)
    second = jnp.logical_or(lane == 1, lane == 126)
    high = twice_high(mku)
    return {
        "c": at(3),
        "m": twice_low(mku),
        "u": jnp.where(second, high, twice_low(uv)),
        "v": twice_high(uv),
        "w": twice_high(sw),
        "sx": twice_low(sw),
        "k": high,
    }


def plus(tiles):
    last = lane_of() == LANES - 1
    turned = [pltpu.roll(t, LANES - 1, 1) for t in tiles]
    return [jnp.where(last, turned[(i + 1) % 3], turned[i]) for i in range(3)]


def minus(tiles, count=3):
    first = lane_of() == 0
    turned = [pltpu.roll(t, 1, 1) for t in tiles]
    return [jnp.where(first, turned[(i + 2) % 3], turned[i]) for i in range(count)]


def each(function, *lists):
    return [function(*values) for values in zip(*lists)]


def below(x):
    return pltpu.roll(x, 7, 0)


def above(x):
    return pltpu.roll(x, 1, 0)


def face_flux(here, there, speed, back, step, ahead):
    positive = speed >= 0.0
    upwind = jnp.where(positive, back, ahead)
    size = jnp.abs(speed)
    limited = jnp.maximum(jnp.minimum(upwind, step), 0.0) + jnp.minimum(jnp.maximum(upwind, step), 0.0)
    return speed * jnp.where(positive, here, there) + 0.5 * (size - size * size) * limited


def not_bottom():
    return lax.broadcasted_iota(jnp.int32, (8, LANES), 0) % 4 != 3


def open_below(marker):
    return jnp.where(not_bottom(), marker * below(marker), 0.0)


def face_speed(one, two, opened):
    return 0.5 * (one + two) * opened


def advect_rows(get, first, count):
    c = {j: get("c", first + j) for j in range(-2, count + 2)}
    m = {j: get("m", first + j) for j in range(-2, count + 2)}
    v = {j: get("v", first + j) for j in range(-1, count + 1)}
    opened = {j: each(jnp.multiply, m[j], m[j + 1]) for j in range(-2, count + 1)}
    step = {j: each(lambda a, b, o: (b - a) * o, c[j], c[j + 1], opened[j]) for j in range(-2, count + 1)}
    flux = {}
    for j in range(-1, count):
        speed = each(face_speed, v[j], v[j + 1], opened[j])
        flux[j] = each(face_flux, c[j], c[j + 1], speed, step[j - 1], step[j], step[j + 1])
    result = []
    for j in range(count):
        east = plus(c[j])
        opened_x = each(jnp.multiply, m[j], plus(m[j]))
        u = get("u", first + j)
        speed = each(face_speed, u, plus(u), opened_x)
        step_x = each(lambda a, b, o: (b - a) * o, c[j], east, opened_x)
        flux_x = each(face_flux, c[j], east, speed, minus(step_x), step_x, plus(step_x))
        total = each(lambda f, g, a, b: (f - g) + (a - b), flux_x, minus(flux_x), flux[j], flux[j - 1])
        w = get("w", first + j)

        def finish(value, marker, down, across):
            opened_z = open_below(marker)
            under = below(value)
            step_z = (under - value) * opened_z
            speed_z = face_speed(down, below(down), opened_z)
            flux_z = face_flux(value, under, speed_z, above(step_z), step_z, below(step_z))
            return (value - across - (flux_z - above(flux_z))) * marker

        result.append(each(finish, c[j], m[j], w, total))
    return result


def diffuse_rows(get, first, count):
    a = {j: get("a", first + j) for j in range(-1, count + 1)}
    m = {j: get("m", first + j) for j in range(-1, count + 1)}
    k = {j: get("k", first + j) for j in range(-1, count + 1)}
    sy = {j: get("sy", first + j) for j in range(-1, count + 1)}
    step_z, twice_z = {}, {}
    for j in range(-1, count + 1):
        wide = 3 if 0 <= j < count else 2
        step_z[j] = each(lambda x, o: (below(x) - x) * open_below(o), a[j][:wide], m[j])
        twice_z[j] = each(lambda x: above(x) + x, step_z[j])
    step_y, flux_y = {}, {}
    for j in range(-1, count):
        opened = each(jnp.multiply, m[j][:2], m[j + 1][:2])
        step_y[j] = each(lambda x, y, o: (y - x) * o, a[j][:2], a[j + 1][:2], opened)
        flux_y[j] = each(
            lambda k1, k2, o, s, s1, s2, z1, z2: 0.5 * (k1 + k2) * o * (s + 0.125 * (s1 + s2) * (z1 + z2)),
            k[j], k[j + 1], opened, step_y[j], sy[j], sy[j + 1], twice_z[j], twice_z[j + 1],
        )
    result = []
    for j in range(count):
        sx = get("sx", first + j)
        opened = each(jnp.multiply, m[j], plus(m[j]))
        step_x = each(lambda x, y, o: (y - x) * o, a[j], plus(a[j]), opened)
        flux_x = each(
            lambda k1, k2, o, s, s1, s2, z1, z2: 0.5 * (k1 + k2) * o * (s + 0.125 * (s1 + s2) * (z1 + z2)),
            k[j], plus(k[j]), opened, step_x, sx, plus(sx), twice_z[j], plus(twice_z[j]),
        )
        twice_x = each(jnp.add, step_x, minus(step_x, 2))
        twice_y = each(jnp.add, step_y[j - 1], step_y[j])
        total = each(lambda f, g, p, q: (f - g) + (p - q), flux_x, minus(flux_x, 2), flux_y[j], flux_y[j - 1])

        def finish(value, marker, kappa, east, north, tx, ty, sz, across):
            face_east, face_north = 0.5 * (east + below(east)), 0.5 * (north + below(north))
            flux_z = (
                0.5 * (kappa + below(kappa)) * open_below(marker)
                * (0.25 * (face_east * (tx + below(tx)) + face_north * (ty + below(ty)))
                   + (face_east * face_east + face_north * face_north) * sz)
            )
            return (value + across + (flux_z - above(flux_z))) * marker

        result.append(each(finish, a[j][:2], m[j], k[j], sx, sy[j], twice_x, twice_y, step_z[j], total))
    return result


def tiles_of(ref, row, count):
    return [ref[row, :, t * LANES : (t + 1) * LANES] for t in range(count)]


def interior_kernel(*refs):
    fields, rim = dict(zip(FIELDS, refs[:8])), refs[8]
    sides = dict(zip(SIDE, refs[9:16]))
    advected, out = refs[16:]

    def spread(g, carry):
        for part in range(8):
            row = part * 8 + g
            for name, value in decode_rim(rim[g], part).items():
                sides[name][row] = value
        return carry

    lax.fori_loop(0, 8, spread, 0)

    def get(name, row):
        if name == "a":
            return tiles_of(advected, row, 3)
        if name == "sy":
            return tiles_of(fields[name], row, 2)
        return tiles_of(fields[name], row, 2) + [sides[name][row]]

    def advect_block(block, carry):
        first = 2 + 4 * block
        for j, tiles in enumerate(advect_rows(get, first, 4)):
            for t in range(3):
                advected[first + j, :, t * LANES : (t + 1) * LANES] = tiles[t]
        return carry

    lax.fori_loop(0, 15, advect_block, 0)

    def diffuse_block(block, carry):
        first = 3 + 2 * block
        for j, tiles in enumerate(diffuse_rows(get, first, 2)):
            for t in range(2):
                out[first + j, :, t * LANES : (t + 1) * LANES] = tiles[t]
        return carry

    lax.fori_loop(0, 29, diffuse_block, 0)


def rim_kernel(*refs):
    got_a, got_b = refs[0], refs[1]
    fields = dict(zip(FIELDS, refs[2:10]))
    sides = dict(zip(SIDE, refs[10:17]))
    advected, inner, out, edges, sems = refs[17:]
    middle = pltpu.make_async_copy
    copies = [middle(inner.at[8:56, i], out.at[i, 8:56], sems.at[i]) for i in range(8)]
    for copy in copies:
        copy.start()
    low = low_of()
    lat = lax.axis_index("lat")
    even = jnp.broadcast_to(lat % 2, (8, LANES)) == 0
    floor = jnp.broadcast_to(lat, (8, LANES)) == 0

    def halo(is_north):
        def tile(i, h):
            a = got_a[i, :, h * LANES : (h + 1) * LANES]
            b = got_b[i, :, h * LANES : (h + 1) * LANES]
            if is_north:
                return jnp.where(even, a, b)
            return jnp.where(floor, 0.0, jnp.where(even, b, a))

        tiles = [[tile(i, h) for h in range(2)] for i in range(8)]
        high = lambda i: [twice_high(x) for x in tiles[i]]
        below_four = lambda i: [twice_low(x) for x in tiles[i]]
        corner = jnp.where(low, pltpu.roll(tiles[7][0], 4, 0), tiles[7][1])
        rows = []
        for q in range(3):
            side = decode_rim(corner, q)
            main = {"c": tiles[q], "m": below_four(3 + q)}
            if q < 2:
                main["v"] = high(3 + q)
            if q == 0:
                main.update(u=high(5), w=below_four(6), sy=high(6), k=below_four(7))
                main["sx"] = main["k"]
            rows.append({n: x + [side[n]] if n in side else x for n, x in main.items()})
        return rows

    for is_north in (False, True):
        rows = halo(is_north)
        start = ROWS - 2 if is_north else -1
        made = {}

        def get(name, row):
            if name == "a":
                return made[row] if row in made else tiles_of(advected, row, 3)
            if row < 0:
                return rows[-row - 1][name]
            if row >= ROWS:
                return rows[row - ROWS][name]
            if name == "sy":
                return tiles_of(fields[name], row, 2)
            return tiles_of(fields[name], row, 2) + [sides[name][row]]

        for j, tiles in enumerate(advect_rows(get, start, 3)):
            made[start + j] = tiles
        final = ROWS - 3 if is_north else 0
        base = ROWS - 8 if is_north else 0
        done = {final + j: x for j, x in enumerate(diffuse_rows(get, final, 3))}
        for h in range(2):
            stack = [done[j][h] if j in done else inner[j, :, h * LANES : (h + 1) * LANES] for j in range(base, base + 8)]
            edges[int(is_north), :, :, h * LANES : (h + 1) * LANES] = jnp.transpose(jnp.stack(stack), (1, 0, 2))
        copy = middle(edges.at[int(is_north)], out.at[:, base : base + 8], sems.at[8 + int(is_north)])
        copy.start()
        copies.append(copy)
    for copy in copies:
        copy.wait()


def call(kernel, shapes, *operands, **options):
    return pl.pallas_call(
        kernel,
        out_shape=[jax.ShapeDtypeStruct(s, F32) for s in shapes],
        in_specs=[VMEM] * len(operands),
        out_specs=[VMEM] * len(shapes),
        compiler_params=pltpu.CompilerParams(vmem_limit_bytes=LIMIT),
        **options,
    )(*operands)


def from_fields(kernel, shapes, arrays, **options):
    specs, operands = [], []
    for x in arrays:
        for h in range(2):
            specs.append(pl.BlockSpec((x.shape[0], ROWS, LANES), lambda i, h=h: (0, 0, h)))
            operands.append(x)
    return pl.pallas_call(
        kernel,
        grid=(1,),
        out_shape=[jax.ShapeDtypeStruct(s, F32) for s in shapes],
        in_specs=specs,
        out_specs=[VMEM] * len(shapes),
        compiler_params=pltpu.CompilerParams(vmem_limit_bytes=LIMIT),
        **options,
    )(*operands)


def make(lons, lats):
    def spot(lon, lat):
        return (lon % lons) * lats + lat

    near = [(spot(i, j), spot(i ^ 1, j)) for i in range(lons) for j in range(lats)]
    far = [(spot(i, j), spot(i + 1 if i % 2 else i - 1, j)) for i in range(lons) for j in range(lats)]
    pair_a = [(spot(i, j), spot(i, j ^ 1)) for i in range(lons) for j in range(lats)]
    pair_b = []
    for i in range(lons):
        for j in range(lats):
            if j == 0:
                pair_b.append((spot(i, j), spot(i ^ 1, j)))
            elif j == lats - 1:
                pair_b.append((spot(i, j), spot(lons - 1 - i, j)))
            else:
                pair_b.append((spot(i, j), spot(i, j + 1 if j % 2 else j - 1)))

    def move(x, route):
        return lax.ppermute(x, ("lon", "lat"), route)

    def shards(tracers, velocity, slopes, diffusivity, sea_mask):
        plane = lambda x: x.reshape(-1, ROWS, 2 * LANES)
        arrays = [plane(tracers), plane(velocity), plane(slopes), diffusivity, sea_mask]
        full, side = (ROWS, 8, 2 * LANES), (ROWS, 8, LANES)
        (packed,) = from_fields(pack_kernel, [(8, 8, LANES)], arrays)
        far_got, near_got = move(packed, far), move(packed, near)
        fields = from_fields(
            rows_kernel, [full] * 8, arrays,
            cost_estimate=pl.CostEstimate(flops=10**7, bytes_accessed=6 * 10**6, transcendentals=0),
        )
        rim, send_a, send_b = call(edge_kernel, [(8, 8, LANES), (8, 8, 2 * LANES), (8, 8, 2 * LANES)], far_got, near_got, *fields)
        got_b, got_a = move(send_b, pair_b), move(send_a, pair_a)
        *rest, advected, inner = call(
            interior_kernel, [side] * 7 + [(ROWS, 8, 3 * LANES), full], *fields, rim,
            cost_estimate=pl.CostEstimate(flops=2 * 10**7, bytes_accessed=10**7, transcendentals=0),
        )
        out = pl.pallas_call(
            rim_kernel,
            out_shape=jax.ShapeDtypeStruct((8, ROWS, 2 * LANES), F32),
            in_specs=[VMEM] * 19,
            out_specs=pl.BlockSpec(memory_space=pl.ANY),
            scratch_shapes=[pltpu.VMEM((2, 8, 8, 2 * LANES), F32), pltpu.SemaphoreType.DMA((10,))],
            compiler_params=pltpu.CompilerParams(vmem_limit_bytes=LIMIT),
        )(got_a, got_b, *fields, *rest, advected, inner)
        return out.reshape(tracers.shape)

    return shards


def solution(mesh):
    return jax.shard_map(
        make(mesh.shape["lon"], mesh.shape["lat"]),
        mesh=mesh,
        in_specs=(
            P(None, None, "lat", "lon"),
            P(None, None, "lat", "lon"),
            P(None, None, "lat", "lon"),
            P(None, "lat", "lon"),
            P(None, "lat", "lon"),
        ),
        out_specs=P(None, None, "lat", "lon"),
        check_vma=False,
    )
```

time: 82.5 us -> 37.3 us (0.45)
  the two profiles are of different devices: /device:TPU:30 before, /device:TPU:32 now
where the time goes in v1:
time: 37.3 us; the launch traced here: 37 us
  Pallas kernels  20.9 us (56%)
  starting transfers between devices  9.63 us (26%)
  local copies, waits for them, and re-layouts  6.4 us (17%)
    pallas_call x2, Pallas kernels, call(): pl.pallas_call(kernel, out_shape=[jax.ShapeDtypeStruct(s, F32) for s in s...  12.4 us
    ppermute x4, starting transfers between devices, move(): return lax.ppermute(x, ('lon', 'lat'), route)  9.63 us
    unnamed x22, local copies, waits for them, and re-layouts  6.4 us
    pallas_call x2, Pallas kernels, from_fields(): pl.pallas_call(kernel, grid=(1,), out_shape=[jax.ShapeDtypeStruct(s, F32)...  5.93 us
    pallas_call x1, Pallas kernels, shards(): pl.pallas_call(rim_kernel, out_shape=jax.ShapeDtypeStruct((8, ROWS, 2 * L...  2.55 us
  transfers between devices with their start and end apart: 4, of which 0 were waited for; matrix products, arithmetic and copies ran while one was open for 0% of the time, Pallas kernels for 42%

profile of v1, /device:TPU:32, one launch (start us, length us, event | category | flops | bytes accessed | tf_op | source)
XLA Modules:
  0.0 37.0 jit_solution(17336280693111196374)
XLA Ops:
  0.0 0.0 copy-start
  0.0 1.1 %copy-done = f32[3,4,64,256]{3,2,1,0:T(8,128)S(1)} copy-done((f32[3,4,64,256]{3,2,1,0:T(8,128)S(1)}, f32[3,4,64,256]{3,2,1,0:T(8,128)}, u32[]{:S(2)}) %copy-start) | copy-done | bytes 786456
  1.1 0.0 copy-start.1
  1.1 1.0 %copy-done.1 = f32[2,4,64,256]{3,2,1,0:T(8,128)S(1)} copy-done((f32[2,4,64,256]{3,2,1,0:T(8,128)S(1)}, f32[2,4,64,256]{3,2,1,0:T(8,128)}, u32[]{:S(2)}) %copy-start.1) | copy-done | bytes 524312
  2.2 0.0 copy-start.2
  2.2 1.0 %copy-done.2 = f32[2,4,64,256]{3,2,1,0:T(8,128)S(1)} copy-done((f32[2,4,64,256]{3,2,1,0:T(8,128)S(1)}, f32[2,4,64,256]{3,2,1,0:T(8,128)}, u32[]{:S(2)}) %copy-start.2) | copy-done | bytes 524312
  3.2 0.0 copy-start.6
  3.2 0.9 %copy-done.6 = f32[4,64,256]{2,1,0:T(8,128)S(1)} copy-done((f32[4,64,256]{2,1,0:T(8,128)S(1)}, f32[4,64,256]{2,1,0:T(8,128)}, u32[]{:S(2)}) %copy-start.6) | copy-done | bytes 262168
  4.2 0.0 copy-start.8
  4.2 0.9 %copy-done.8 = s32[4,64,256]{2,1,0:T(8,128)S(1)} copy-done((s32[4,64,256]{2,1,0:T(8,128)S(1)}, s32[4,64,256]{2,1,0:T(8,128)}, u32[]{:S(2)}) %copy-start.8) | copy-done | bytes 262168
  5.1 0.0 copy-start.3
  5.1 0.0 copy-start.7
  5.1 2.6 %shard_map.55 = f32[8,8,128]{2,1,0:T(8,128)S(1)} custom-call(f32[8,64,256]{2,1,0:T(8,128)S(1)} %bitcast.8, f32[8,64,256]{2,1,0:T(8,128)S(1)} %bitcast.9, f32[12,64,256]{2,1,0:T(8,128)S(1)} %bitcast.6, f32[12,64,256]{2,1,0:T(8,128)S(1)} %bitcast.7, f32[8,64,256]{2,1,0:T(8,128)S(1)} %bitcast.12, f32[8,64,256]{2,1,0:T(8,128)S(1)} %bitcast.13, ...), custom_call_target="tpu_custom_call" | custom-call | tf_op jit(solution)/shard_map/pallas_call | solution.py:431
  7.7 0.1 collective-permute-start.1
  7.8 5.5 %collective-permute-start = (f32[8,8,128]{2,1,0:T(8,128)S(1)}, f32[8,8,128]{2,1,0:T(8,128)S(1)}, u32[]{:S(2)}, u32[]{:S(2)}) collective-permute-start(f32[8,8,128]{2,1,0:T(8,128)S(1)} %shard_map.55), channel_id=1, source_target_pairs={{0,120},{1,121},{2,122},{3,123},{4,124},{5,125},{6,126},{7,127},{8... | collective-permute-start | bytes 98312 | tf_op jit(solution)/shard_map/ppermute | solution.py:460
  13.3 0.0 copy-done.3
  13.3 0.0 copy-done.7
  13.3 0.0 copy-done.9
  13.3 3.3 %shard_map.56 = (f32[64,8,256]{2,1,0:T(8,128)S(1)}, f32[64,8,256]{2,1,0:T(8,128)S(1)}, f32[64,8,256]{2,1,0:T(8,128)S(1)}, f32[64,8,256]{2,1,0:T(8,128)S(1)}, f32...) custom-call(f32[8,64,256]{2,1,0:T(8,128)S(1)} %bitcast.10, ...), custom_call_target="tpu_custom_call" | custom-call | flops 10000000 | bytes 6000000 | tf_op jit(solution)/shard_map/pallas_call | solution.py:431
  16.7 0.0 copy-start.4
  16.7 0.0 collective-permute-done.1.refs_1_
  16.7 0.0 collective-permute-done.refs_0_
  16.7 0.3 shard_map.57
  17.0 0.5 %copy-done.4 = f32[64,8,256]{2,1,0:T(8,128)} copy-done((f32[64,8,256]{2,1,0:T(8,128)}, f32[64,8,256]{2,1,0:T(8,128)S(1)}, u32[]{:S(2)}) %copy-start.4) | copy-done | bytes 524312
  17.5 1.5 %collective-permute-start.2 = (f32[8,8,256]{2,1,0:T(8,128)S(1)}, f32[8,8,256]{2,1,0:T(8,128)S(1)}, u32[]{:S(2)}, u32[]{:S(2)}) collective-permute-start(f32[8,8,256]{2,1,0:T(8,128)S(1)} %get-tuple-element.33), channel_id=1, source_target_pairs={{0,1},{1,0},{2,3},{3,2},{4,5},{5,4},{6,7},{7,6},{8,9},{9,8},{10,11... | collective-permute-start | bytes 196616 | tf_op jit(solution)/shard_map/ppermute | solution.py:460
  19.0 2.5 %collective-permute-start.3 = (f32[8,8,256]{2,1,0:T(8,128)S(1)}, f32[8,8,256]{2,1,0:T(8,128)S(1)}, u32[]{:S(2)}, u32[]{:S(2)}) collective-permute-start(f32[8,8,256]{2,1,0:T(8,128)S(1)} %get-tuple-element.34), channel_id=1, source_target_pairs={{0,8},{1,2},{2,1},{3,4},{4,3},{5,6},{6,5},{7,127},{8,0},{9,10},{10... | collective-permute-start | bytes 196616 | tf_op jit(solution)/shard_map/ppermute | solution.py:460
  21.5 12.1 %shard_map.58 = (f32[64,8,128]{2,1,0:T(8,128)S(1)}, f32[64,8,128]{2,1,0:T(8,128)S(1)}, f32[64,8,128]{2,1,0:T(8,128)S(1)}, f32[64,8,128]{2,1,0:T(8,128)S(1)}, f32...) custom-call(f32[64,8,256]{2,1,0:T(8,128)S(1)} %get-tuple-element.25., ...), custom_call_target="tpu_custom_call" | custom-call | flops 20000000 | bytes 10000000 | tf_op jit(solution)/shard_map/pallas_call | solution.py:415
  33.6 0.8 %copy-done.10 = f32[64,8,256]{2,1,0:T(8,128)} copy-done((f32[64,8,256]{2,1,0:T(8,128)}, f32[64,8,256]{2,1,0:T(8,128)S(1)}, u32[]{:S(2)}) %copy-start.10) | copy-done | bytes 524312
  34.4 0.0 collective-permute-done.2.refs_0_
  34.4 0.0 collective-permute-done.3.refs_1_
  34.4 0.0 copy-done.5
  34.4 2.5 %shard_map.59 = f32[8,64,256]{2,1,0:T(8,128)} custom-call(f32[8,8,256]{2,1,0:T(8,128)S(1)} %collective-permute-done.2.refs_0_, f32[8,8,256]{2,1,0:T(8,128)S(1)} %collective-permute-done.3.refs_1_, f32[64,8,256]{2,1,0:T(8,128)S(1)} %get-tuple-element.25.refs_2_.refs_0_, f32[64,8,256]{2,1,0:T(8,128)S(1)} %get-tuple-element.26.refs_3_.refs_1_, ...), custom_call_target="tpu_custom_call" | custom-call | tf_op jit(solution)/shard_map/pallas_call | solution.py:478
  (3 shorter events, 0.0 us)
Async XLA Ops:
  0.0 1.1 %copy-start = (f32[3,4,64,256]{3,2,1,0:T(8,128)S(1)}, f32[3,4,64,256]{3,2,1,0:T(8,128)}, u32[]{:S(2)}) copy-start(f32[3,4,64,256]{3,2,1,0:T(8,128)} %param.6) | copy-start | bytes 2359300
  1.1 1.0 %copy-start.1 = (f32[2,4,64,256]{3,2,1,0:T(8,128)S(1)}, f32[2,4,64,256]{3,2,1,0:T(8,128)}, u32[]{:S(2)}) copy-start(f32[2,4,64,256]{3,2,1,0:T(8,128)} %param.5) | copy-start | bytes 1572868
  2.2 1.0 %copy-start.2 = (f32[2,4,64,256]{3,2,1,0:T(8,128)S(1)}, f32[2,4,64,256]{3,2,1,0:T(8,128)}, u32[]{:S(2)}) copy-start(f32[2,4,64,256]{3,2,1,0:T(8,128)} %param.7) | copy-start | bytes 1572868
  3.2 0.9 %copy-start.6 = (f32[4,64,256]{2,1,0:T(8,128)S(1)}, f32[4,64,256]{2,1,0:T(8,128)}, u32[]{:S(2)}) copy-start(f32[4,64,256]{2,1,0:T(8,128)} %refs_7_.3) | copy-start | bytes 786436
  4.2 0.9 %copy-start.8 = (s32[4,64,256]{2,1,0:T(8,128)S(1)}, s32[4,64,256]{2,1,0:T(8,128)}, u32[]{:S(2)}) copy-start(s32[4,64,256]{2,1,0:T(8,128)} %refs_9_.3) | copy-start | bytes 786436
  5.1 8.2 %copy-start.3 = (f32[2,4,64,256]{3,2,1,0:T(8,128)S(1)}, f32[2,4,64,256]{3,2,1,0:T(8,128)}, u32[]{:S(2)}) copy-start(f32[2,4,64,256]{3,2,1,0:T(8,128)} %param.7) | copy-start | bytes 1572868
  5.1 8.2 %copy-start.7 = (f32[4,64,256]{2,1,0:T(8,128)S(1)}, f32[4,64,256]{2,1,0:T(8,128)}, u32[]{:S(2)}) copy-start(f32[4,64,256]{2,1,0:T(8,128)} %refs_7_.3) | copy-start | bytes 786436
  5.1 8.2 %copy-start.9 = (s32[4,64,256]{2,1,0:T(8,128)S(1)}, s32[4,64,256]{2,1,0:T(8,128)}, u32[]{:S(2)}) copy-start(s32[4,64,256]{2,1,0:T(8,128)} %refs_9_.3) | copy-start | bytes 786436
  7.7 9.0 %collective-permute-start.1 = (f32[8,8,128]{2,1,0:T(8,128)S(1)}, f32[8,8,128]{2,1,0:T(8,128)S(1)}, u32[]{:S(2)}, u32[]{:S(2)}) collective-permute-start(f32[8,8,128]{2,1,0:T(8,128)S(1)} %shard_map.55), channel_id=1, source_target_pairs={{0,8},{1,9},{2,10},{3,11},{4,12},{5,13},{6,14},{7,15},{8,0},{9,1},... | collective-permute-start | bytes 98312 | tf_op jit(solution)/shard_map/ppermute | solution.py:460
  7.8 8.9 %collective-permute-start = (f32[8,8,128]{2,1,0:T(8,128)S(1)}, f32[8,8,128]{2,1,0:T(8,128)S(1)}, u32[]{:S(2)}, u32[]{:S(2)}) collective-permute-start(f32[8,8,128]{2,1,0:T(8,128)S(1)} %shard_map.55), channel_id=1, source_target_pairs={{0,120},{1,121},{2,122},{3,123},{4,124},{5,125},{6,126},{7,127},{8... | collective-permute-start | bytes 98312 | tf_op jit(solution)/shard_map/ppermute | solution.py:460
  16.7 0.8 %copy-start.4 = (f32[64,8,256]{2,1,0:T(8,128)}, f32[64,8,256]{2,1,0:T(8,128)S(1)}, u32[]{:S(2)}) copy-start(f32[64,8,256]{2,1,0:T(8,128)S(1)} %get-tuple-element.32.refs_9_.refs_7_) | copy-start | bytes 1572868
  17.5 16.9 %collective-permute-start.2 = (f32[8,8,256]{2,1,0:T(8,128)S(1)}, f32[8,8,256]{2,1,0:T(8,128)S(1)}, u32[]{:S(2)}, u32[]{:S(2)}) collective-permute-start(f32[8,8,256]{2,1,0:T(8,128)S(1)} %get-tuple-element.33), channel_id=1, source_target_pairs={{0,1},{1,0},{2,3},{3,2},{4,5},{5,4},{6,7},{7,6},{8,9},{9,8},{10,11... | collective-permute-start | bytes 196616 | tf_op jit(solution)/shard_map/ppermute | solution.py:460
  19.0 15.4 %collective-permute-start.3 = (f32[8,8,256]{2,1,0:T(8,128)S(1)}, f32[8,8,256]{2,1,0:T(8,128)S(1)}, u32[]{:S(2)}, u32[]{:S(2)}) collective-permute-start(f32[8,8,256]{2,1,0:T(8,128)S(1)} %get-tuple-element.34), channel_id=1, source_target_pairs={{0,8},{1,2},{2,1},{3,4},{4,3},{5,6},{6,5},{7,127},{8,0},{9,10},{10... | collective-permute-start | bytes 196616 | tf_op jit(solution)/shard_map/ppermute | solution.py:460
  21.5 12.9 %copy-start.5 = (f32[64,8,256]{2,1,0:T(8,128)S(1)}, f32[64,8,256]{2,1,0:T(8,128)}, u32[]{:S(2)}) copy-start(f32[64,8,256]{2,1,0:T(8,128)} %copy-done.4) | copy-start | bytes 1572868
  33.6 0.8 %copy-start.10 = (f32[64,8,256]{2,1,0:T(8,128)}, f32[64,8,256]{2,1,0:T(8,128)S(1)}, u32[]{:S(2)}) copy-start(f32[64,8,256]{2,1,0:T(8,128)S(1)} %get-tuple-element.44.refs_18_) | copy-start | bytes 1572868

commit v2 on v1

--- a/solution.py
+++ b/solution.py
@@ -10,9 +10,9 @@
 LANES = 128
 F32 = jnp.float32
 VMEM = pl.BlockSpec(memory_space=pltpu.VMEM)
-LIMIT = 48 * 1024 * 1024
+LIMIT = 16 * 1024 * 1024
 FIELDS = ("c", "m", "u", "v", "w", "sx", "k", "sy")
-SIDE = FIELDS[:7]
+GROUPS = ("c", "mu", "vw", "sk")
 
 
 def lane_of():
@@ -49,43 +49,56 @@
     return out
 
 
-def halves_of(refs):
-    return [refs[0::2], refs[1::2]]
-
-
 def pack_kernel(*refs):
-    halves, packed = halves_of(refs[:10]), refs[10]
+    arrays, parts, message, spare, sems = refs[:5], refs[5:15], refs[15], refs[16], refs[17]
+    copies = []
+    for i, array in enumerate(arrays):
+        for h in range(2):
+            part = pltpu.make_async_copy(
+                array.at[:, :, h * LANES : (h + 1) * LANES], parts[2 * i + h], sems.at[2 * i + h]
+            )
+            part.start()
+            copies.append(part)
+    for part in copies:
+        part.wait()
+    halves = [parts[0::2], parts[1::2]]
     lane, low = lane_of(), low_of()
-    second = jnp.logical_or(lane == 1, lane == 126)
 
     def group(g, carry):
-        total = jnp.zeros((8, LANES), F32)
+        first = second = jnp.zeros((8, LANES), F32)
         for part in range(8):
             left, right = load_rows(halves, part * 8 + g)
             rim = {n: jnp.where(lane[: left[n].shape[0]] < 64, left[n], right[n]) for n in left}
             mk = jnp.concatenate([rim["m"], rim["k"]], axis=0)
-            mku = jnp.where(jnp.logical_and(second, jnp.logical_not(low)), pltpu.roll(rim["uv"], 4, 0), mk)
-            sw = jnp.where(low, rim["s"], rim["vw"])
-            slots = jnp.where(lane < 14, pltpu.roll(rim["uv"], 13, 1), pltpu.roll(sw, 15, 1))
-            slots = jnp.where(lane < 12, pltpu.roll(mku, 9, 1), slots)
-            slots = jnp.where(lane < 6, pltpu.roll(rim["c"], 3, 1), slots)
-            if part:
-                slots = pltpu.roll(slots, 16 * part, 1)
-                total = jnp.where(lane < 16 * part, total, slots)
-            else:
-                total = slots
-        packed[g] = total
+            mu = jnp.where(low, mk, pltpu.roll(rim["uv"], 4, 0))
+            sk = jnp.where(low, rim["s"], mk)
+            base = 16 * part
+            before, half = lane < base, lane < base + 8
+            one = jnp.where(half, pltpu.roll(rim["c"], (base + 4) % LANES, 1), pltpu.roll(mu, (base + 12) % LANES, 1))
+            two = jnp.where(half, pltpu.roll(rim["vw"], (base + 4) % LANES, 1), pltpu.roll(sk, (base + 12) % LANES, 1))
+            first = jnp.where(before, first, one)
+            second = jnp.where(before, second, two)
+        message[g] = first
+        spare[g] = second
         return carry
 
     lax.fori_loop(0, 8, group, 0)
+    slot = lane % 8
+    for pair in range(2):
+        total = pltpu.roll(spare[4 * pair], LANES - 2, 1)
+        for i in range(1, 4):
+            moved = spare[4 * pair + i] if i == 1 else pltpu.roll(spare[4 * pair + i], 2 * i - 2, 1)
+            total = jnp.where((slot == (2 * i + 1) % 8) | (slot == (2 * i + 2) % 8), moved, total)
+        message[8 + pair] = total
 
 
 def rows_kernel(*refs):
-    halves, outs = halves_of(refs[:10]), dict(zip(FIELDS, refs[10:]))
+    parts, outs, advected = refs[:10], dict(zip(FIELDS, refs[10:18])), refs[18]
+    halves = [parts[0::2], parts[1::2]]
 
     def row_group(block, carry):
-        for inner in range(4):
-            row = block * 4 + inner
+        for inner in range(8):
+            row = block * 8 + inner
             for half, values in enumerate(load_rows(halves, row)):
                 full = {
                     "c": values["c"],
@@ -101,21 +114,45 @@
                     outs[name][row, :, half * LANES : (half + 1) * LANES] = full[name]
         return carry
 
-    lax.fori_loop(0, ROWS // 4, row_group, 0)
+    lax.fori_loop(0, ROWS // 8, row_group, 0)
+    get = lambda name, row: tiles_of(outs[name], row, 2)
+
+    def advect_block(block, carry):
+        first = 2 + 10 * block
+        for j, tiles in enumerate(advect_rows(get, first, 10)):
+            for t in range(2):
+                advected[first + j, :, t * LANES : (t + 1) * LANES] = tiles[t]
+        return carry
+
+    lax.fori_loop(0, 6, advect_block, 0)
 
 
 def edge_kernel(*refs):
-    from_far, from_near = refs[0], refs[1]
-    fields = dict(zip(FIELDS, refs[2:10]))
-    rim, send_a, send_b = refs[10:]
+    from_far, from_near, own, spare = refs[:4]
+    fields = dict(zip(FIELDS, refs[4:12]))
+    strips, send_a, send_b = refs[12:]
     lane, low = lane_of(), low_of()
     lon, lat = lax.axis_index("lon"), lax.axis_index("lat")
     slot = lane % 16
-    west = (slot < 3) | ((slot >= 6) & (slot < 9)) | (slot == 12) | (slot == 14)
     far_is_west = jnp.broadcast_to(lon % 2, (8, LANES)) == 0
-    take_far = west == far_is_west
+
+    def strip(mine, east, west, late):
+        shift = lambda x, by: pltpu.roll(x, (by - 8 * late) % LANES, 1) if by != 8 * late else x
+        inner = jnp.where(slot < 4, shift(mine, 0), shift(east, 0))
+        outer = jnp.where(slot < 10, shift(west, 6), shift(mine, 6))
+        return jnp.where(slot < 7, inner, outer)
+
     for g in range(8):
-        rim[g] = jnp.where(take_far, from_far[g], from_near[g])
+        for which in range(2):
+            if which == 0:
+                far, near, mine = from_far[g], from_near[g], own[g]
+            else:
+                back = (2 - 2 * (g % 4)) % LANES
+                turn = lambda x: pltpu.roll(x, back, 1) if back else x
+                far, near, mine = turn(from_far[8 + g // 4]), turn(from_near[8 + g // 4]), spare[g]
+            east, west = jnp.where(far_is_west, near, far), jnp.where(far_is_west, far, near)
+            for late in range(2):
+                strips[2 * which + late, g] = strip(mine, east, west, late)
 
     def message(top):
         row = lambda q: jnp.where(top, ROWS - 1 - q, q)
@@ -123,7 +160,9 @@
         pair = lambda n1, q1, n2, q2: [jnp.where(low, part(n1, q1, h), part(n2, q2, h)) for h in range(2)]
         tiles = [[part("c", q, h) for h in range(2)] for q in range(3)]
         tiles += [pair("m", 0, "v", 0), pair("m", 1, "v", 1), pair("m", 2, "u", 0), pair("w", 0, "sy", 0)]
-        corners = [pltpu.roll(rim[jnp.where(top, 7 - q, q)], jnp.where(top, 16, 0), 1) for q in range(3)]
+        corners = [
+            pltpu.roll(strips[i, jnp.where(top, 7 - q, q)], jnp.where(top, 16, 0), 1) for q in range(2) for i in range(3)
+        ]
         return tiles, [part("k", 0, h) for h in range(2)], corners
 
     def store(ref, tiles, kappa, corners):
@@ -131,8 +170,8 @@
             for h in range(2):
                 ref[i, :, h * LANES : (h + 1) * LANES] = tile[h]
         packed = corners[0]
-        for q in (1, 2):
-            packed = jnp.where(lane < 16 * q, packed, pltpu.roll(corners[q], 16 * q, 1))
+        for i in range(1, 6):
+            packed = jnp.where(lane < 16 * i, packed, pltpu.roll(corners[i], 16 * i, 1))
         ref[7, :, :LANES] = jnp.where(low, kappa[0], pltpu.roll(packed, 4, 0))
         ref[7, :, LANES:] = jnp.where(low, kappa[1], packed)
 
@@ -153,40 +192,46 @@
         sign = jnp.where(low, 1.0, -1.0)
         turned = [flip_tile(tile) for tile in tiles]
         turned = turned[:3] + [[sign * x for x in tile] for tile in turned[3:]]
-        index = jnp.where(lane < 6, 5 - lane, jnp.where(lane < 12, 17 - lane, jnp.where(lane < 14, 25 - lane, 29 - lane)))
-        index = jnp.where(lane < 16, index, lane)
-        uv = (lane == 12) | (lane == 13) | (((lane == 7) | (lane == 10)) & jnp.logical_not(low))
-        corner_sign = jnp.where(uv, -1.0, 1.0)
-        store(send_b, turned, flip_tile(kappa), [corner_sign * flip(x, index) for x in corners])
-
-
-def decode_rim(vector, part):
-    lane = lane_of()
-    at = lambda first: pltpu.roll(vector, lax.rem(2 * LANES - 16 * part - first, LANES), 1)
-    mku, uv, sw = at(9), at(13), at(15)
-    second = jnp.logical_or(lane == 1, lane == 126)
-    high = twice_high(mku)
+        index = jnp.where(lane < 14, 13 - lane, lane)
+        corner_signs = [1.0, sign, -sign]
+        store(send_b, turned, flip_tile(kappa), [corner_signs[i % 3] * flip(x, index) for i, x in enumerate(corners)])
+
+
+def split_groups(groups):
     return {
-        "c": at(3),
-        "m": twice_low(mku),
-        "u": jnp.where(second, high, twice_low(uv)),
-        "v": twice_high(uv),
-        "w": twice_high(sw),
-        "sx": twice_low(sw),
-        "k": high,
+        "c": groups["c"],
+        "m": twice_low(groups["mu"]),
+        "u": twice_high(groups["mu"]),
+        "v": twice_low(groups["vw"]),
+        "w": twice_high(groups["vw"]),
+        "sx": twice_low(groups["sk"]),
+        "k": twice_high(groups["sk"]),
     }
+
+
+def third_tile(groups, bases):
+    east = lane_of() < 64
+    tile = lambda x, base: jnp.where(
+        east, pltpu.roll(x, (2 * LANES - 4 - base) % LANES, 1), pltpu.roll(x, (2 * LANES - 10 - base) % LANES, 1)
+    )
+    return split_groups({n: tile(groups[n], bases[n]) for n in GROUPS})
 
 
 def plus(tiles):
     last = lane_of() == LANES - 1
     turned = [pltpu.roll(t, LANES - 1, 1) for t in tiles]
-    return [jnp.where(last, turned[(i + 1) % 3], turned[i]) for i in range(3)]
-
-
-def minus(tiles, count=3):
+    if len(tiles) == 1:
+        return turned
+    return [jnp.where(last, turned[(i + 1) % len(tiles)], turned[i]) for i in range(len(tiles))]
+
+
+def minus(tiles, count=3, west=None):
     first = lane_of() == 0
     turned = [pltpu.roll(t, 1, 1) for t in tiles]
-    return [jnp.where(first, turned[(i + 2) % 3], turned[i]) for i in range(count)]
+    if len(tiles) == 1:
+        return turned
+    before = [turned[-1] if west is None else west] + turned[:-1]
+    return [jnp.where(first, before[i], turned[i]) for i in range(min(count, len(tiles)))]
 
 
 def each(function, *lists):
@@ -254,7 +299,17 @@
     return result
 
 
-def diffuse_rows(get, first, count):
+def slope_flux(k1, k2, opened, step, s1, s2, z1, z2):
+    return 0.5 * (k1 + k2) * opened * (step + 0.125 * (s1 + s2) * (z1 + z2))
+
+
+def eastward(a, m, k, sx, twice_z):
+    opened = each(jnp.multiply, m, plus(m))
+    step = each(lambda x, y, o: (y - x) * o, a, plus(a), opened)
+    return step, each(slope_flux, k, plus(k), opened, step, sx, plus(sx), twice_z, plus(twice_z))
+
+
+def diffuse_rows(get, first, count, beside=None):
     a = {j: get("a", first + j) for j in range(-1, count + 1)}
     m = {j: get("m", first + j) for j in range(-1, count + 1)}
     k = {j: get("k", first + j) for j in range(-1, count + 1)}
@@ -269,21 +324,21 @@
         opened = each(jnp.multiply, m[j][:2], m[j + 1][:2])
         step_y[j] = each(lambda x, y, o: (y - x) * o, a[j][:2], a[j + 1][:2], opened)
         flux_y[j] = each(
-            lambda k1, k2, o, s, s1, s2, z1, z2: 0.5 * (k1 + k2) * o * (s + 0.125 * (s1 + s2) * (z1 + z2)),
-            k[j], k[j + 1], opened, step_y[j], sy[j], sy[j + 1], twice_z[j], twice_z[j + 1],
+            slope_flux, k[j], k[j + 1], opened, step_y[j], sy[j], sy[j + 1], twice_z[j], twice_z[j + 1]
         )
     result = []
+    last = lane_of() == LANES - 1
     for j in range(count):
         sx = get("sx", first + j)
-        opened = each(jnp.multiply, m[j], plus(m[j]))
-        step_x = each(lambda x, y, o: (y - x) * o, a[j], plus(a[j]), opened)
-        flux_x = each(
-            lambda k1, k2, o, s, s1, s2, z1, z2: 0.5 * (k1 + k2) * o * (s + 0.125 * (s1 + s2) * (z1 + z2)),
-            k[j], plus(k[j]), opened, step_x, sx, plus(sx), twice_z[j], plus(twice_z[j]),
-        )
-        twice_x = each(jnp.add, step_x, minus(step_x, 2))
+        step_x, flux_x = eastward(a[j], m[j], k[j], sx, twice_z[j])
+        west = [None, None]
+        if beside:
+            east, west = beside(first + j)
+            step_x = [step_x[0], jnp.where(last, east[0], step_x[1])]
+            flux_x = [flux_x[0], jnp.where(last, east[1], flux_x[1])]
+        twice_x = each(jnp.add, step_x, minus(step_x, 2, west[0]))
         twice_y = each(jnp.add, step_y[j - 1], step_y[j])
-        total = each(lambda f, g, p, q: (f - g) + (p - q), flux_x, minus(flux_x, 2), flux_y[j], flux_y[j - 1])
+        total = each(lambda f, g, p, q: (f - g) + (p - q), flux_x, minus(flux_x, 2, west[1]), flux_y[j], flux_y[j - 1])
 
         def finish(value, marker, kappa, east, north, tx, ty, sz, across):
             face_east, face_north = 0.5 * (east + below(east)), 0.5 * (north + below(north))
@@ -303,50 +358,57 @@
 
 
 def interior_kernel(*refs):
-    fields, rim = dict(zip(FIELDS, refs[:8])), refs[8]
-    sides = dict(zip(SIDE, refs[9:16]))
-    advected, out = refs[16:]
-
-    def spread(g, carry):
-        for part in range(8):
-            row = part * 8 + g
-            for name, value in decode_rim(rim[g], part).items():
-                sides[name][row] = value
-        return carry
-
-    lax.fori_loop(0, 8, spread, 0)
+    fields, advected, strips = dict(zip(FIELDS, refs[:8])), refs[8], refs[9]
+    out, kept, narrow = refs[10:]
+    lane = lane_of()
+    near_east, near_west = lane >= LANES - 2, lane < 2
+
+    full = [split_groups({n: strips[i, g] for i, n in enumerate(GROUPS)}) for g in range(8)]
+
+    def get_strip(name, g):
+        x = full[g % 8][name]
+        return [x if 0 <= g < 8 else pltpu.roll(x, 16 if g < 0 else LANES - 16, 1)]
+
+    for g, (a,) in enumerate(advect_rows(get_strip, 0, 8)):
+        part = full[g]
+        step_z = (below(a) - a) * open_below(part["m"])
+        step, flux = eastward([a], [part["m"]], [part["k"]], [part["sx"]], [above(step_z) + step_z])
+        narrow[0, g], narrow[1, g], narrow[2, g] = a, step[0], flux[0]
+
+    def lanes_to(which, row, lane_from, lane_to):
+        part = row // 8
+        return pltpu.roll(narrow[which, row - 8 * part], lax.rem(2 * LANES + lane_to - lane_from - 16 * part, LANES), 1)
 
     def get(name, row):
-        if name == "a":
-            return tiles_of(advected, row, 3)
-        if name == "sy":
+        if name != "a":
             return tiles_of(fields[name], row, 2)
-        return tiles_of(fields[name], row, 2) + [sides[name][row]]
-
-    def advect_block(block, carry):
-        first = 2 + 4 * block
-        for j, tiles in enumerate(advect_rows(get, first, 4)):
-            for t in range(3):
-                advected[first + j, :, t * LANES : (t + 1) * LANES] = tiles[t]
-        return carry
-
-    lax.fori_loop(0, 15, advect_block, 0)
+        left, right = tiles_of(advected, row, 2)
+        return [
+            jnp.where(near_west, lanes_to(0, row, 10, 0), left),
+            jnp.where(near_east, lanes_to(0, row, 3, LANES - 1), right),
+        ]
+
+    def beside(row):
+        return [lanes_to(i, row, 3, LANES - 1) for i in (1, 2)], [lanes_to(i, row, 9, 0) for i in (1, 2)]
+
+    for i, row in enumerate((3, ROWS - 4)):
+        for t, tile in enumerate(get("a", row)):
+            kept[i, :, t * LANES : (t + 1) * LANES] = tile
 
     def diffuse_block(block, carry):
-        first = 3 + 2 * block
-        for j, tiles in enumerate(diffuse_rows(get, first, 2)):
+        first = jnp.minimum(3 + 6 * block, ROWS - 3 - 6)
+        for j, tiles in enumerate(diffuse_rows(get, first, 6, beside)):
             for t in range(2):
                 out[first + j, :, t * LANES : (t + 1) * LANES] = tiles[t]
         return carry
 
-    lax.fori_loop(0, 29, diffuse_block, 0)
+    lax.fori_loop(0, 10, diffuse_block, 0)
 
 
 def rim_kernel(*refs):
     got_a, got_b = refs[0], refs[1]
     fields = dict(zip(FIELDS, refs[2:10]))
-    sides = dict(zip(SIDE, refs[10:17]))
-    advected, inner, out, edges, sems = refs[17:]
+    strips, inner, kept, out, edges, sems = refs[10:]
     middle = pltpu.make_async_copy
     copies = [middle(inner.at[8:56, i], out.at[i, 8:56], sems.at[i]) for i in range(8)]
     for copy in copies:
@@ -370,7 +432,8 @@
         corner = jnp.where(low, pltpu.roll(tiles[7][0], 4, 0), tiles[7][1])
         rows = []
         for q in range(3):
-            side = decode_rim(corner, q)
+            bases = {n: 16 * (3 * min(q, 1) + min(i, 2)) for i, n in enumerate(GROUPS)}
+            side = third_tile({n: corner for n in GROUPS}, bases)
             main = {"c": tiles[q], "m": below_four(3 + q)}
             if q < 2:
                 main["v"] = high(3 + q)
@@ -382,21 +445,24 @@
 
     for is_north in (False, True):
         rows = halo(is_north)
-        start = ROWS - 2 if is_north else -1
-        made = {}
+        start = ROWS - 3 if is_north else -1
+        made, sides = {}, {}
+        for row in range(*((ROWS - 5, ROWS) if is_north else (0, 5))):
+            base = 16 * (row // 8)
+            sides[row] = third_tile({n: strips[i, row % 8] for i, n in enumerate(GROUPS)}, dict.fromkeys(GROUPS, base))
 
         def get(name, row):
             if name == "a":
-                return made[row] if row in made else tiles_of(advected, row, 3)
+                return made[row] if row in made else tiles_of(kept, int(is_north), 2)
             if row < 0:
                 return rows[-row - 1][name]
             if row >= ROWS:
                 return rows[row - ROWS][name]
             if name == "sy":
                 return tiles_of(fields[name], row, 2)
-            return tiles_of(fields[name], row, 2) + [sides[name][row]]
-
-        for j, tiles in enumerate(advect_rows(get, start, 3)):
+            return tiles_of(fields[name], row, 2) + [sides[row][name]]
+
+        for j, tiles in enumerate(advect_rows(get, start, 4)):
             made[start + j] = tiles
         final = ROWS - 3 if is_north else 0
         base = ROWS - 8 if is_north else 0
@@ -422,23 +488,6 @@
     )(*operands)
 
 
-def from_fields(kernel, shapes, arrays, **options):
-    specs, operands = [], []
-    for x in arrays:
-        for h in range(2):
-            specs.append(pl.BlockSpec((x.shape[0], ROWS, LANES), lambda i, h=h: (0, 0, h)))
-            operands.append(x)
-    return pl.pallas_call(
-        kernel,
-        grid=(1,),
-        out_shape=[jax.ShapeDtypeStruct(s, F32) for s in shapes],
-        in_specs=specs,
-        out_specs=[VMEM] * len(shapes),
-        compiler_params=pltpu.CompilerParams(vmem_limit_bytes=LIMIT),
-        **options,
-    )(*operands)
-
-
 def make(lons, lats):
     def spot(lon, lat):
         return (lon % lons) * lats + lat
@@ -462,27 +511,38 @@
     def shards(tracers, velocity, slopes, diffusivity, sea_mask):
         plane = lambda x: x.reshape(-1, ROWS, 2 * LANES)
         arrays = [plane(tracers), plane(velocity), plane(slopes), diffusivity, sea_mask]
-        full, side = (ROWS, 8, 2 * LANES), (ROWS, 8, LANES)
-        (packed,) = from_fields(pack_kernel, [(8, 8, LANES)], arrays)
+        full, side = (ROWS, 8, 2 * LANES), (8, 8, LANES)
+        *parts, packed, spare = pl.pallas_call(
+            pack_kernel,
+            out_shape=[jax.ShapeDtypeStruct(x.shape[:2] + (LANES,), x.dtype) for x in arrays for _ in range(2)]
+            + [jax.ShapeDtypeStruct((10, 8, LANES), F32), jax.ShapeDtypeStruct(side, F32)],
+            in_specs=[pl.BlockSpec(memory_space=pl.ANY)] * 5,
+            out_specs=[VMEM] * 12,
+            scratch_shapes=[pltpu.SemaphoreType.DMA((10,))],
+            compiler_params=pltpu.CompilerParams(vmem_limit_bytes=LIMIT),
+        )(*arrays)
         far_got, near_got = move(packed, far), move(packed, near)
-        fields = from_fields(
-            rows_kernel, [full] * 8, arrays,
+        *fields, advected = call(
+            rows_kernel, [full] * 9, *parts,
             cost_estimate=pl.CostEstimate(flops=10**7, bytes_accessed=6 * 10**6, transcendentals=0),
         )
-        rim, send_a, send_b = call(edge_kernel, [(8, 8, LANES), (8, 8, 2 * LANES), (8, 8, 2 * LANES)], far_got, near_got, *fields)
+        strips, send_a, send_b = call(
+            edge_kernel, [(4,) + side, (8, 8, 2 * LANES), (8, 8, 2 * LANES)], far_got, near_got, packed, spare, *fields
+        )
         got_b, got_a = move(send_b, pair_b), move(send_a, pair_a)
-        *rest, advected, inner = call(
-            interior_kernel, [side] * 7 + [(ROWS, 8, 3 * LANES), full], *fields, rim,
+        inner, kept = call(
+            interior_kernel, [full, (2, 8, 2 * LANES)], *fields, advected, strips,
+            scratch_shapes=[pltpu.VMEM((3,) + side, F32)],
             cost_estimate=pl.CostEstimate(flops=2 * 10**7, bytes_accessed=10**7, transcendentals=0),
         )
         out = pl.pallas_call(
             rim_kernel,
             out_shape=jax.ShapeDtypeStruct((8, ROWS, 2 * LANES), F32),
-            in_specs=[VMEM] * 19,
+            in_specs=[VMEM] * 13,
             out_specs=pl.BlockSpec(memory_space=pl.ANY),
             scratch_shapes=[pltpu.VMEM((2, 8, 8, 2 * LANES), F32), pltpu.SemaphoreType.DMA((10,))],
             compiler_params=pltpu.CompilerParams(vmem_limit_bytes=LIMIT),
-        )(got_a, got_b, *fields, *rest, advected, inner)
+        )(got_a, got_b, *fields, strips, inner, kept)
         return out.reshape(tracers.shape)
 
     return shards

time: 37.3 us -> 28 us (0.75)
  the two profiles are of different devices: /device:TPU:32 before, /device:TPU:39 now
where the time goes in v2:
time: 28 us; the launch traced here: 27.7 us
  Pallas kernels  12.2 us (44%)
  starting transfers between devices  7.32 us (26%)
  local copies, waits for them, and re-layouts  5.11 us (18%)
  waiting for transfers between devices  2.95 us (11%)
    pallas_call x3, Pallas kernels, call(): pl.pallas_call(kernel, out_shape=[jax.ShapeDtypeStruct(s, F32) for s in s...  8.14 us
    ppermute x4, starting transfers between devices, move(): return lax.ppermute(x, ('lon', 'lat'), route)  7.32 us
    unnamed x10, local copies, waits for them, and re-layouts  5.11 us
    ppermute x4, waiting for transfers between devices, move(): return lax.ppermute(x, ('lon', 'lat'), route)  2.95 us
    pallas_call x1, Pallas kernels, shards(): pl.pallas_call(pack_kernel, out_shape=[jax.ShapeDtypeStruct(x.shape[:2] +...  2.63 us
    pallas_call x1, Pallas kernels, shards(): pl.pallas_call(rim_kernel, out_shape=jax.ShapeDtypeStruct((8, ROWS, 2 * L...  1.47 us
  transfers between devices with their start and end apart: 4, of which 1 were waited for; matrix products, arithmetic and copies ran while one was open for 0% of the time, Pallas kernels for 28%

profile of v2, /device:TPU:39, one launch (start us, length us, event | category | flops | bytes accessed | tf_op | source)
XLA Modules:
  0.0 27.7 jit_solution(9641404346747245229)
XLA Ops:
  0.0 0.0 copy-start
  0.0 1.1 %copy-done = f32[3,4,64,256]{3,2,1,0:T(8,128)S(1)} copy-done((f32[3,4,64,256]{3,2,1,0:T(8,128)S(1)}, f32[3,4,64,256]{3,2,1,0:T(8,128)}, u32[]{:S(2)}) %copy-start) | copy-done | bytes 786456
  1.1 0.0 copy-start.1
  1.1 1.0 %copy-done.1 = f32[2,4,64,256]{3,2,1,0:T(8,128)S(1)} copy-done((f32[2,4,64,256]{3,2,1,0:T(8,128)S(1)}, f32[2,4,64,256]{3,2,1,0:T(8,128)}, u32[]{:S(2)}) %copy-start.1) | copy-done | bytes 524312
  2.2 0.0 copy-start.2
  2.2 1.0 %copy-done.2 = f32[2,4,64,256]{3,2,1,0:T(8,128)S(1)} copy-done((f32[2,4,64,256]{3,2,1,0:T(8,128)S(1)}, f32[2,4,64,256]{3,2,1,0:T(8,128)}, u32[]{:S(2)}) %copy-start.2) | copy-done | bytes 524312
  3.2 0.0 copy-start.3
  3.2 0.9 %copy-done.3 = f32[4,64,256]{2,1,0:T(8,128)S(1)} copy-done((f32[4,64,256]{2,1,0:T(8,128)S(1)}, f32[4,64,256]{2,1,0:T(8,128)}, u32[]{:S(2)}) %copy-start.3) | copy-done | bytes 262168
  4.2 0.0 copy-start.4
  4.2 0.9 %copy-done.4 = s32[4,64,256]{2,1,0:T(8,128)S(1)} copy-done((s32[4,64,256]{2,1,0:T(8,128)S(1)}, s32[4,64,256]{2,1,0:T(8,128)}, u32[]{:S(2)}) %copy-start.4) | copy-done | bytes 262168
  5.1 2.6 %shard_map.55 = (f32[8,64,128]{2,1,0:T(8,128)S(1)}, f32[8,64,128]{2,1,0:T(8,128)S(1)}, f32[12,64,128]{2,1,0:T(8,128)S(1)}, f32[12,64,128]{2,1,0:T(8,128)S(1)}, f...) custom-call(f32[8,64,256]{2,1,0:T(8,128)S(1)} %bitcast.5, ...), custom_call_target="tpu_custom_call" | custom-call | tf_op jit(solution)/shard_map/pallas_call | solution.py:515
  7.8 3.3 %collective-permute-start = (f32[10,8,128]{2,1,0:T(8,128)S(1)}, f32[10,8,128]{2,1,0:T(8,128)S(1)}, u32[]{:S(2)}, u32[]{:S(2)}) collective-permute-start(f32[10,8,128]{2,1,0:T(8,128)S(1)} %get-tuple-element.31.refs_2_), channel_id=1, source_target_pairs={{0,120},{1,121},{2,122},{3,123},{4,124},{5,125},{6,126},{7,127},{8... | collective-permute-start | bytes 122888 | tf_op jit(solution)/shard_map/ppermute | solution.py:509
  11.1 2.3 %collective-permute-start.1 = (f32[10,8,128]{2,1,0:T(8,128)S(1)}, f32[10,8,128]{2,1,0:T(8,128)S(1)}, u32[]{:S(2)}, u32[]{:S(2)}) collective-permute-start(f32[10,8,128]{2,1,0:T(8,128)S(1)} %get-tuple-element.31.refs_2_), channel_id=1, source_target_pairs={{0,8},{1,9},{2,10},{3,11},{4,12},{5,13},{6,14},{7,15},{8,0},{9,1},... | collective-permute-start | bytes 122888 | tf_op jit(solution)/shard_map/ppermute | solution.py:509
  13.4 4.2 %shard_map.56 = (f32[64,8,256]{2,1,0:T(8,128)S(1)}, f32[64,8,256]{2,1,0:T(8,128)S(1)}, f32[64,8,256]{2,1,0:T(8,128)S(1)}, f32[64,8,256]{2,1,0:T(8,128)S(1)}, f32...) custom-call(f32[8,64,128]{2,1,0:T(8,128)S(1)} %get-tuple-element.33., ...), custom_call_target="tpu_custom_call" | custom-call | flops 10000000 | bytes 6000000 | tf_op jit(solution)/shard_map/pallas_call | solution.py:481
  17.6 0.0 collective-permute-done.refs_0_
  17.6 0.0 collective-permute-done.1.refs_1_
  17.6 0.5 %shard_map.57 = (f32[4,8,8,128]{3,2,1,0:T(8,128)S(1)}, f32[8,8,256]{2,1,0:T(8,128)S(1)}, f32[8,8,256]{2,1,0:T(8,128)S(1)}) custom-call(f32[10,8,128]{2,1,0:T(8,128)S(1)} %collective-permute-done.refs_0_, f32[10,8,128]{2,1,0:T(8,128)S(1)} %collective-permute-done.1.refs_1_, f32[10,8,128]{2,1,0:T(8,128)S(1)} %get-tuple-element.31.refs_2_, ...), custom_call_target="tpu_custom_call" | custom-call | tf_op jit(solution)/shard_map/pallas_call | solution.py:481
  18.1 0.5 %collective-permute-start.2 = (f32[8,8,256]{2,1,0:T(8,128)S(1)}, f32[8,8,256]{2,1,0:T(8,128)S(1)}, u32[]{:S(2)}, u32[]{:S(2)}) collective-permute-start(f32[8,8,256]{2,1,0:T(8,128)S(1)} %get-tuple-element.51), channel_id=1, source_target_pairs={{0,1},{1,0},{2,3},{3,2},{4,5},{5,4},{6,7},{7,6},{8,9},{9,8},{10,11... | collective-permute-start | bytes 196616 | tf_op jit(solution)/shard_map/ppermute | solution.py:509
  18.6 1.2 %collective-permute-start.3 = (f32[8,8,256]{2,1,0:T(8,128)S(1)}, f32[8,8,256]{2,1,0:T(8,128)S(1)}, u32[]{:S(2)}, u32[]{:S(2)}) collective-permute-start(f32[8,8,256]{2,1,0:T(8,128)S(1)} %get-tuple-element.52), channel_id=1, source_target_pairs={{0,8},{1,2},{2,1},{3,4},{4,3},{5,6},{6,5},{7,127},{8,0},{9,10},{10... | collective-permute-start | bytes 196616 | tf_op jit(solution)/shard_map/ppermute | solution.py:509
  19.8 3.5 %shard_map.58 = (f32[64,8,256]{2,1,0:T(8,128)S(1)}, f32[2,8,256]{2,1,0:T(8,128)S(1)}) custom-call(f32[64,8,256]{2,1,0:T(8,128)S(1)} %get-tuple-element.43.refs_4_.refs_0_.refs_2_, f32[64,8,256]{2,1,0:T(8,128)S(1)} %get-tuple-element.44.refs_5_.refs_1_.refs_3_, f32[64,8,256]{2,1,0:T(8,128)S(1)} %get-tuple-element.45.refs_6_.refs_2_.refs_4_, ...), custom_call_target="tpu_custom_call" | custom-call | flops 20000000 | bytes 10000000 | tf_op jit(solution)/shard_map/pallas_call | solution.py:481
  23.3 0.0 collective-permute-done.2.refs_0_
  23.3 2.9 %collective-permute-done.3.refs_1_ = f32[8,8,256]{2,1,0:T(8,128)S(1)} collective-permute-done((f32[8,8,256]{2,1,0:T(8,128)S(1)}, f32[8,8,256]{2,1,0:T(8,128)S(1)}, u32[]{:S(2)}, u32[]{:S(2)}) %collective-permute-start.3) | collective-permute-done | bytes 65568 | tf_op jit(solution)/shard_map/ppermute | solution.py:509
  26.2 1.5 %shard_map.59 = f32[8,64,256]{2,1,0:T(8,128)} custom-call(f32[8,8,256]{2,1,0:T(8,128)S(1)} %collective-permute-done.2.refs_0_, f32[8,8,256]{2,1,0:T(8,128)S(1)} %collective-permute-done.3.refs_1_, f32[64,8,256]{2,1,0:T(8,128)S(1)} %get-tuple-element.43.refs_4_.refs_0_.refs_2_, f32[64,8,256]{2,1,0:T(8,128)S(1)} %get-tuple-element.44.refs_5_.refs_1_.refs_3_, ...), custom_call_target="tpu_custom_call" | custom-call | tf_op jit(solution)/shard_map/pallas_call | solution.py:538
Async XLA Ops:
  0.0 1.1 %copy-start = (f32[3,4,64,256]{3,2,1,0:T(8,128)S(1)}, f32[3,4,64,256]{3,2,1,0:T(8,128)}, u32[]{:S(2)}) copy-start(f32[3,4,64,256]{3,2,1,0:T(8,128)} %param.6) | copy-start | bytes 2359300
  1.1 1.0 %copy-start.1 = (f32[2,4,64,256]{3,2,1,0:T(8,128)S(1)}, f32[2,4,64,256]{3,2,1,0:T(8,128)}, u32[]{:S(2)}) copy-start(f32[2,4,64,256]{3,2,1,0:T(8,128)} %param.5) | copy-start | bytes 1572868
  2.2 1.0 %copy-start.2 = (f32[2,4,64,256]{3,2,1,0:T(8,128)S(1)}, f32[2,4,64,256]{3,2,1,0:T(8,128)}, u32[]{:S(2)}) copy-start(f32[2,4,64,256]{3,2,1,0:T(8,128)} %param.7) | copy-start | bytes 1572868
  3.2 0.9 %copy-start.3 = (f32[4,64,256]{2,1,0:T(8,128)S(1)}, f32[4,64,256]{2,1,0:T(8,128)}, u32[]{:S(2)}) copy-start(f32[4,64,256]{2,1,0:T(8,128)} %refs_3_.1) | copy-start | bytes 786436
  4.2 0.9 %copy-start.4 = (s32[4,64,256]{2,1,0:T(8,128)S(1)}, s32[4,64,256]{2,1,0:T(8,128)}, u32[]{:S(2)}) copy-start(s32[4,64,256]{2,1,0:T(8,128)} %refs_4_.1) | copy-start | bytes 786436
  7.8 9.8 %collective-permute-start = (f32[10,8,128]{2,1,0:T(8,128)S(1)}, f32[10,8,128]{2,1,0:T(8,128)S(1)}, u32[]{:S(2)}, u32[]{:S(2)}) collective-permute-start(f32[10,8,128]{2,1,0:T(8,128)S(1)} %get-tuple-element.31.refs_2_), channel_id=1, source_target_pairs={{0,120},{1,121},{2,122},{3,123},{4,124},{5,125},{6,126},{7,127},{8... | collective-permute-start | bytes 122888 | tf_op jit(solution)/shard_map/ppermute | solution.py:509
  11.1 6.5 %collective-permute-start.1 = (f32[10,8,128]{2,1,0:T(8,128)S(1)}, f32[10,8,128]{2,1,0:T(8,128)S(1)}, u32[]{:S(2)}, u32[]{:S(2)}) collective-permute-start(f32[10,8,128]{2,1,0:T(8,128)S(1)} %get-tuple-element.31.refs_2_), channel_id=1, source_target_pairs={{0,8},{1,9},{2,10},{3,11},{4,12},{5,13},{6,14},{7,15},{8,0},{9,1},... | collective-permute-start | bytes 122888 | tf_op jit(solution)/shard_map/ppermute | solution.py:509
  18.1 5.2 %collective-permute-start.2 = (f32[8,8,256]{2,1,0:T(8,128)S(1)}, f32[8,8,256]{2,1,0:T(8,128)S(1)}, u32[]{:S(2)}, u32[]{:S(2)}) collective-permute-start(f32[8,8,256]{2,1,0:T(8,128)S(1)} %get-tuple-element.51), channel_id=1, source_target_pairs={{0,1},{1,0},{2,3},{3,2},{4,5},{5,4},{6,7},{7,6},{8,9},{9,8},{10,11... | collective-permute-start | bytes 196616 | tf_op jit(solution)/shard_map/ppermute | solution.py:509
  18.6 7.6 %collective-permute-start.3 = (f32[8,8,256]{2,1,0:T(8,128)S(1)}, f32[8,8,256]{2,1,0:T(8,128)S(1)}, u32[]{:S(2)}, u32[]{:S(2)}) collective-permute-start(f32[8,8,256]{2,1,0:T(8,128)S(1)} %get-tuple-element.52), channel_id=1, source_target_pairs={{0,8},{1,2},{2,1},{3,4},{4,3},{5,6},{6,5},{7,127},{8,0},{9,10},{10... | collective-permute-start | bytes 196616 | tf_op jit(solution)/shard_map/ppermute | solution.py:509

commit v3 on v2

--- a/solution.py
+++ b/solution.py
@@ -11,7 +11,6 @@
 F32 = jnp.float32
 VMEM = pl.BlockSpec(memory_space=pltpu.VMEM)
 LIMIT = 16 * 1024 * 1024
-FIELDS = ("c", "m", "u", "v", "w", "sx", "k", "sy")
 GROUPS = ("c", "mu", "vw", "sk")
 
 
@@ -31,22 +30,33 @@
     return jnp.where(low_of(), pltpu.roll(x, 4, 0), x)
 
 
-def load_rows(halves, row):
-    out = []
-    for tracer, velocity, slope, kappa, mask in halves:
-        eight = lambda ref, start: ref.reshape(ref.shape[0] * ROWS, LANES)[pl.ds(start + row, 8, stride=ROWS), :]
-        four = lambda ref: ref.reshape(ref.shape[0] * ROWS, LANES)[pl.ds(row, 4, stride=ROWS), :]
-        out.append(
-            {
-                "c": eight(tracer, 0),
-                "uv": eight(velocity, 0),
-                "vw": eight(velocity, 4 * ROWS),
-                "s": eight(slope, 0),
-                "k": four(kappa),
-                "m": four(mask).astype(F32),
-            }
-        )
-    return out
+def eight(ref, start, row):
+    return ref.reshape(ref.shape[0] * ROWS, LANES)[pl.ds(start * ROWS + row, 8, stride=ROWS), :]
+
+
+def four(ref, row):
+    return ref.reshape(ref.shape[0] * ROWS, LANES)[pl.ds(row, 4, stride=ROWS), :].astype(F32)
+
+
+def field_half(parts, name, row, h):
+    tracer, velocity, slope, kappa, mask = parts[h::2]
+    if name == "c":
+        return eight(tracer, 0, row)
+    if name == "u":
+        return twice_low(eight(velocity, 0, row))
+    if name == "v":
+        return twice_low(eight(velocity, 4, row))
+    if name == "w":
+        return twice_high(eight(velocity, 4, row))
+    if name == "sx":
+        return twice_low(eight(slope, 0, row))
+    if name == "sy":
+        return twice_high(eight(slope, 0, row))
+    return jnp.concatenate([four(kappa if name == "k" else mask, row)] * 2, axis=0)
+
+
+def field_tiles(parts, name, row):
+    return [field_half(parts, name, row, h) for h in range(2)]
 
 
 def pack_kernel(*refs):
@@ -61,21 +71,23 @@
             copies.append(part)
     for part in copies:
         part.wait()
-    halves = [parts[0::2], parts[1::2]]
     lane, low = lane_of(), low_of()
+    rim_of = lambda load: jnp.where(lane < 64, load(0), load(1))
 
     def group(g, carry):
         first = second = jnp.zeros((8, LANES), F32)
         for part in range(8):
-            left, right = load_rows(halves, part * 8 + g)
-            rim = {n: jnp.where(lane[: left[n].shape[0]] < 64, left[n], right[n]) for n in left}
-            mk = jnp.concatenate([rim["m"], rim["k"]], axis=0)
-            mu = jnp.where(low, mk, pltpu.roll(rim["uv"], 4, 0))
-            sk = jnp.where(low, rim["s"], mk)
+            row = part * 8 + g
+            c, uv, vw, s = [
+                rim_of(lambda h: eight(parts[2 * i + h], start, row)) for i, start in ((0, 0), (1, 0), (1, 4), (2, 0))
+            ]
+            mk = rim_of(lambda h: jnp.concatenate([four(parts[8 + h], row), four(parts[6 + h], row)], axis=0))
+            mu = jnp.where(low, mk, pltpu.roll(uv, 4, 0))
+            sk = jnp.where(low, s, mk)
             base = 16 * part
             before, half = lane < base, lane < base + 8
-            one = jnp.where(half, pltpu.roll(rim["c"], (base + 4) % LANES, 1), pltpu.roll(mu, (base + 12) % LANES, 1))
-            two = jnp.where(half, pltpu.roll(rim["vw"], (base + 4) % LANES, 1), pltpu.roll(sk, (base + 12) % LANES, 1))
+            one = jnp.where(half, pltpu.roll(c, (base + 4) % LANES, 1), pltpu.roll(mu, (base + 12) % LANES, 1))
+            two = jnp.where(half, pltpu.roll(vw, (base + 4) % LANES, 1), pltpu.roll(sk, (base + 12) % LANES, 1))
             first = jnp.where(before, first, one)
             second = jnp.where(before, second, two)
         message[g] = first
@@ -92,45 +104,24 @@
         message[8 + pair] = total
 
 
-def rows_kernel(*refs):
-    parts, outs, advected = refs[:10], dict(zip(FIELDS, refs[10:18])), refs[18]
-    halves = [parts[0::2], parts[1::2]]
-
-    def row_group(block, carry):
-        for inner in range(8):
-            row = block * 8 + inner
-            for half, values in enumerate(load_rows(halves, row)):
-                full = {
-                    "c": values["c"],
-                    "m": jnp.concatenate([values["m"]] * 2, axis=0),
-                    "u": twice_low(values["uv"]),
-                    "v": twice_low(values["vw"]),
-                    "w": twice_high(values["vw"]),
-                    "sx": twice_low(values["s"]),
-                    "sy": twice_high(values["s"]),
-                    "k": jnp.concatenate([values["k"]] * 2, axis=0),
-                }
-                for name in FIELDS:
-                    outs[name][row, :, half * LANES : (half + 1) * LANES] = full[name]
-        return carry
-
-    lax.fori_loop(0, ROWS // 8, row_group, 0)
-    get = lambda name, row: tiles_of(outs[name], row, 2)
+def advect_kernel(*refs):
+    parts, advected = refs[:10], refs[10]
+    get = lambda name, row: field_tiles(parts, name, row)
 
     def advect_block(block, carry):
-        first = 2 + 10 * block
-        for j, tiles in enumerate(advect_rows(get, first, 10)):
+        first = 2 + 15 * block
+        for j, tiles in enumerate(advect_rows(get, first, 15)):
             for t in range(2):
                 advected[first + j, :, t * LANES : (t + 1) * LANES] = tiles[t]
         return carry
 
-    lax.fori_loop(0, 6, advect_block, 0)
+    lax.fori_loop(0, 4, advect_block, 0)
 
 
 def edge_kernel(*refs):
     from_far, from_near, own, spare = refs[:4]
-    fields = dict(zip(FIELDS, refs[4:12]))
-    strips, send_a, send_b = refs[12:]
+    parts = refs[4:14]
+    strips, send_a, send_b = refs[15:]
     lane, low = lane_of(), low_of()
     lon, lat = lax.axis_index("lon"), lax.axis_index("lat")
     slot = lane % 16
@@ -156,7 +147,7 @@
 
     def message(top):
         row = lambda q: jnp.where(top, ROWS - 1 - q, q)
-        part = lambda name, q, h: fields[name][row(q), :, h * LANES : (h + 1) * LANES]
+        part = lambda name, q, h: field_half(parts, name, row(q), h)
         pair = lambda n1, q1, n2, q2: [jnp.where(low, part(n1, q1, h), part(n2, q2, h)) for h in range(2)]
         tiles = [[part("c", q, h) for h in range(2)] for q in range(3)]
         tiles += [pair("m", 0, "v", 0), pair("m", 1, "v", 1), pair("m", 2, "u", 0), pair("w", 0, "sy", 0)]
@@ -358,8 +349,8 @@
 
 
 def interior_kernel(*refs):
-    fields, advected, strips = dict(zip(FIELDS, refs[:8])), refs[8], refs[9]
-    out, kept, narrow = refs[10:]
+    parts, advected, strips = refs[:10], refs[10], refs[11]
+    out, kept, narrow = refs[12:]
     lane = lane_of()
     near_east, near_west = lane >= LANES - 2, lane < 2
 
@@ -381,7 +372,7 @@
 
     def get(name, row):
         if name != "a":
-            return tiles_of(fields[name], row, 2)
+            return field_tiles(parts, name, row)
         left, right = tiles_of(advected, row, 2)
         return [
             jnp.where(near_west, lanes_to(0, row, 10, 0), left),
@@ -407,8 +398,8 @@
 
 def rim_kernel(*refs):
     got_a, got_b = refs[0], refs[1]
-    fields = dict(zip(FIELDS, refs[2:10]))
-    strips, inner, kept, out, edges, sems = refs[10:]
+    parts = refs[2:12]
+    strips, inner, kept, out, edges, sems = refs[12:]
     middle = pltpu.make_async_copy
     copies = [middle(inner.at[8:56, i], out.at[i, 8:56], sems.at[i]) for i in range(8)]
     for copy in copies:
@@ -458,9 +449,8 @@
                 return rows[-row - 1][name]
             if row >= ROWS:
                 return rows[row - ROWS][name]
-            if name == "sy":
-                return tiles_of(fields[name], row, 2)
-            return tiles_of(fields[name], row, 2) + [sides[row][name]]
+            tiles = field_tiles(parts, name, row)
+            return tiles if name == "sy" else tiles + [sides[row][name]]
 
         for j, tiles in enumerate(advect_rows(get, start, 4)):
             made[start + j] = tiles
@@ -511,38 +501,39 @@
     def shards(tracers, velocity, slopes, diffusivity, sea_mask):
         plane = lambda x: x.reshape(-1, ROWS, 2 * LANES)
         arrays = [plane(tracers), plane(velocity), plane(slopes), diffusivity, sea_mask]
+        arrays = [pltpu.with_memory_space_constraint(x, pltpu.HBM) for x in arrays]
         full, side = (ROWS, 8, 2 * LANES), (8, 8, LANES)
         *parts, packed, spare = pl.pallas_call(
             pack_kernel,
             out_shape=[jax.ShapeDtypeStruct(x.shape[:2] + (LANES,), x.dtype) for x in arrays for _ in range(2)]
             + [jax.ShapeDtypeStruct((10, 8, LANES), F32), jax.ShapeDtypeStruct(side, F32)],
-            in_specs=[pl.BlockSpec(memory_space=pl.ANY)] * 5,
+            in_specs=[pl.BlockSpec(memory_space=pltpu.HBM)] * 5,
             out_specs=[VMEM] * 12,
             scratch_shapes=[pltpu.SemaphoreType.DMA((10,))],
             compiler_params=pltpu.CompilerParams(vmem_limit_bytes=LIMIT),
         )(*arrays)
         far_got, near_got = move(packed, far), move(packed, near)
-        *fields, advected = call(
-            rows_kernel, [full] * 9, *parts,
+        (advected,) = call(
+            advect_kernel, [full], *parts,
             cost_estimate=pl.CostEstimate(flops=10**7, bytes_accessed=6 * 10**6, transcendentals=0),
         )
         strips, send_a, send_b = call(
-            edge_kernel, [(4,) + side, (8, 8, 2 * LANES), (8, 8, 2 * LANES)], far_got, near_got, packed, spare, *fields
+            edge_kernel, [(4,) + side, (8, 8, 2 * LANES), (8, 8, 2 * LANES)], far_got, near_got, packed, spare, *parts, advected
         )
         got_b, got_a = move(send_b, pair_b), move(send_a, pair_a)
         inner, kept = call(
-            interior_kernel, [full, (2, 8, 2 * LANES)], *fields, advected, strips,
+            interior_kernel, [full, (2, 8, 2 * LANES)], *parts, advected, strips,
             scratch_shapes=[pltpu.VMEM((3,) + side, F32)],
             cost_estimate=pl.CostEstimate(flops=2 * 10**7, bytes_accessed=10**7, transcendentals=0),
         )
         out = pl.pallas_call(
             rim_kernel,
             out_shape=jax.ShapeDtypeStruct((8, ROWS, 2 * LANES), F32),
-            in_specs=[VMEM] * 13,
+            in_specs=[VMEM] * 15,
             out_specs=pl.BlockSpec(memory_space=pl.ANY),
             scratch_shapes=[pltpu.VMEM((2, 8, 8, 2 * LANES), F32), pltpu.SemaphoreType.DMA((10,))],
             compiler_params=pltpu.CompilerParams(vmem_limit_bytes=LIMIT),
-        )(got_a, got_b, *fields, strips, inner, kept)
+        )(got_a, got_b, *parts, strips, inner, kept)
         return out.reshape(tracers.shape)
 
     return shards

time: 28 us -> 23 us (0.82)
  the two profiles are of different devices: /device:TPU:39 before, /device:TPU:38 now
where the time goes in v3:
time: 23 us; the launch traced here: 22.9 us
  Pallas kernels  12.1 us (53%)
  starting transfers between devices  10.7 us (47%)
    ppermute x4, starting transfers between devices, move(): return lax.ppermute(x, ('lon', 'lat'), route)  10.7 us
    pallas_call x3, Pallas kernels, call(): pl.pallas_call(kernel, out_shape=[jax.ShapeDtypeStruct(s, F32) for s in s...  6.55 us
    pallas_call x1, Pallas kernels, shards(): pl.pallas_call(pack_kernel, out_shape=[jax.ShapeDtypeStruct(x.shape[:2] +...  4 us
    pallas_call x1, Pallas kernels, shards(): pl.pallas_call(rim_kernel, out_shape=jax.ShapeDtypeStruct((8, ROWS, 2 * L...  1.56 us
  transfers between devices with their start and end apart: 4, of which 0 were waited for; matrix products, arithmetic and copies ran while one was open for 0% of the time, Pallas kernels for 26%

profile of v3, /device:TPU:38, one launch (start us, length us, event | category | flops | bytes accessed | tf_op | source)
XLA Modules:
  0.0 22.9 jit_solution(14191976556848815418)
XLA Ops:
  0.0 4.0 %shard_map.55 = (f32[8,64,128]{2,1,0:T(8,128)S(1)}, f32[8,64,128]{2,1,0:T(8,128)S(1)}, f32[12,64,128]{2,1,0:T(8,128)S(1)}, f32[12,64,128]{2,1,0:T(8,128)S(1)}, f...) custom-call(f32[8,64,256]{2,1,0:T(8,128)} %bitcast.5, ...), custom_call_target="tpu_custom_call" | custom-call | tf_op jit(solution)/shard_map/pallas_call | solution.py:506
  4.0 0.1 collective-permute-start.1
  4.1 5.5 %collective-permute-start = (f32[10,8,128]{2,1,0:T(8,128)S(1)}, f32[10,8,128]{2,1,0:T(8,128)S(1)}, u32[]{:S(2)}, u32[]{:S(2)}) collective-permute-start(f32[10,8,128]{2,1,0:T(8,128)S(1)} %get-tuple-element.22.refs_2_), channel_id=1, source_target_pairs={{0,120},{1,121},{2,122},{3,123},{4,124},{5,125},{6,126},{7,127},{8... | collective-permute-start | bytes 122888 | tf_op jit(solution)/shard_map/ppermute | solution.py:499
  9.6 2.5 %shard_map.56.refs_14_.refs_10_ = f32[64,8,256]{2,1,0:T(8,128)S(1)} custom-call(f32[8,64,128]{2,1,0:T(8,128)S(1)} %get-tuple-element.24.refs_0_.refs_4_.refs_2_, f32[8,64,128]{2,1,0:T(8,128)S(1)} %get-tuple-element.25.refs_1_.refs_5_.refs_3_, f32[12,64,128]{2,1,0:T(8,128)S(1)} %get-tuple-element.26.refs_2_.refs_6_.refs_4_, ...), custom_call_target="tpu_custom_call" | custom-call | flops 10000000 | bytes 6000000 | tf_op jit(solution)/shard_map/pallas_call | solution.py:471
  12.1 0.0 collective-permute-done.1.refs_1_
  12.1 0.0 collective-permute-done.refs_0_
  12.1 0.5 %shard_map.57 = (f32[4,8,8,128]{3,2,1,0:T(8,128)S(1)}, f32[8,8,256]{2,1,0:T(8,128)S(1)}, f32[8,8,256]{2,1,0:T(8,128)S(1)}) custom-call(f32[10,8,128]{2,1,0:T(8,128)S(1)} %collective-permute-done.refs_0_, f32[10,8,128]{2,1,0:T(8,128)S(1)} %collective-permute-done.1.refs_1_, f32[10,8,128]{2,1,0:T(8,128)S(1)} %get-tuple-element.22.refs_2_, ...), custom_call_target="tpu_custom_call" | custom-call | tf_op jit(solution)/shard_map/pallas_call | solution.py:471
  12.7 0.8 %collective-permute-start.2 = (f32[8,8,256]{2,1,0:T(8,128)S(1)}, f32[8,8,256]{2,1,0:T(8,128)S(1)}, u32[]{:S(2)}, u32[]{:S(2)}) collective-permute-start(f32[8,8,256]{2,1,0:T(8,128)S(1)} %get-tuple-element.34), channel_id=1, source_target_pairs={{0,1},{1,0},{2,3},{3,2},{4,5},{5,4},{6,7},{7,6},{8,9},{9,8},{10,11... | collective-permute-start | bytes 196616 | tf_op jit(solution)/shard_map/ppermute | solution.py:499
  13.5 4.3 %collective-permute-start.3 = (f32[8,8,256]{2,1,0:T(8,128)S(1)}, f32[8,8,256]{2,1,0:T(8,128)S(1)}, u32[]{:S(2)}, u32[]{:S(2)}) collective-permute-start(f32[8,8,256]{2,1,0:T(8,128)S(1)} %get-tuple-element.35), channel_id=1, source_target_pairs={{0,8},{1,2},{2,1},{3,4},{4,3},{5,6},{6,5},{7,127},{8,0},{9,10},{10... | collective-permute-start | bytes 196616 | tf_op jit(solution)/shard_map/ppermute | solution.py:499
  17.8 3.6 %shard_map.58 = (f32[64,8,256]{2,1,0:T(8,128)S(1)}, f32[2,8,256]{2,1,0:T(8,128)S(1)}) custom-call(f32[8,64,128]{2,1,0:T(8,128)S(1)} %get-tuple-element.24.refs_0_.refs_4_.refs_2_, f32[8,64,128]{2,1,0:T(8,128)S(1)} %get-tuple-element.25.refs_1_.refs_5_.refs_3_, f32[12,64,128]{2,1,0:T(8,128)S(1)} %get-tuple-element.26.refs_2_.refs_6_.refs_4_, ...), custom_call_target="tpu_custom_call" | custom-call | flops 20000000 | bytes 10000000 | tf_op jit(solution)/shard_map/pallas_call | solution.py:471
  21.3 0.0 collective-permute-done.2.refs_0_
  21.3 0.0 collective-permute-done.3.refs_1_
  21.3 1.6 %shard_map.59 = f32[8,64,256]{2,1,0:T(8,128)} custom-call(f32[8,8,256]{2,1,0:T(8,128)S(1)} %collective-permute-done.2.refs_0_, f32[8,8,256]{2,1,0:T(8,128)S(1)} %collective-permute-done.3.refs_1_, f32[8,64,128]{2,1,0:T(8,128)S(1)} %get-tuple-element.24.refs_0_.refs_4_.refs_2_, f32[8,64,128]{2,1,0:T(8,128)S(1)} %get-tuple-element.25.refs_1_.refs_5_.refs_3_, ...), custom_call_target="tpu_custom_call" | custom-call | tf_op jit(solution)/shard_map/pallas_call | solution.py:529
Async XLA Ops:
  4.0 8.1 %collective-permute-start.1 = (f32[10,8,128]{2,1,0:T(8,128)S(1)}, f32[10,8,128]{2,1,0:T(8,128)S(1)}, u32[]{:S(2)}, u32[]{:S(2)}) collective-permute-start(f32[10,8,128]{2,1,0:T(8,128)S(1)} %get-tuple-element.22.refs_2_), channel_id=1, source_target_pairs={{0,8},{1,9},{2,10},{3,11},{4,12},{5,13},{6,14},{7,15},{8,0},{9,1},... | collective-permute-start | bytes 122888 | tf_op jit(solution)/shard_map/ppermute | solution.py:499
  4.1 8.0 %collective-permute-start = (f32[10,8,128]{2,1,0:T(8,128)S(1)}, f32[10,8,128]{2,1,0:T(8,128)S(1)}, u32[]{:S(2)}, u32[]{:S(2)}) collective-permute-start(f32[10,8,128]{2,1,0:T(8,128)S(1)} %get-tuple-element.22.refs_2_), channel_id=1, source_target_pairs={{0,120},{1,121},{2,122},{3,123},{4,124},{5,125},{6,126},{7,127},{8... | collective-permute-start | bytes 122888 | tf_op jit(solution)/shard_map/ppermute | solution.py:499
  12.7 8.7 %collective-permute-start.2 = (f32[8,8,256]{2,1,0:T(8,128)S(1)}, f32[8,8,256]{2,1,0:T(8,128)S(1)}, u32[]{:S(2)}, u32[]{:S(2)}) collective-permute-start(f32[8,8,256]{2,1,0:T(8,128)S(1)} %get-tuple-element.34), channel_id=1, source_target_pairs={{0,1},{1,0},{2,3},{3,2},{4,5},{5,4},{6,7},{7,6},{8,9},{9,8},{10,11... | collective-permute-start | bytes 196616 | tf_op jit(solution)/shard_map/ppermute | solution.py:499
  13.5 7.8 %collective-permute-start.3 = (f32[8,8,256]{2,1,0:T(8,128)S(1)}, f32[8,8,256]{2,1,0:T(8,128)S(1)}, u32[]{:S(2)}, u32[]{:S(2)}) collective-permute-start(f32[8,8,256]{2,1,0:T(8,128)S(1)} %get-tuple-element.35), channel_id=1, source_target_pairs={{0,8},{1,2},{2,1},{3,4},{4,3},{5,6},{6,5},{7,127},{8,0},{9,10},{10... | collective-permute-start | bytes 196616 | tf_op jit(solution)/shard_map/ppermute | solution.py:499

commit v4 on v3

--- a/solution.py
+++ b/solution.py
@@ -74,7 +74,7 @@
     lane, low = lane_of(), low_of()
     rim_of = lambda load: jnp.where(lane < 64, load(0), load(1))
 
-    def group(g, carry):
+    def group(g):
         first = second = jnp.zeros((8, LANES), F32)
         for part in range(8):
             row = part * 8 + g
@@ -92,9 +92,9 @@
             second = jnp.where(before, second, two)
         message[g] = first
         spare[g] = second
-        return carry
-
-    lax.fori_loop(0, 8, group, 0)
+
+    for g in range(8):
+        group(g)
     slot = lane % 8
     for pair in range(2):
         total = pltpu.roll(spare[4 * pair], LANES - 2, 1)
@@ -119,7 +119,7 @@
 
 
 def edge_kernel(*refs):
-    from_far, from_near, own, spare = refs[:4]
+    from_near, from_far, own, spare = refs[:4]
     parts = refs[4:14]
     strips, send_a, send_b = refs[15:]
     lane, low = lane_of(), low_of()
@@ -387,17 +387,17 @@
             kept[i, :, t * LANES : (t + 1) * LANES] = tile
 
     def diffuse_block(block, carry):
-        first = jnp.minimum(3 + 6 * block, ROWS - 3 - 6)
-        for j, tiles in enumerate(diffuse_rows(get, first, 6, beside)):
+        first = jnp.minimum(3 + 10 * block, ROWS - 3 - 10)
+        for j, tiles in enumerate(diffuse_rows(get, first, 10, beside)):
             for t in range(2):
                 out[first + j, :, t * LANES : (t + 1) * LANES] = tiles[t]
         return carry
 
-    lax.fori_loop(0, 10, diffuse_block, 0)
+    lax.fori_loop(0, 6, diffuse_block, 0)
 
 
 def rim_kernel(*refs):
-    got_a, got_b = refs[0], refs[1]
+    got_b, got_a = refs[0], refs[1]
     parts = refs[2:12]
     strips, inner, kept, out, edges, sems = refs[12:]
     middle = pltpu.make_async_copy
@@ -518,7 +518,7 @@
             cost_estimate=pl.CostEstimate(flops=10**7, bytes_accessed=6 * 10**6, transcendentals=0),
         )
         strips, send_a, send_b = call(
-            edge_kernel, [(4,) + side, (8, 8, 2 * LANES), (8, 8, 2 * LANES)], far_got, near_got, packed, spare, *parts, advected
+            edge_kernel, [(4,) + side, (8, 8, 2 * LANES), (8, 8, 2 * LANES)], near_got, far_got, packed, spare, *parts, advected
         )
         got_b, got_a = move(send_b, pair_b), move(send_a, pair_a)
         inner, kept = call(
@@ -533,7 +533,7 @@
             out_specs=pl.BlockSpec(memory_space=pl.ANY),
             scratch_shapes=[pltpu.VMEM((2, 8, 8, 2 * LANES), F32), pltpu.SemaphoreType.DMA((10,))],
             compiler_params=pltpu.CompilerParams(vmem_limit_bytes=LIMIT),
-        )(got_a, got_b, *parts, strips, inner, kept)
+        )(got_b, got_a, *parts, strips, inner, kept)
         return out.reshape(tracers.shape)
 
     return shards

time: 23 us -> 22.1 us (0.961)
  the two profiles are of different devices: /device:TPU:38 before, /device:TPU:36 now
where the time goes in v4:
time: 22.1 us; the launch traced here: 22 us
  Pallas kernels  11.1 us (50%)
  starting transfers between devices  10.8 us (49%)
    ppermute x4, starting transfers between devices, move(): return lax.ppermute(x, ('lon', 'lat'), route)  10.8 us
    pallas_call x3, Pallas kernels, call(): pl.pallas_call(kernel, out_shape=[jax.ShapeDtypeStruct(s, F32) for s in s...  6.18 us
    pallas_call x1, Pallas kernels, shards(): pl.pallas_call(pack_kernel, out_shape=[jax.ShapeDtypeStruct(x.shape[:2] +...  3.34 us
    pallas_call x1, Pallas kernels, shards(): pl.pallas_call(rim_kernel, out_shape=jax.ShapeDtypeStruct((8, ROWS, 2 * L...  1.56 us
  transfers between devices with their start and end apart: 4, of which 0 were waited for; matrix products, arithmetic and copies ran while one was open for 0% of the time, Pallas kernels for 26%

profile of v4, /device:TPU:36, one launch (start us, length us, event | category | flops | bytes accessed | tf_op | source)
XLA Modules:
  0.0 22.0 jit_solution(5096632659794053896)
XLA Ops:
  0.0 3.3 %shard_map.55 = (f32[8,64,128]{2,1,0:T(8,128)S(1)}, f32[8,64,128]{2,1,0:T(8,128)S(1)}, f32[12,64,128]{2,1,0:T(8,128)S(1)}, f32[12,64,128]{2,1,0:T(8,128)S(1)}, f...) custom-call(f32[8,64,256]{2,1,0:T(8,128)} %bitcast.5, ...), custom_call_target="tpu_custom_call" | custom-call | tf_op jit(solution)/shard_map/pallas_call | solution.py:506
  3.4 4.9 %collective-permute-start.1 = (f32[10,8,128]{2,1,0:T(8,128)S(1)}, f32[10,8,128]{2,1,0:T(8,128)S(1)}, u32[]{:S(2)}, u32[]{:S(2)}) collective-permute-start(f32[10,8,128]{2,1,0:T(8,128)S(1)} %get-tuple-element.22.refs_2_), channel_id=1, source_target_pairs={{0,120},{1,121},{2,122},{3,123},{4,124},{5,125},{6,126},{7,127},{8... | collective-permute-start | bytes 122888 | tf_op jit(solution)/shard_map/ppermute | solution.py:499
  8.3 0.0 collective-permute-start
  8.3 2.5 %shard_map.56.refs_14_.refs_10_ = f32[64,8,256]{2,1,0:T(8,128)S(1)} custom-call(f32[8,64,128]{2,1,0:T(8,128)S(1)} %get-tuple-element.24.refs_0_.refs_4_.refs_2_, f32[8,64,128]{2,1,0:T(8,128)S(1)} %get-tuple-element.25.refs_1_.refs_5_.refs_3_, f32[12,64,128]{2,1,0:T(8,128)S(1)} %get-tuple-element.26.refs_2_.refs_6_.refs_4_, ...), custom_call_target="tpu_custom_call" | custom-call | flops 10000000 | bytes 6000000 | tf_op jit(solution)/shard_map/pallas_call | solution.py:471
  10.8 0.0 collective-permute-done.1.refs_1_
  10.8 0.0 collective-permute-done.refs_0_
  10.8 0.5 %shard_map.57 = (f32[4,8,8,128]{3,2,1,0:T(8,128)S(1)}, f32[8,8,256]{2,1,0:T(8,128)S(1)}, f32[8,8,256]{2,1,0:T(8,128)S(1)}) custom-call(f32[10,8,128]{2,1,0:T(8,128)S(1)} %collective-permute-done.refs_0_, f32[10,8,128]{2,1,0:T(8,128)S(1)} %collective-permute-done.1.refs_1_, f32[10,8,128]{2,1,0:T(8,128)S(1)} %get-tuple-element.22.refs_2_, ...), custom_call_target="tpu_custom_call" | custom-call | tf_op jit(solution)/shard_map/pallas_call | solution.py:471
  11.3 0.6 %collective-permute-start.2 = (f32[8,8,256]{2,1,0:T(8,128)S(1)}, f32[8,8,256]{2,1,0:T(8,128)S(1)}, u32[]{:S(2)}, u32[]{:S(2)}) collective-permute-start(f32[8,8,256]{2,1,0:T(8,128)S(1)} %get-tuple-element.34), channel_id=1, source_target_pairs={{0,8},{1,2},{2,1},{3,4},{4,3},{5,6},{6,5},{7,127},{8,0},{9,10},{10... | collective-permute-start | bytes 196616 | tf_op jit(solution)/shard_map/ppermute | solution.py:499
  11.9 5.3 %collective-permute-start.3 = (f32[8,8,256]{2,1,0:T(8,128)S(1)}, f32[8,8,256]{2,1,0:T(8,128)S(1)}, u32[]{:S(2)}, u32[]{:S(2)}) collective-permute-start(f32[8,8,256]{2,1,0:T(8,128)S(1)} %get-tuple-element.35), channel_id=1, source_target_pairs={{0,1},{1,0},{2,3},{3,2},{4,5},{5,4},{6,7},{7,6},{8,9},{9,8},{10,11... | collective-permute-start | bytes 196616 | tf_op jit(solution)/shard_map/ppermute | solution.py:499
  17.1 3.3 %shard_map.58 = (f32[64,8,256]{2,1,0:T(8,128)S(1)}, f32[2,8,256]{2,1,0:T(8,128)S(1)}) custom-call(f32[8,64,128]{2,1,0:T(8,128)S(1)} %get-tuple-element.24.refs_0_.refs_4_.refs_2_, f32[8,64,128]{2,1,0:T(8,128)S(1)} %get-tuple-element.25.refs_1_.refs_5_.refs_3_, f32[12,64,128]{2,1,0:T(8,128)S(1)} %get-tuple-element.26.refs_2_.refs_6_.refs_4_, ...), custom_call_target="tpu_custom_call" | custom-call | flops 20000000 | bytes 10000000 | tf_op jit(solution)/shard_map/pallas_call | solution.py:471
  20.4 0.0 collective-permute-done.2.refs_0_
  20.4 0.0 collective-permute-done.3.refs_1_
  20.4 1.6 %shard_map.59 = f32[8,64,256]{2,1,0:T(8,128)} custom-call(f32[8,8,256]{2,1,0:T(8,128)S(1)} %collective-permute-done.2.refs_0_, f32[8,8,256]{2,1,0:T(8,128)S(1)} %collective-permute-done.3.refs_1_, f32[8,64,128]{2,1,0:T(8,128)S(1)} %get-tuple-element.24.refs_0_.refs_4_.refs_2_, f32[8,64,128]{2,1,0:T(8,128)S(1)} %get-tuple-element.25.refs_1_.refs_5_.refs_3_, ...), custom_call_target="tpu_custom_call" | custom-call | tf_op jit(solution)/shard_map/pallas_call | solution.py:529
Async XLA Ops:
  3.4 7.4 %collective-permute-start.1 = (f32[10,8,128]{2,1,0:T(8,128)S(1)}, f32[10,8,128]{2,1,0:T(8,128)S(1)}, u32[]{:S(2)}, u32[]{:S(2)}) collective-permute-start(f32[10,8,128]{2,1,0:T(8,128)S(1)} %get-tuple-element.22.refs_2_), channel_id=1, source_target_pairs={{0,120},{1,121},{2,122},{3,123},{4,124},{5,125},{6,126},{7,127},{8... | collective-permute-start | bytes 122888 | tf_op jit(solution)/shard_map/ppermute | solution.py:499
  8.3 2.5 %collective-permute-start = (f32[10,8,128]{2,1,0:T(8,128)S(1)}, f32[10,8,128]{2,1,0:T(8,128)S(1)}, u32[]{:S(2)}, u32[]{:S(2)}) collective-permute-start(f32[10,8,128]{2,1,0:T(8,128)S(1)} %get-tuple-element.22.refs_2_), channel_id=1, source_target_pairs={{0,8},{1,9},{2,10},{3,11},{4,12},{5,13},{6,14},{7,15},{8,0},{9,1},... | collective-permute-start | bytes 122888 | tf_op jit(solution)/shard_map/ppermute | solution.py:499
  11.3 9.1 %collective-permute-start.2 = (f32[8,8,256]{2,1,0:T(8,128)S(1)}, f32[8,8,256]{2,1,0:T(8,128)S(1)}, u32[]{:S(2)}, u32[]{:S(2)}) collective-permute-start(f32[8,8,256]{2,1,0:T(8,128)S(1)} %get-tuple-element.34), channel_id=1, source_target_pairs={{0,8},{1,2},{2,1},{3,4},{4,3},{5,6},{6,5},{7,127},{8,0},{9,10},{10... | collective-permute-start | bytes 196616 | tf_op jit(solution)/shard_map/ppermute | solution.py:499
  11.9 8.5 %collective-permute-start.3 = (f32[8,8,256]{2,1,0:T(8,128)S(1)}, f32[8,8,256]{2,1,0:T(8,128)S(1)}, u32[]{:S(2)}, u32[]{:S(2)}) collective-permute-start(f32[8,8,256]{2,1,0:T(8,128)S(1)} %get-tuple-element.35), channel_id=1, source_target_pairs={{0,1},{1,0},{2,3},{3,2},{4,5},{5,4},{6,7},{7,6},{8,9},{9,8},{10,11... | collective-permute-start | bytes 196616 | tf_op jit(solution)/shard_map/ppermute | solution.py:499

commit v5 on v4

--- a/solution.py
+++ b/solution.py
@@ -12,6 +12,7 @@
 VMEM = pl.BlockSpec(memory_space=pltpu.VMEM)
 LIMIT = 16 * 1024 * 1024
 GROUPS = ("c", "mu", "vw", "sk")
+KEPT = (2, 3, ROWS - 4, ROWS - 3)
 
 
 def lane_of():
@@ -38,29 +39,21 @@
     return ref.reshape(ref.shape[0] * ROWS, LANES)[pl.ds(row, 4, stride=ROWS), :].astype(F32)
 
 
-def field_half(parts, name, row, h):
-    tracer, velocity, slope, kappa, mask = parts[h::2]
-    if name == "c":
-        return eight(tracer, 0, row)
-    if name == "u":
-        return twice_low(eight(velocity, 0, row))
-    if name == "v":
-        return twice_low(eight(velocity, 4, row))
-    if name == "w":
-        return twice_high(eight(velocity, 4, row))
-    if name == "sx":
-        return twice_low(eight(slope, 0, row))
-    if name == "sy":
-        return twice_high(eight(slope, 0, row))
-    return jnp.concatenate([four(kappa if name == "k" else mask, row)] * 2, axis=0)
-
-
-def field_tiles(parts, name, row):
-    return [field_half(parts, name, row, h) for h in range(2)]
+def field_half(rows, name, row, h):
+    which, turn = {
+        "u": (1, twice_low), "v": (1, twice_high), "w": (2, twice_high),
+        "sx": (3, twice_low), "sy": (3, twice_high), "m": (4, twice_low), "k": (4, twice_high),
+    }.get(name, (0, None))
+    value = rows[which][row, :, h * LANES : (h + 1) * LANES]
+    return turn(value) if turn else value
+
+
+def field_tiles(rows, name, row):
+    return [field_half(rows, name, row, h) for h in range(2)]
 
 
 def pack_kernel(*refs):
-    arrays, parts, message, spare, sems = refs[:5], refs[5:15], refs[15], refs[16], refs[17]
+    arrays, rows, message, spare, parts, sems = refs[:5], refs[5:10], refs[10], refs[11], refs[12:22], refs[22]
     copies = []
     for i, array in enumerate(arrays):
         for h in range(2):
@@ -72,16 +65,24 @@
     for part in copies:
         part.wait()
     lane, low = lane_of(), low_of()
-    rim_of = lambda load: jnp.where(lane < 64, load(0), load(1))
+    scale = jnp.where(low, 1.0, 0.5)
 
     def group(g):
         first = second = jnp.zeros((8, LANES), F32)
         for part in range(8):
             row = part * 8 + g
-            c, uv, vw, s = [
-                rim_of(lambda h: eight(parts[2 * i + h], start, row)) for i, start in ((0, 0), (1, 0), (1, 4), (2, 0))
-            ]
-            mk = rim_of(lambda h: jnp.concatenate([four(parts[8 + h], row), four(parts[6 + h], row)], axis=0))
+            rims = []
+            for h in range(2):
+                tracer, velocity, slope, kappa, mask = parts[h::2]
+                mk = jnp.concatenate([four(mask, row), four(kappa, row)], axis=0) * scale
+                loaded = (
+                    eight(tracer, 0, row), eight(velocity, 0, row), eight(velocity, 4, row),
+                    eight(slope, 0, row) * 0.125, mk,
+                )
+                for ref, value in zip(rows, loaded):
+                    ref[row, :, h * LANES : (h + 1) * LANES] = value
+                rims.append(loaded)
+            c, uv, vw, s, mk = [jnp.where(lane < 64, a, b) for a, b in zip(*rims)]
             mu = jnp.where(low, mk, pltpu.roll(uv, 4, 0))
             sk = jnp.where(low, s, mk)
             base = 16 * part
@@ -105,8 +106,8 @@
 
 
 def advect_kernel(*refs):
-    parts, advected = refs[:10], refs[10]
-    get = lambda name, row: field_tiles(parts, name, row)
+    rows, advected = refs[:5], refs[5]
+    get = lambda name, row: field_tiles(rows, name, row)
 
     def advect_block(block, carry):
         first = 2 + 15 * block
@@ -120,8 +121,8 @@
 
 def edge_kernel(*refs):
     from_near, from_far, own, spare = refs[:4]
-    parts = refs[4:14]
-    strips, send_a, send_b = refs[15:]
+    rows = refs[4:9]
+    strips, send_a, send_b = refs[10:]
     lane, low = lane_of(), low_of()
     lon, lat = lax.axis_index("lon"), lax.axis_index("lat")
     slot = lane % 16
@@ -147,7 +148,7 @@
 
     def message(top):
         row = lambda q: jnp.where(top, ROWS - 1 - q, q)
-        part = lambda name, q, h: field_half(parts, name, row(q), h)
+        part = lambda name, q, h: field_half(rows, name, row(q), h)
         pair = lambda n1, q1, n2, q2: [jnp.where(low, part(n1, q1, h), part(n2, q2, h)) for h in range(2)]
         tiles = [[part("c", q, h) for h in range(2)] for q in range(3)]
         tiles += [pair("m", 0, "v", 0), pair("m", 1, "v", 1), pair("m", 2, "u", 0), pair("w", 0, "sy", 0)]
@@ -241,8 +242,8 @@
     positive = speed >= 0.0
     upwind = jnp.where(positive, back, ahead)
     size = jnp.abs(speed)
-    limited = jnp.maximum(jnp.minimum(upwind, step), 0.0) + jnp.minimum(jnp.maximum(upwind, step), 0.0)
-    return speed * jnp.where(positive, here, there) + 0.5 * (size - size * size) * limited
+    limited = jnp.minimum(jnp.maximum(upwind, jnp.minimum(step, 0.0)), jnp.maximum(step, 0.0))
+    return speed * jnp.where(positive, here, there) + (size - size * size) * limited
 
 
 def not_bottom():
@@ -250,18 +251,19 @@
 
 
 def open_below(marker):
-    return jnp.where(not_bottom(), marker * below(marker), 0.0)
-
-
-def face_speed(one, two, opened):
-    return 0.5 * (one + two) * opened
+    return jnp.where(not_bottom(), below(marker), 0.0)
+
+
+def face_speed(one, two, half_open):
+    return (one + two) * half_open
 
 
 def advect_rows(get, first, count):
     c = {j: get("c", first + j) for j in range(-2, count + 2)}
     m = {j: get("m", first + j) for j in range(-2, count + 2)}
     v = {j: get("v", first + j) for j in range(-1, count + 1)}
-    opened = {j: each(jnp.multiply, m[j], m[j + 1]) for j in range(-2, count + 1)}
+    half = {j: each(lambda x: 0.5 * x, m[j]) for j in range(-2, count + 2)}
+    opened = {j: each(jnp.multiply, half[j], m[j + 1]) for j in range(-2, count + 1)}
     step = {j: each(lambda a, b, o: (b - a) * o, c[j], c[j + 1], opened[j]) for j in range(-2, count + 1)}
     flux = {}
     for j in range(-1, count):
@@ -270,7 +272,7 @@
     result = []
     for j in range(count):
         east = plus(c[j])
-        opened_x = each(jnp.multiply, m[j], plus(m[j]))
+        opened_x = each(jnp.multiply, half[j], plus(m[j]))
         u = get("u", first + j)
         speed = each(face_speed, u, plus(u), opened_x)
         step_x = each(lambda a, b, o: (b - a) * o, c[j], east, opened_x)
@@ -278,20 +280,20 @@
         total = each(lambda f, g, a, b: (f - g) + (a - b), flux_x, minus(flux_x), flux[j], flux[j - 1])
         w = get("w", first + j)
 
-        def finish(value, marker, down, across):
-            opened_z = open_below(marker)
+        def finish(value, marker, halved, down, across):
+            opened_z = open_below(halved)
             under = below(value)
             step_z = (under - value) * opened_z
             speed_z = face_speed(down, below(down), opened_z)
             flux_z = face_flux(value, under, speed_z, above(step_z), step_z, below(step_z))
             return (value - across - (flux_z - above(flux_z))) * marker
 
-        result.append(each(finish, c[j], m[j], w, total))
+        result.append(each(finish, c[j], m[j], half[j], w, total))
     return result
 
 
 def slope_flux(k1, k2, opened, step, s1, s2, z1, z2):
-    return 0.5 * (k1 + k2) * opened * (step + 0.125 * (s1 + s2) * (z1 + z2))
+    return (k1 + k2) * opened * (step + (s1 + s2) * (z1 + z2))
 
 
 def eastward(a, m, k, sx, twice_z):
@@ -332,11 +334,10 @@
         total = each(lambda f, g, p, q: (f - g) + (p - q), flux_x, minus(flux_x, 2, west[1]), flux_y[j], flux_y[j - 1])
 
         def finish(value, marker, kappa, east, north, tx, ty, sz, across):
-            face_east, face_north = 0.5 * (east + below(east)), 0.5 * (north + below(north))
-            flux_z = (
-                0.5 * (kappa + below(kappa)) * open_below(marker)
-                * (0.25 * (face_east * (tx + below(tx)) + face_north * (ty + below(ty)))
-                   + (face_east * face_east + face_north * face_north) * sz)
+            face_east, face_north = east + below(east), north + below(north)
+            flux_z = (kappa + below(kappa)) * open_below(marker) * (
+                face_east * (tx + below(tx)) + face_north * (ty + below(ty))
+                + (face_east * face_east + face_north * face_north) * (16.0 * sz)
             )
             return (value + across + (flux_z - above(flux_z))) * marker
 
@@ -349,8 +350,8 @@
 
 
 def interior_kernel(*refs):
-    parts, advected, strips = refs[:10], refs[10], refs[11]
-    out, kept, narrow = refs[12:]
+    rows, advected, strips = refs[:5], refs[5], refs[6]
+    out, kept, narrow = refs[7:]
     lane = lane_of()
     near_east, near_west = lane >= LANES - 2, lane < 2
 
@@ -372,7 +373,7 @@
 
     def get(name, row):
         if name != "a":
-            return field_tiles(parts, name, row)
+            return field_tiles(rows, name, row)
         left, right = tiles_of(advected, row, 2)
         return [
             jnp.where(near_west, lanes_to(0, row, 10, 0), left),
@@ -382,8 +383,9 @@
     def beside(row):
         return [lanes_to(i, row, 3, LANES - 1) for i in (1, 2)], [lanes_to(i, row, 9, 0) for i in (1, 2)]
 
-    for i, row in enumerate((3, ROWS - 4)):
-        for t, tile in enumerate(get("a", row)):
+    for i, row in enumerate(KEPT):
+        third = jnp.where(lane < 64, lanes_to(0, row, 4, 0), lanes_to(0, row, 9, LANES - 1))
+        for t, tile in enumerate(get("a", row) + [third]):
             kept[i, :, t * LANES : (t + 1) * LANES] = tile
 
     def diffuse_block(block, carry):
@@ -398,8 +400,8 @@
 
 def rim_kernel(*refs):
     got_b, got_a = refs[0], refs[1]
-    parts = refs[2:12]
-    strips, inner, kept, out, edges, sems = refs[12:]
+    fields = refs[2:7]
+    strips, inner, kept, out, edges, sems = refs[7:]
     middle = pltpu.make_async_copy
     copies = [middle(inner.at[8:56, i], out.at[i, 8:56], sems.at[i]) for i in range(8)]
     for copy in copies:
@@ -436,23 +438,23 @@
 
     for is_north in (False, True):
         rows = halo(is_north)
-        start = ROWS - 3 if is_north else -1
+        start = ROWS - 2 if is_north else -1
         made, sides = {}, {}
-        for row in range(*((ROWS - 5, ROWS) if is_north else (0, 5))):
+        for row in range(*((ROWS - 4, ROWS) if is_north else (0, 4))):
             base = 16 * (row // 8)
             sides[row] = third_tile({n: strips[i, row % 8] for i, n in enumerate(GROUPS)}, dict.fromkeys(GROUPS, base))
 
         def get(name, row):
             if name == "a":
-                return made[row] if row in made else tiles_of(kept, int(is_north), 2)
+                return made[row] if row in made else tiles_of(kept, KEPT.index(row), 3)
             if row < 0:
                 return rows[-row - 1][name]
             if row >= ROWS:
                 return rows[row - ROWS][name]
-            tiles = field_tiles(parts, name, row)
+            tiles = field_tiles(fields, name, row)
             return tiles if name == "sy" else tiles + [sides[row][name]]
 
-        for j, tiles in enumerate(advect_rows(get, start, 4)):
+        for j, tiles in enumerate(advect_rows(get, start, 3)):
             made[start + j] = tiles
         final = ROWS - 3 if is_north else 0
         base = ROWS - 8 if is_north else 0
@@ -503,37 +505,37 @@
         arrays = [plane(tracers), plane(velocity), plane(slopes), diffusivity, sea_mask]
         arrays = [pltpu.with_memory_space_constraint(x, pltpu.HBM) for x in arrays]
         full, side = (ROWS, 8, 2 * LANES), (8, 8, LANES)
-        *parts, packed, spare = pl.pallas_call(
+        *rows, packed, spare = pl.pallas_call(
             pack_kernel,
-            out_shape=[jax.ShapeDtypeStruct(x.shape[:2] + (LANES,), x.dtype) for x in arrays for _ in range(2)]
-            + [jax.ShapeDtypeStruct((10, 8, LANES), F32), jax.ShapeDtypeStruct(side, F32)],
+            out_shape=[jax.ShapeDtypeStruct(shape, F32) for shape in [full] * 5 + [(10, 8, LANES), side]],
             in_specs=[pl.BlockSpec(memory_space=pltpu.HBM)] * 5,
-            out_specs=[VMEM] * 12,
-            scratch_shapes=[pltpu.SemaphoreType.DMA((10,))],
+            out_specs=[VMEM] * 7,
+            scratch_shapes=[pltpu.VMEM(x.shape[:2] + (LANES,), x.dtype) for x in arrays for _ in range(2)]
+            + [pltpu.SemaphoreType.DMA((10,))],
             compiler_params=pltpu.CompilerParams(vmem_limit_bytes=LIMIT),
         )(*arrays)
         far_got, near_got = move(packed, far), move(packed, near)
         (advected,) = call(
-            advect_kernel, [full], *parts,
+            advect_kernel, [full], *rows,
             cost_estimate=pl.CostEstimate(flops=10**7, bytes_accessed=6 * 10**6, transcendentals=0),
         )
         strips, send_a, send_b = call(
-            edge_kernel, [(4,) + side, (8, 8, 2 * LANES), (8, 8, 2 * LANES)], near_got, far_got, packed, spare, *parts, advected
+            edge_kernel, [(4,) + side, (8, 8, 2 * LANES), (8, 8, 2 * LANES)], near_got, far_got, packed, spare, *rows, advected
         )
         got_b, got_a = move(send_b, pair_b), move(send_a, pair_a)
         inner, kept = call(
-            interior_kernel, [full, (2, 8, 2 * LANES)], *parts, advected, strips,
+            interior_kernel, [full, (4, 8, 3 * LANES)], *rows, advected, strips,
             scratch_shapes=[pltpu.VMEM((3,) + side, F32)],
             cost_estimate=pl.CostEstimate(flops=2 * 10**7, bytes_accessed=10**7, transcendentals=0),
         )
         out = pl.pallas_call(
             rim_kernel,
             out_shape=jax.ShapeDtypeStruct((8, ROWS, 2 * LANES), F32),
-            in_specs=[VMEM] * 15,
+            in_specs=[VMEM] * 10,
             out_specs=pl.BlockSpec(memory_space=pl.ANY),
             scratch_shapes=[pltpu.VMEM((2, 8, 8, 2 * LANES), F32), pltpu.SemaphoreType.DMA((10,))],
             compiler_params=pltpu.CompilerParams(vmem_limit_bytes=LIMIT),
-        )(got_b, got_a, *parts, strips, inner, kept)
+        )(got_b, got_a, *rows, strips, inner, kept)
         return out.reshape(tracers.shape)
 
     return shards

time: 22.1 us -> 22 us (level)
  Pallas kernels: 11.1 us -> 10.2 us
  waiting for transfers between devices: 0.01 us -> 0.5 us
  starting transfers between devices: 10.8 us -> 11.2 us
    pallas_call x3, Pallas kernels: 6.18 us -> 5.17 us  [call(): pl.pallas_call(kernel, out_shape=[jax.ShapeDtypeStruct(s, F32) for s in s...]
    ppermute x4, waiting for transfers between devices: 0.01 us -> 0.5 us  [move(): return lax.ppermute(x, ('lon', 'lat'), route)]
    ppermute x4, starting transfers between devices: 10.8 us -> 11.2 us  [move(): return lax.ppermute(x, ('lon', 'lat'), route)]
  transfers between devices with their start and end apart: 4 -> 4, of which waited for: 0 -> 1; matrix products, arithmetic and copies ran while one was open for 0% -> 0% of each run, Pallas kernels for 26% -> 22%
where the time goes in v5:
time: 22 us; the launch traced here: 21.9 us
  starting transfers between devices  11.2 us (51%)
  Pallas kernels  10.2 us (46%)
  waiting for transfers between devices  0.5 us (2%)
    ppermute x4, starting transfers between devices, move(): return lax.ppermute(x, ('lon', 'lat'), route)  11.2 us
    pallas_call x3, Pallas kernels, call(): pl.pallas_call(kernel, out_shape=[jax.ShapeDtypeStruct(s, F32) for s in s...  5.17 us
    pallas_call x1, Pallas kernels, shards(): pl.pallas_call(pack_kernel, out_shape=[jax.ShapeDtypeStruct(shape, F32) f...  3.56 us
    pallas_call x1, Pallas kernels, shards(): pl.pallas_call(rim_kernel, out_shape=jax.ShapeDtypeStruct((8, ROWS, 2 * L...  1.43 us
    ppermute x4, waiting for transfers between devices, move(): return lax.ppermute(x, ('lon', 'lat'), route)  0.5 us
  transfers between devices with their start and end apart: 4, of which 1 were waited for; matrix products, arithmetic and copies ran while one was open for 0% of the time, Pallas kernels for 22%

profile of v5, /device:TPU:36, one launch (start us, length us, event | category | flops | bytes accessed | tf_op | source)
XLA Modules:
  0.0 21.9 jit_solution(8039241712615831329)
XLA Ops:
  0.0 3.6 %shard_map.55 = (f32[64,8,256]{2,1,0:T(8,128)S(1)}, f32[64,8,256]{2,1,0:T(8,128)S(1)}, f32[64,8,256]{2,1,0:T(8,128)S(1)}, f32[64,8,256]{2,1,0:T(8,128)S(1)}, f32...) custom-call(f32[8,64,256]{2,1,0:T(8,128)} %bitcast.5, f32[12,64,256]{2,1,0:T(8,128)} %bitcast.4, ...), custom_call_target="tpu_custom_call" | custom-call | tf_op jit(solution)/shard_map/pallas_call | solution.py:508
  3.6 4.9 %collective-permute-start.1 = (f32[10,8,128]{2,1,0:T(8,128)S(1)}, f32[10,8,128]{2,1,0:T(8,128)S(1)}, u32[]{:S(2)}, u32[]{:S(2)}) collective-permute-start(f32[10,8,128]{2,1,0:T(8,128)S(1)} %get-tuple-element.17.refs_2_), channel_id=1, source_target_pairs={{0,120},{1,121},{2,122},{3,123},{4,124},{5,125},{6,126},{7,127},{8... | collective-permute-start | bytes 122888 | tf_op jit(solution)/shard_map/ppermute | solution.py:501
  8.5 0.0 collective-permute-start
  8.5 1.7 %shard_map.56.refs_9_.refs_5_ = f32[64,8,256]{2,1,0:T(8,128)S(1)} custom-call(f32[64,8,256]{2,1,0:T(8,128)S(1)} %get-tuple-element.19.refs_0_.refs_4_.refs_2_, f32[64,8,256]{2,1,0:T(8,128)S(1)} %get-tuple-element.20.refs_1_.refs_5_.refs_3_, f32[64,8,256]{2,1,0:T(8,128)S(1)} %get-tuple-element.21.refs_2_.refs_6_.refs_4_, ...), custom_call_target="tpu_custom_call" | custom-call | flops 10000000 | bytes 6000000 | tf_op jit(solution)/shard_map/pallas_call | solution.py:473
  10.2 0.5 %collective-permute-done.1.refs_1_ = f32[10,8,128]{2,1,0:T(8,128)S(1)} collective-permute-done((f32[10,8,128]{2,1,0:T(8,128)S(1)}, f32[10,8,128]{2,1,0:T(8,128)S(1)}, u32[]{:S(2)}, u32[]{:S(2)}) %collective-permute-start.1) | collective-permute-done | bytes 40992 | tf_op jit(solution)/shard_map/ppermute | solution.py:501
  10.7 0.0 collective-permute-done.refs_0_
  10.7 0.4 %shard_map.57 = (f32[4,8,8,128]{3,2,1,0:T(8,128)S(1)}, f32[8,8,256]{2,1,0:T(8,128)S(1)}, f32[8,8,256]{2,1,0:T(8,128)S(1)}) custom-call(f32[10,8,128]{2,1,0:T(8,128)S(1)} %collective-permute-done.refs_0_, f32[10,8,128]{2,1,0:T(8,128)S(1)} %collective-permute-done.1.refs_1_, f32[10,8,128]{2,1,0:T(8,128)S(1)} %get-tuple-element.17.refs_2_, ...), custom_call_target="tpu_custom_call" | custom-call | tf_op jit(solution)/shard_map/pallas_call | solution.py:473
  11.1 0.6 %collective-permute-start.2 = (f32[8,8,256]{2,1,0:T(8,128)S(1)}, f32[8,8,256]{2,1,0:T(8,128)S(1)}, u32[]{:S(2)}, u32[]{:S(2)}) collective-permute-start(f32[8,8,256]{2,1,0:T(8,128)S(1)} %get-tuple-element.24), channel_id=1, source_target_pairs={{0,8},{1,2},{2,1},{3,4},{4,3},{5,6},{6,5},{7,127},{8,0},{9,10},{10... | collective-permute-start | bytes 196616 | tf_op jit(solution)/shard_map/ppermute | solution.py:501
  11.7 5.6 %collective-permute-start.3 = (f32[8,8,256]{2,1,0:T(8,128)S(1)}, f32[8,8,256]{2,1,0:T(8,128)S(1)}, u32[]{:S(2)}, u32[]{:S(2)}) collective-permute-start(f32[8,8,256]{2,1,0:T(8,128)S(1)} %get-tuple-element.25), channel_id=1, source_target_pairs={{0,1},{1,0},{2,3},{3,2},{4,5},{5,4},{6,7},{7,6},{8,9},{9,8},{10,11... | collective-permute-start | bytes 196616 | tf_op jit(solution)/shard_map/ppermute | solution.py:501
  17.4 3.1 %shard_map.58 = (f32[64,8,256]{2,1,0:T(8,128)S(1)}, f32[4,8,384]{2,1,0:T(8,128)S(1)}) custom-call(f32[64,8,256]{2,1,0:T(8,128)S(1)} %get-tuple-element.19.refs_0_.refs_4_.refs_2_, f32[64,8,256]{2,1,0:T(8,128)S(1)} %get-tuple-element.20.refs_1_.refs_5_.refs_3_, f32[64,8,256]{2,1,0:T(8,128)S(1)} %get-tuple-element.21.refs_2_.refs_6_.refs_4_, ...), custom_call_target="tpu_custom_call" | custom-call | flops 20000000 | bytes 10000000 | tf_op jit(solution)/shard_map/pallas_call | solution.py:473
  20.4 0.0 collective-permute-done.2.refs_0_
  20.4 0.0 collective-permute-done.3.refs_1_
  20.4 1.4 %shard_map.59 = f32[8,64,256]{2,1,0:T(8,128)} custom-call(f32[8,8,256]{2,1,0:T(8,128)S(1)} %collective-permute-done.2.refs_0_, f32[8,8,256]{2,1,0:T(8,128)S(1)} %collective-permute-done.3.refs_1_, f32[64,8,256]{2,1,0:T(8,128)S(1)} %get-tuple-element.19.refs_0_.refs_4_.refs_2_, f32[64,8,256]{2,1,0:T(8,128)S(1)} %get-tuple-element.20.refs_1_.refs_5_.refs_3_, ...), custom_call_target="tpu_custom_call" | custom-call | tf_op jit(solution)/shard_map/pallas_call | solution.py:531
Async XLA Ops:
  3.6 7.1 %collective-permute-start.1 = (f32[10,8,128]{2,1,0:T(8,128)S(1)}, f32[10,8,128]{2,1,0:T(8,128)S(1)}, u32[]{:S(2)}, u32[]{:S(2)}) collective-permute-start(f32[10,8,128]{2,1,0:T(8,128)S(1)} %get-tuple-element.17.refs_2_), channel_id=1, source_target_pairs={{0,120},{1,121},{2,122},{3,123},{4,124},{5,125},{6,126},{7,127},{8... | collective-permute-start | bytes 122888 | tf_op jit(solution)/shard_map/ppermute | solution.py:501
  8.5 2.2 %collective-permute-start = (f32[10,8,128]{2,1,0:T(8,128)S(1)}, f32[10,8,128]{2,1,0:T(8,128)S(1)}, u32[]{:S(2)}, u32[]{:S(2)}) collective-permute-start(f32[10,8,128]{2,1,0:T(8,128)S(1)} %get-tuple-element.17.refs_2_), channel_id=1, source_target_pairs={{0,8},{1,9},{2,10},{3,11},{4,12},{5,13},{6,14},{7,15},{8,0},{9,1},... | collective-permute-start | bytes 122888 | tf_op jit(solution)/shard_map/ppermute | solution.py:501
  11.1 9.3 %collective-permute-start.2 = (f32[8,8,256]{2,1,0:T(8,128)S(1)}, f32[8,8,256]{2,1,0:T(8,128)S(1)}, u32[]{:S(2)}, u32[]{:S(2)}) collective-permute-start(f32[8,8,256]{2,1,0:T(8,128)S(1)} %get-tuple-element.24), channel_id=1, source_target_pairs={{0,8},{1,2},{2,1},{3,4},{4,3},{5,6},{6,5},{7,127},{8,0},{9,10},{10... | collective-permute-start | bytes 196616 | tf_op jit(solution)/shard_map/ppermute | solution.py:501
  11.7 8.7 %collective-permute-start.3 = (f32[8,8,256]{2,1,0:T(8,128)S(1)}, f32[8,8,256]{2,1,0:T(8,128)S(1)}, u32[]{:S(2)}, u32[]{:S(2)}) collective-permute-start(f32[8,8,256]{2,1,0:T(8,128)S(1)} %get-tuple-element.25), channel_id=1, source_target_pairs={{0,1},{1,0},{2,3},{3,2},{4,5},{5,4},{6,7},{7,6},{8,9},{9,8},{10,11... | collective-permute-start | bytes 196616 | tf_op jit(solution)/shard_map/ppermute | solution.py:501

commit v6 on v5

--- a/solution.py
+++ b/solution.py
@@ -11,6 +11,7 @@
 F32 = jnp.float32
 VMEM = pl.BlockSpec(memory_space=pltpu.VMEM)
 LIMIT = 16 * 1024 * 1024
+CHUNKS = 2
 GROUPS = ("c", "mu", "vw", "sk")
 KEPT = (2, 3, ROWS - 4, ROWS - 3)
 
@@ -29,14 +30,6 @@
 
 def twice_high(x):
     return jnp.where(low_of(), pltpu.roll(x, 4, 0), x)
-
-
-def eight(ref, start, row):
-    return ref.reshape(ref.shape[0] * ROWS, LANES)[pl.ds(start * ROWS + row, 8, stride=ROWS), :]
-
-
-def four(ref, row):
-    return ref.reshape(ref.shape[0] * ROWS, LANES)[pl.ds(row, 4, stride=ROWS), :].astype(F32)
 
 
 def field_half(rows, name, row, h):
@@ -53,54 +46,60 @@
 
 
 def pack_kernel(*refs):
-    arrays, rows, message, spare, parts, sems = refs[:5], refs[5:10], refs[10], refs[11], refs[12:22], refs[22]
+    arrays, rows, message, spare, held, sems = refs[:5], refs[5:10], refs[10], refs[11], refs[12:17], refs[17]
     copies = []
-    for i, array in enumerate(arrays):
-        for h in range(2):
-            part = pltpu.make_async_copy(
-                array.at[:, :, h * LANES : (h + 1) * LANES], parts[2 * i + h], sems.at[2 * i + h]
-            )
-            part.start()
-            copies.append(part)
-    for part in copies:
-        part.wait()
+    for chunk in range(CHUNKS):
+        span = slice(chunk * ROWS // CHUNKS, (chunk + 1) * ROWS // CHUNKS)
+        copies.append(
+            [
+                pltpu.make_async_copy(array.at[:, span], hold.at[:, span], sems.at[chunk, i])
+                for i, (array, hold) in enumerate(zip(arrays, held))
+            ]
+        )
+        for copy in copies[-1]:
+            copy.start()
     lane, low = lane_of(), low_of()
     scale = jnp.where(low, 1.0, 0.5)
-
-    def group(g):
-        first = second = jnp.zeros((8, LANES), F32)
-        for part in range(8):
-            row = part * 8 + g
+    tracer, velocity, slope, kappa, mask = held
+    first, second = [None] * 8, [None] * 8
+    for part in range(8):
+        if part * CHUNKS % 8 == 0:
+            for copy in copies[part * CHUNKS // 8]:
+                copy.wait()
+        span = slice(8 * part, 8 * part + 8)
+        halves = []
+        for h in range(2):
+            wide = slice(h * LANES, (h + 1) * LANES)
+            planes = [
+                tracer[:, span, wide], velocity[0:8, span, wide], velocity[4:12, span, wide], slope[:, span, wide],
+                jnp.concatenate([mask[:, span, wide].astype(F32), kappa[:, span, wide]], axis=0),
+            ]
+            halves.append([jnp.transpose(x, (1, 0, 2)) for x in planes])
+        base = 16 * part
+        before, half = lane < base, lane < base + 8
+        for g in range(8):
             rims = []
             for h in range(2):
-                tracer, velocity, slope, kappa, mask = parts[h::2]
-                mk = jnp.concatenate([four(mask, row), four(kappa, row)], axis=0) * scale
-                loaded = (
-                    eight(tracer, 0, row), eight(velocity, 0, row), eight(velocity, 4, row),
-                    eight(slope, 0, row) * 0.125, mk,
-                )
+                c, uv, vw, s, mk = [x[g] for x in halves[h]]
+                loaded = (c, uv, vw, s * 0.125, mk * scale)
                 for ref, value in zip(rows, loaded):
-                    ref[row, :, h * LANES : (h + 1) * LANES] = value
+                    ref[8 * part + g, :, h * LANES : (h + 1) * LANES] = value
                 rims.append(loaded)
             c, uv, vw, s, mk = [jnp.where(lane < 64, a, b) for a, b in zip(*rims)]
             mu = jnp.where(low, mk, pltpu.roll(uv, 4, 0))
             sk = jnp.where(low, s, mk)
-            base = 16 * part
-            before, half = lane < base, lane < base + 8
             one = jnp.where(half, pltpu.roll(c, (base + 4) % LANES, 1), pltpu.roll(mu, (base + 12) % LANES, 1))
             two = jnp.where(half, pltpu.roll(vw, (base + 4) % LANES, 1), pltpu.roll(sk, (base + 12) % LANES, 1))
-            first = jnp.where(before, first, one)
-            second = jnp.where(before, second, two)
-        message[g] = first
-        spare[g] = second
-
+            first[g] = jnp.where(before, first[g], one) if part else one
+            second[g] = jnp.where(before, second[g], two) if part else two
     for g in range(8):
-        group(g)
+        message[g] = first[g]
+        spare[g] = second[g]
     slot = lane % 8
     for pair in range(2):
-        total = pltpu.roll(spare[4 * pair], LANES - 2, 1)
+        total = pltpu.roll(second[4 * pair], LANES - 2, 1)
         for i in range(1, 4):
-            moved = spare[4 * pair + i] if i == 1 else pltpu.roll(spare[4 * pair + i], 2 * i - 2, 1)
+            moved = second[4 * pair + i] if i == 1 else pltpu.roll(second[4 * pair + i], 2 * i - 2, 1)
             total = jnp.where((slot == (2 * i + 1) % 8) | (slot == (2 * i + 2) % 8), moved, total)
         message[8 + pair] = total
 
@@ -119,32 +118,28 @@
     lax.fori_loop(0, 4, advect_block, 0)
 
 
+def strip_at(g, which, late, from_near, from_far, own, spare):
+    slot = lane_of() % 16
+    far_is_west = jnp.broadcast_to(lax.axis_index("lon") % 2, (8, LANES)) == 0
+    if which == 0:
+        far, near, mine = from_far[g], from_near[g], own[g]
+    else:
+        back = (2 - 2 * (g % 4)) % LANES
+        turn = lambda x: pltpu.roll(x, back, 1) if back else x
+        far, near, mine = turn(from_far[8 + g // 4]), turn(from_near[8 + g // 4]), spare[g]
+    east, west = jnp.where(far_is_west, near, far), jnp.where(far_is_west, far, near)
+    shift = lambda x, by: pltpu.roll(x, (by - 8 * late) % LANES, 1) if by != 8 * late else x
+    inner = jnp.where(slot < 4, shift(mine, 0), shift(east, 0))
+    outer = jnp.where(slot < 10, shift(west, 6), shift(mine, 6))
+    return jnp.where(slot < 7, inner, outer)
+
+
 def edge_kernel(*refs):
-    from_near, from_far, own, spare = refs[:4]
-    rows = refs[4:9]
-    strips, send_a, send_b = refs[10:]
+    sources, rows = refs[:4], refs[4:9]
+    send_a, send_b = refs[10:]
     lane, low = lane_of(), low_of()
-    lon, lat = lax.axis_index("lon"), lax.axis_index("lat")
-    slot = lane % 16
-    far_is_west = jnp.broadcast_to(lon % 2, (8, LANES)) == 0
-
-    def strip(mine, east, west, late):
-        shift = lambda x, by: pltpu.roll(x, (by - 8 * late) % LANES, 1) if by != 8 * late else x
-        inner = jnp.where(slot < 4, shift(mine, 0), shift(east, 0))
-        outer = jnp.where(slot < 10, shift(west, 6), shift(mine, 6))
-        return jnp.where(slot < 7, inner, outer)
-
-    for g in range(8):
-        for which in range(2):
-            if which == 0:
-                far, near, mine = from_far[g], from_near[g], own[g]
-            else:
-                back = (2 - 2 * (g % 4)) % LANES
-                turn = lambda x: pltpu.roll(x, back, 1) if back else x
-                far, near, mine = turn(from_far[8 + g // 4]), turn(from_near[8 + g // 4]), spare[g]
-            east, west = jnp.where(far_is_west, near, far), jnp.where(far_is_west, far, near)
-            for late in range(2):
-                strips[2 * which + late, g] = strip(mine, east, west, late)
+    lat = lax.axis_index("lat")
+    strips = {(i, g): strip_at(g, i // 2, i % 2, *sources) for i in range(3) for g in (0, 1, 6, 7)}
 
     def message(top):
         row = lambda q: jnp.where(top, ROWS - 1 - q, q)
@@ -153,7 +148,7 @@
         tiles = [[part("c", q, h) for h in range(2)] for q in range(3)]
         tiles += [pair("m", 0, "v", 0), pair("m", 1, "v", 1), pair("m", 2, "u", 0), pair("w", 0, "sy", 0)]
         corners = [
-            pltpu.roll(strips[i, jnp.where(top, 7 - q, q)], jnp.where(top, 16, 0), 1) for q in range(2) for i in range(3)
+            jnp.where(top, pltpu.roll(strips[i, 7 - q], 16, 1), strips[i, q]) for q in range(2) for i in range(3)
         ]
         return tiles, [part("k", 0, h) for h in range(2)], corners
 
@@ -350,12 +345,17 @@
 
 
 def interior_kernel(*refs):
-    rows, advected, strips = refs[:5], refs[5], refs[6]
-    out, kept, narrow = refs[7:]
+    rows, advected, sources = refs[:5], refs[5], refs[6:10]
+    out, kept, strips, narrow = refs[10:]
     lane = lane_of()
     near_east, near_west = lane >= LANES - 2, lane < 2
 
-    full = [split_groups({n: strips[i, g] for i, n in enumerate(GROUPS)}) for g in range(8)]
+    full = []
+    for g in range(8):
+        groups = {n: strip_at(g, i // 2, i % 2, *sources) for i, n in enumerate(GROUPS)}
+        full.append(split_groups(groups))
+        for i, n in enumerate(GROUPS):
+            strips[i, g] = groups[n]
 
     def get_strip(name, g):
         x = full[g % 8][name]
@@ -399,7 +399,7 @@
 
 
 def rim_kernel(*refs):
-    got_b, got_a = refs[0], refs[1]
+    got_a, got_b = refs[0], refs[1]
     fields = refs[2:7]
     strips, inner, kept, out, edges, sems = refs[7:]
     middle = pltpu.make_async_copy
@@ -510,8 +510,7 @@
             out_shape=[jax.ShapeDtypeStruct(shape, F32) for shape in [full] * 5 + [(10, 8, LANES), side]],
             in_specs=[pl.BlockSpec(memory_space=pltpu.HBM)] * 5,
             out_specs=[VMEM] * 7,
-            scratch_shapes=[pltpu.VMEM(x.shape[:2] + (LANES,), x.dtype) for x in arrays for _ in range(2)]
-            + [pltpu.SemaphoreType.DMA((10,))],
+            scratch_shapes=[pltpu.VMEM(x.shape, x.dtype) for x in arrays] + [pltpu.SemaphoreType.DMA((CHUNKS, 5))],
             compiler_params=pltpu.CompilerParams(vmem_limit_bytes=LIMIT),
         )(*arrays)
         far_got, near_got = move(packed, far), move(packed, near)
@@ -519,12 +518,12 @@
             advect_kernel, [full], *rows,
             cost_estimate=pl.CostEstimate(flops=10**7, bytes_accessed=6 * 10**6, transcendentals=0),
         )
-        strips, send_a, send_b = call(
-            edge_kernel, [(4,) + side, (8, 8, 2 * LANES), (8, 8, 2 * LANES)], near_got, far_got, packed, spare, *rows, advected
+        send_a, send_b = call(
+            edge_kernel, [(8, 8, 2 * LANES)] * 2, near_got, far_got, packed, spare, *rows, advected
         )
-        got_b, got_a = move(send_b, pair_b), move(send_a, pair_a)
-        inner, kept = call(
-            interior_kernel, [full, (4, 8, 3 * LANES)], *rows, advected, strips,
+        got_a, got_b = move(send_a, pair_a), move(send_b, pair_b)
+        inner, kept, strips = call(
+            interior_kernel, [full, (4, 8, 3 * LANES), (4,) + side], *rows, advected, near_got, far_got, packed, spare,
             scratch_shapes=[pltpu.VMEM((3,) + side, F32)],
             cost_estimate=pl.CostEstimate(flops=2 * 10**7, bytes_accessed=10**7, transcendentals=0),
         )
@@ -535,7 +534,7 @@
             out_specs=pl.BlockSpec(memory_space=pl.ANY),
             scratch_shapes=[pltpu.VMEM((2, 8, 8, 2 * LANES), F32), pltpu.SemaphoreType.DMA((10,))],
             compiler_params=pltpu.CompilerParams(vmem_limit_bytes=LIMIT),
-        )(got_b, got_a, *rows, strips, inner, kept)
+        )(got_a, got_b, *rows, strips, inner, kept)
         return out.reshape(tracers.shape)
 
     return shards

time: 22 us -> 20.1 us (0.914)
  the two profiles are of different devices: /device:TPU:36 before, /device:TPU:39 now
where the time goes in v6:
time: 20.1 us; the launch traced here: 20 us
  starting transfers between devices  9.79 us (49%)
  Pallas kernels  8.81 us (44%)
  waiting for transfers between devices  1.33 us (7%)
    ppermute x4, starting transfers between devices, move(): return lax.ppermute(x, ('lon', 'lat'), route)  9.79 us
    pallas_call x3, Pallas kernels, call(): pl.pallas_call(kernel, out_shape=[jax.ShapeDtypeStruct(s, F32) for s in s...  5.34 us
    pallas_call x1, Pallas kernels, shards(): pl.pallas_call(pack_kernel, out_shape=[jax.ShapeDtypeStruct(shape, F32) f...  2.08 us
    pallas_call x1, Pallas kernels, shards(): pl.pallas_call(rim_kernel, out_shape=jax.ShapeDtypeStruct((8, ROWS, 2 * L...  1.4 us
    ppermute x4, waiting for transfers between devices, move(): return lax.ppermute(x, ('lon', 'lat'), route)  1.33 us
  transfers between devices with their start and end apart: 4, of which 1 were waited for; matrix products, arithmetic and copies ran while one was open for 0% of the time, Pallas kernels for 25%

profile of v6, /device:TPU:39, one launch (start us, length us, event | category | flops | bytes accessed | tf_op | source)
XLA Modules:
  0.0 20.0 jit_solution(2332543874073473888)
XLA Ops:
  0.0 2.1 %shard_map.55 = (f32[64,8,256]{2,1,0:T(8,128)S(1)}, f32[64,8,256]{2,1,0:T(8,128)S(1)}, f32[64,8,256]{2,1,0:T(8,128)S(1)}, f32[64,8,256]{2,1,0:T(8,128)S(1)}, f32...) custom-call(f32[8,64,256]{2,1,0:T(8,128)} %bitcast.5, f32[12,64,256]{2,1,0:T(8,128)} %bitcast.4, ...), custom_call_target="tpu_custom_call" | custom-call | tf_op jit(solution)/shard_map/pallas_call | solution.py:508
  2.1 3.3 %collective-permute-start.1 = (f32[10,8,128]{2,1,0:T(8,128)S(1)}, f32[10,8,128]{2,1,0:T(8,128)S(1)}, u32[]{:S(2)}, u32[]{:S(2)}) collective-permute-start(f32[10,8,128]{2,1,0:T(8,128)S(1)} %get-tuple-element.17.refs_2_.refs_8_), channel_id=1, source_target_pairs={{0,120},{1,121},{2,122},{3,123},{4,124},{5,125},{6,126},{7,127},{8... | collective-permute-start | bytes 122888 | tf_op jit(solution)/shard_map/ppermute | solution.py:501
  5.4 2.3 %collective-permute-start = (f32[10,8,128]{2,1,0:T(8,128)S(1)}, f32[10,8,128]{2,1,0:T(8,128)S(1)}, u32[]{:S(2)}, u32[]{:S(2)}) collective-permute-start(f32[10,8,128]{2,1,0:T(8,128)S(1)} %get-tuple-element.17.refs_2_.refs_8_), channel_id=1, source_target_pairs={{0,8},{1,9},{2,10},{3,11},{4,12},{5,13},{6,14},{7,15},{8,0},{9,1},... | collective-permute-start | bytes 122888 | tf_op jit(solution)/shard_map/ppermute | solution.py:501
  7.7 1.7 %shard_map.56.refs_9_.refs_5_ = f32[64,8,256]{2,1,0:T(8,128)S(1)} custom-call(f32[64,8,256]{2,1,0:T(8,128)S(1)} %get-tuple-element.19.refs_0_.refs_4_.refs_2_, f32[64,8,256]{2,1,0:T(8,128)S(1)} %get-tuple-element.20.refs_1_.refs_5_.refs_3_, f32[64,8,256]{2,1,0:T(8,128)S(1)} %get-tuple-element.21.refs_2_.refs_6_.refs_4_, ...), custom_call_target="tpu_custom_call" | custom-call | flops 10000000 | bytes 6000000 | tf_op jit(solution)/shard_map/pallas_call | solution.py:473
  9.4 0.0 collective-permute-done.1.refs_1_.refs_7_
  9.4 0.0 collective-permute-done.refs_0_.refs_6_
  9.4 0.4 %shard_map.57 = (f32[8,8,256]{2,1,0:T(8,128)S(1)}, f32[8,8,256]{2,1,0:T(8,128)S(1)}) custom-call(f32[10,8,128]{2,1,0:T(8,128)S(1)} %collective-permute-done.refs_0_.refs_6_, f32[10,8,128]{2,1,0:T(8,128)S(1)} %collective-permute-done.1.refs_1_.refs_7_, f32[10,8,128]{2,1,0:T(8,128)S(1)} %get-tuple-element.17.refs_2_.refs_8_, ...), custom_call_target="tpu_custom_call" | custom-call | tf_op jit(solution)/shard_map/pallas_call | solution.py:473
  9.8 0.5 %collective-permute-start.2 = (f32[8,8,256]{2,1,0:T(8,128)S(1)}, f32[8,8,256]{2,1,0:T(8,128)S(1)}, u32[]{:S(2)}, u32[]{:S(2)}) collective-permute-start(f32[8,8,256]{2,1,0:T(8,128)S(1)} %get-tuple-element.24), channel_id=1, source_target_pairs={{0,1},{1,0},{2,3},{3,2},{4,5},{5,4},{6,7},{7,6},{8,9},{9,8},{10,11... | collective-permute-start | bytes 196616 | tf_op jit(solution)/shard_map/ppermute | solution.py:501
  10.3 3.7 %collective-permute-start.3 = (f32[8,8,256]{2,1,0:T(8,128)S(1)}, f32[8,8,256]{2,1,0:T(8,128)S(1)}, u32[]{:S(2)}, u32[]{:S(2)}) collective-permute-start(f32[8,8,256]{2,1,0:T(8,128)S(1)} %get-tuple-element.25), channel_id=1, source_target_pairs={{0,8},{1,2},{2,1},{3,4},{4,3},{5,6},{6,5},{7,127},{8,0},{9,10},{10... | collective-permute-start | bytes 196616 | tf_op jit(solution)/shard_map/ppermute | solution.py:501
  14.0 3.2 %shard_map.58 = (f32[64,8,256]{2,1,0:T(8,128)S(1)}, f32[4,8,384]{2,1,0:T(8,128)S(1)}, f32[4,8,8,128]{3,2,1,0:T(8,128)S(1)}) custom-call(f32[64,8,256]{2,1,0:T(8,128)S(1)} %get-tuple-element.19.refs_0_.refs_4_.refs_2_, f32[64,8,256]{2,1,0:T(8,128)S(1)} %get-tuple-element.20.refs_1_.refs_5_.refs_3_, ...), custom_call_target="tpu_custom_call" | custom-call | flops 20000000 | bytes 10000000 | tf_op jit(solution)/shard_map/pallas_call | solution.py:473
  17.3 0.0 collective-permute-done.2.refs_0_
  17.3 1.3 %collective-permute-done.3.refs_1_ = f32[8,8,256]{2,1,0:T(8,128)S(1)} collective-permute-done((f32[8,8,256]{2,1,0:T(8,128)S(1)}, f32[8,8,256]{2,1,0:T(8,128)S(1)}, u32[]{:S(2)}, u32[]{:S(2)}) %collective-permute-start.3) | collective-permute-done | bytes 65568 | tf_op jit(solution)/shard_map/ppermute | solution.py:501
  18.6 1.4 %shard_map.59 = f32[8,64,256]{2,1,0:T(8,128)} custom-call(f32[8,8,256]{2,1,0:T(8,128)S(1)} %collective-permute-done.2.refs_0_, f32[8,8,256]{2,1,0:T(8,128)S(1)} %collective-permute-done.3.refs_1_, f32[64,8,256]{2,1,0:T(8,128)S(1)} %get-tuple-element.19.refs_0_.refs_4_.refs_2_, f32[64,8,256]{2,1,0:T(8,128)S(1)} %get-tuple-element.20.refs_1_.refs_5_.refs_3_, ...), custom_call_target="tpu_custom_call" | custom-call | tf_op jit(solution)/shard_map/pallas_call | solution.py:530
Async XLA Ops:
  2.1 7.3 %collective-permute-start.1 = (f32[10,8,128]{2,1,0:T(8,128)S(1)}, f32[10,8,128]{2,1,0:T(8,128)S(1)}, u32[]{:S(2)}, u32[]{:S(2)}) collective-permute-start(f32[10,8,128]{2,1,0:T(8,128)S(1)} %get-tuple-element.17.refs_2_.refs_8_), channel_id=1, source_target_pairs={{0,120},{1,121},{2,122},{3,123},{4,124},{5,125},{6,126},{7,127},{8... | collective-permute-start | bytes 122888 | tf_op jit(solution)/shard_map/ppermute | solution.py:501
  5.4 4.0 %collective-permute-start = (f32[10,8,128]{2,1,0:T(8,128)S(1)}, f32[10,8,128]{2,1,0:T(8,128)S(1)}, u32[]{:S(2)}, u32[]{:S(2)}) collective-permute-start(f32[10,8,128]{2,1,0:T(8,128)S(1)} %get-tuple-element.17.refs_2_.refs_8_), channel_id=1, source_target_pairs={{0,8},{1,9},{2,10},{3,11},{4,12},{5,13},{6,14},{7,15},{8,0},{9,1},... | collective-permute-start | bytes 122888 | tf_op jit(solution)/shard_map/ppermute | solution.py:501
  9.8 7.4 %collective-permute-start.2 = (f32[8,8,256]{2,1,0:T(8,128)S(1)}, f32[8,8,256]{2,1,0:T(8,128)S(1)}, u32[]{:S(2)}, u32[]{:S(2)}) collective-permute-start(f32[8,8,256]{2,1,0:T(8,128)S(1)} %get-tuple-element.24), channel_id=1, source_target_pairs={{0,1},{1,0},{2,3},{3,2},{4,5},{5,4},{6,7},{7,6},{8,9},{9,8},{10,11... | collective-permute-start | bytes 196616 | tf_op jit(solution)/shard_map/ppermute | solution.py:501
  10.3 8.2 %collective-permute-start.3 = (f32[8,8,256]{2,1,0:T(8,128)S(1)}, f32[8,8,256]{2,1,0:T(8,128)S(1)}, u32[]{:S(2)}, u32[]{:S(2)}) collective-permute-start(f32[8,8,256]{2,1,0:T(8,128)S(1)} %get-tuple-element.25), channel_id=1, source_target_pairs={{0,8},{1,2},{2,1},{3,4},{4,3},{5,6},{6,5},{7,127},{8,0},{9,10},{10... | collective-permute-start | bytes 196616 | tf_op jit(solution)/shard_map/ppermute | solution.py:501

commit v7 on v6

--- a/solution.py
+++ b/solution.py
@@ -46,7 +46,7 @@
 
 
 def pack_kernel(*refs):
-    arrays, rows, message, spare, held, sems = refs[:5], refs[5:10], refs[10], refs[11], refs[12:17], refs[17]
+    arrays, rows, (to_near, to_far, own, spare), held, sems = refs[:5], refs[5:10], refs[10:14], refs[14:19], refs[19]
     copies = []
     for chunk in range(CHUNKS):
         span = slice(chunk * ROWS // CHUNKS, (chunk + 1) * ROWS // CHUNKS)
@@ -93,15 +93,19 @@
             first[g] = jnp.where(before, first[g], one) if part else one
             second[g] = jnp.where(before, second[g], two) if part else two
     for g in range(8):
-        message[g] = first[g]
+        own[g] = first[g]
         spare[g] = second[g]
     slot = lane % 8
-    for pair in range(2):
-        total = pltpu.roll(second[4 * pair], LANES - 2, 1)
-        for i in range(1, 4):
-            moved = second[4 * pair + i] if i == 1 else pltpu.roll(second[4 * pair + i], 2 * i - 2, 1)
-            total = jnp.where((slot == (2 * i + 1) % 8) | (slot == (2 * i + 2) % 8), moved, total)
-        message[8 + pair] = total
+    to_east = jnp.broadcast_to(lax.axis_index("lon") % 2, (8, LANES)) == 0
+    for pair in range(4):
+        east, west = [], []
+        for g in (2 * pair, 2 * pair + 1):
+            east.append(jnp.where(slot == 0, pltpu.roll(second[g], LANES - 3, 1), first[g]))
+            west.append(jnp.where(slot == 7, pltpu.roll(second[g], 3, 1), first[g]))
+        eastern = jnp.where(slot < 4, east[0], pltpu.roll(east[1], 4, 1))
+        western = jnp.where(slot < 4, pltpu.roll(west[0], LANES - 4, 1), west[1])
+        to_near[pair] = jnp.where(to_east, eastern, western)
+        to_far[pair] = jnp.where(to_east, western, eastern)
 
 
 def advect_kernel(*refs):
@@ -118,19 +122,17 @@
     lax.fori_loop(0, 4, advect_block, 0)
 
 
-def strip_at(g, which, late, from_near, from_far, own, spare):
+def strip_at(g, which, late, from_far, from_near, own, spare):
     slot = lane_of() % 16
     far_is_west = jnp.broadcast_to(lax.axis_index("lon") % 2, (8, LANES)) == 0
-    if which == 0:
-        far, near, mine = from_far[g], from_near[g], own[g]
-    else:
-        back = (2 - 2 * (g % 4)) % LANES
-        turn = lambda x: pltpu.roll(x, back, 1) if back else x
-        far, near, mine = turn(from_far[8 + g // 4]), turn(from_near[8 + g // 4]), spare[g]
+    near, far, mine = from_near[g // 2], from_far[g // 2], (spare if which else own)[g]
     east, west = jnp.where(far_is_west, near, far), jnp.where(far_is_west, far, near)
-    shift = lambda x, by: pltpu.roll(x, (by - 8 * late) % LANES, 1) if by != 8 * late else x
-    inner = jnp.where(slot < 4, shift(mine, 0), shift(east, 0))
-    outer = jnp.where(slot < 10, shift(west, 6), shift(mine, 6))
+    shift = lambda x, by: pltpu.roll(x, by % LANES, 1) if by else x
+    odd = 4 * (g % 2)
+    east = shift(east, (1 if which else 4) - odd - 8 * late)
+    west = shift(west, (9 if which else 6) - odd - 8 * late)
+    inner = jnp.where(slot < 4, shift(mine, -8 * late), east)
+    outer = jnp.where(slot < 10, west, shift(mine, 6 - 8 * late))
     return jnp.where(slot < 7, inner, outer)
 
 
@@ -399,7 +401,7 @@
 
 
 def rim_kernel(*refs):
-    got_a, got_b = refs[0], refs[1]
+    got_b, got_a = refs[0], refs[1]
     fields = refs[2:7]
     strips, inner, kept, out, edges, sems = refs[7:]
     middle = pltpu.make_async_copy
@@ -505,25 +507,25 @@
         arrays = [plane(tracers), plane(velocity), plane(slopes), diffusivity, sea_mask]
         arrays = [pltpu.with_memory_space_constraint(x, pltpu.HBM) for x in arrays]
         full, side = (ROWS, 8, 2 * LANES), (8, 8, LANES)
-        *rows, packed, spare = pl.pallas_call(
+        *rows, to_near, to_far, own, spare = pl.pallas_call(
             pack_kernel,
-            out_shape=[jax.ShapeDtypeStruct(shape, F32) for shape in [full] * 5 + [(10, 8, LANES), side]],
+            out_shape=[jax.ShapeDtypeStruct(shape, F32) for shape in [full] * 5 + [(4, 8, LANES)] * 2 + [side] * 2],
             in_specs=[pl.BlockSpec(memory_space=pltpu.HBM)] * 5,
-            out_specs=[VMEM] * 7,
+            out_specs=[VMEM] * 9,
             scratch_shapes=[pltpu.VMEM(x.shape, x.dtype) for x in arrays] + [pltpu.SemaphoreType.DMA((CHUNKS, 5))],
             compiler_params=pltpu.CompilerParams(vmem_limit_bytes=LIMIT),
         )(*arrays)
-        far_got, near_got = move(packed, far), move(packed, near)
+        far_got, near_got = move(to_far, far), move(to_near, near)
         (advected,) = call(
             advect_kernel, [full], *rows,
             cost_estimate=pl.CostEstimate(flops=10**7, bytes_accessed=6 * 10**6, transcendentals=0),
         )
         send_a, send_b = call(
-            edge_kernel, [(8, 8, 2 * LANES)] * 2, near_got, far_got, packed, spare, *rows, advected
+            edge_kernel, [(8, 8, 2 * LANES)] * 2, far_got, near_got, own, spare, *rows, advected
         )
         got_a, got_b = move(send_a, pair_a), move(send_b, pair_b)
         inner, kept, strips = call(
-            interior_kernel, [full, (4, 8, 3 * LANES), (4,) + side], *rows, advected, near_got, far_got, packed, spare,
+            interior_kernel, [full, (4, 8, 3 * LANES), (4,) + side], *rows, advected, far_got, near_got, own, spare,
             scratch_shapes=[pltpu.VMEM((3,) + side, F32)],
             cost_estimate=pl.CostEstimate(flops=2 * 10**7, bytes_accessed=10**7, transcendentals=0),
         )
@@ -534,7 +536,7 @@
             out_specs=pl.BlockSpec(memory_space=pl.ANY),
             scratch_shapes=[pltpu.VMEM((2, 8, 8, 2 * LANES), F32), pltpu.SemaphoreType.DMA((10,))],
             compiler_params=pltpu.CompilerParams(vmem_limit_bytes=LIMIT),
-        )(got_a, got_b, *rows, strips, inner, kept)
+        )(got_b, got_a, *rows, strips, inner, kept)
         return out.reshape(tracers.shape)
 
     return shards

time: 20.1 us -> 20.3 us (level)
  the two profiles are of different devices: /device:TPU:39 before, /device:TPU:36 now
where the time goes in v7:
time: 20.3 us; the launch traced here: 20.2 us
  starting transfers between devices  11.2 us (55%)
  Pallas kernels  8.66 us (43%)
  waiting for transfers between devices  0.24 us (1%)
    ppermute x4, starting transfers between devices, move(): return lax.ppermute(x, ('lon', 'lat'), route)  11.2 us
    pallas_call x3, Pallas kernels, call(): pl.pallas_call(kernel, out_shape=[jax.ShapeDtypeStruct(s, F32) for s in s...  5.1 us
    pallas_call x1, Pallas kernels, shards(): pl.pallas_call(pack_kernel, out_shape=[jax.ShapeDtypeStruct(shape, F32) f...  2.13 us
    pallas_call x1, Pallas kernels, shards(): pl.pallas_call(rim_kernel, out_shape=jax.ShapeDtypeStruct((8, ROWS, 2 * L...  1.43 us
  transfers between devices with their start and end apart: 4, of which 1 were waited for; matrix products, arithmetic and copies ran while one was open for 0% of the time, Pallas kernels for 24%

profile of v7, /device:TPU:36, one launch (start us, length us, event | category | flops | bytes accessed | tf_op | source)
XLA Modules:
  0.0 20.2 jit_solution(12033393242252662949)
XLA Ops:
  0.0 2.1 %shard_map.55 = (f32[64,8,256]{2,1,0:T(8,128)S(1)}, f32[64,8,256]{2,1,0:T(8,128)S(1)}, f32[64,8,256]{2,1,0:T(8,128)S(1)}, f32[64,8,256]{2,1,0:T(8,128)S(1)}, f32...) custom-call(f32[8,64,256]{2,1,0:T(8,128)} %bitcast.5, ...), custom_call_target="tpu_custom_call" | custom-call | tf_op jit(solution)/shard_map/pallas_call | solution.py:510
  2.1 4.9 %collective-permute-start = (f32[4,8,128]{2,1,0:T(8,128)S(1)}, f32[4,8,128]{2,1,0:T(8,128)S(1)}, u32[]{:S(2)}, u32[]{:S(2)}) collective-permute-start(f32[4,8,128]{2,1,0:T(8,128)S(1)} %get-tuple-element.19), channel_id=1, source_target_pairs={{0,120},{1,121},{2,122},{3,123},{4,124},{5,125},{6,126},{7,127},{8... | collective-permute-start | bytes 49160 | tf_op jit(solution)/shard_map/ppermute | solution.py:503
  7.1 0.0 collective-permute-start.1
  7.1 1.7 %shard_map.56.refs_9_.refs_5_ = f32[64,8,256]{2,1,0:T(8,128)S(1)} custom-call(f32[64,8,256]{2,1,0:T(8,128)S(1)} %get-tuple-element.23.refs_0_.refs_4_.refs_2_, f32[64,8,256]{2,1,0:T(8,128)S(1)} %get-tuple-element.24.refs_1_.refs_5_.refs_3_, f32[64,8,256]{2,1,0:T(8,128)S(1)} %get-tuple-element.25.refs_2_.refs_6_.refs_4_, ...), custom_call_target="tpu_custom_call" | custom-call | flops 10000000 | bytes 6000000 | tf_op jit(solution)/shard_map/pallas_call | solution.py:475
  8.8 0.2 %collective-permute-done.refs_0_.refs_6_ = f32[4,8,128]{2,1,0:T(8,128)S(1)} collective-permute-done((f32[4,8,128]{2,1,0:T(8,128)S(1)}, f32[4,8,128]{2,1,0:T(8,128)S(1)}, u32[]{:S(2)}, u32[]{:S(2)}) %collective-permute-start) | collective-permute-done | bytes 16416 | tf_op jit(solution)/shard_map/ppermute | solution.py:503
  9.0 0.0 collective-permute-done.1.refs_1_.refs_7_
  9.0 0.2 %shard_map.57 = (f32[8,8,256]{2,1,0:T(8,128)S(1)}, f32[8,8,256]{2,1,0:T(8,128)S(1)}) custom-call(f32[4,8,128]{2,1,0:T(8,128)S(1)} %collective-permute-done.refs_0_.refs_6_, f32[4,8,128]{2,1,0:T(8,128)S(1)} %collective-permute-done.1.refs_1_.refs_7_, f32[8,8,128]{2,1,0:T(8,128)S(1)} %get-tuple-element.21.refs_2_.refs_8_, ...), custom_call_target="tpu_custom_call" | custom-call | tf_op jit(solution)/shard_map/pallas_call | solution.py:475
  9.2 0.6 %collective-permute-start.2 = (f32[8,8,256]{2,1,0:T(8,128)S(1)}, f32[8,8,256]{2,1,0:T(8,128)S(1)}, u32[]{:S(2)}, u32[]{:S(2)}) collective-permute-start(f32[8,8,256]{2,1,0:T(8,128)S(1)} %get-tuple-element.28), channel_id=1, source_target_pairs={{0,8},{1,2},{2,1},{3,4},{4,3},{5,6},{6,5},{7,127},{8,0},{9,10},{10... | collective-permute-start | bytes 196616 | tf_op jit(solution)/shard_map/ppermute | solution.py:503
  9.9 5.6 %collective-permute-start.3 = (f32[8,8,256]{2,1,0:T(8,128)S(1)}, f32[8,8,256]{2,1,0:T(8,128)S(1)}, u32[]{:S(2)}, u32[]{:S(2)}) collective-permute-start(f32[8,8,256]{2,1,0:T(8,128)S(1)} %get-tuple-element.29), channel_id=1, source_target_pairs={{0,1},{1,0},{2,3},{3,2},{4,5},{5,4},{6,7},{7,6},{8,9},{9,8},{10,11... | collective-permute-start | bytes 196616 | tf_op jit(solution)/shard_map/ppermute | solution.py:503
  15.5 3.2 %shard_map.58 = (f32[64,8,256]{2,1,0:T(8,128)S(1)}, f32[4,8,384]{2,1,0:T(8,128)S(1)}, f32[4,8,8,128]{3,2,1,0:T(8,128)S(1)}) custom-call(f32[64,8,256]{2,1,0:T(8,128)S(1)} %get-tuple-element.23.refs_0_.refs_4_.refs_2_, f32[64,8,256]{2,1,0:T(8,128)S(1)} %get-tuple-element.24.refs_1_.refs_5_.refs_3_, ...), custom_call_target="tpu_custom_call" | custom-call | flops 20000000 | bytes 10000000 | tf_op jit(solution)/shard_map/pallas_call | solution.py:475
  18.7 0.0 collective-permute-done.2.refs_0_
  18.7 0.0 collective-permute-done.3.refs_1_
  18.7 1.4 %shard_map.59 = f32[8,64,256]{2,1,0:T(8,128)} custom-call(f32[8,8,256]{2,1,0:T(8,128)S(1)} %collective-permute-done.2.refs_0_, f32[8,8,256]{2,1,0:T(8,128)S(1)} %collective-permute-done.3.refs_1_, f32[64,8,256]{2,1,0:T(8,128)S(1)} %get-tuple-element.23.refs_0_.refs_4_.refs_2_, f32[64,8,256]{2,1,0:T(8,128)S(1)} %get-tuple-element.24.refs_1_.refs_5_.refs_3_, ...), custom_call_target="tpu_custom_call" | custom-call | tf_op jit(solution)/shard_map/pallas_call | solution.py:532
Async XLA Ops:
  2.1 6.9 %collective-permute-start = (f32[4,8,128]{2,1,0:T(8,128)S(1)}, f32[4,8,128]{2,1,0:T(8,128)S(1)}, u32[]{:S(2)}, u32[]{:S(2)}) collective-permute-start(f32[4,8,128]{2,1,0:T(8,128)S(1)} %get-tuple-element.19), channel_id=1, source_target_pairs={{0,120},{1,121},{2,122},{3,123},{4,124},{5,125},{6,126},{7,127},{8... | collective-permute-start | bytes 49160 | tf_op jit(solution)/shard_map/ppermute | solution.py:503
  7.1 1.9 %collective-permute-start.1 = (f32[4,8,128]{2,1,0:T(8,128)S(1)}, f32[4,8,128]{2,1,0:T(8,128)S(1)}, u32[]{:S(2)}, u32[]{:S(2)}) collective-permute-start(f32[4,8,128]{2,1,0:T(8,128)S(1)} %get-tuple-element.20), channel_id=1, source_target_pairs={{0,8},{1,9},{2,10},{3,11},{4,12},{5,13},{6,14},{7,15},{8,0},{9,1},... | collective-permute-start | bytes 49160 | tf_op jit(solution)/shard_map/ppermute | solution.py:503
  9.2 9.5 %collective-permute-start.2 = (f32[8,8,256]{2,1,0:T(8,128)S(1)}, f32[8,8,256]{2,1,0:T(8,128)S(1)}, u32[]{:S(2)}, u32[]{:S(2)}) collective-permute-start(f32[8,8,256]{2,1,0:T(8,128)S(1)} %get-tuple-element.28), channel_id=1, source_target_pairs={{0,8},{1,2},{2,1},{3,4},{4,3},{5,6},{6,5},{7,127},{8,0},{9,10},{10... | collective-permute-start | bytes 196616 | tf_op jit(solution)/shard_map/ppermute | solution.py:503
  9.9 8.8 %collective-permute-start.3 = (f32[8,8,256]{2,1,0:T(8,128)S(1)}, f32[8,8,256]{2,1,0:T(8,128)S(1)}, u32[]{:S(2)}, u32[]{:S(2)}) collective-permute-start(f32[8,8,256]{2,1,0:T(8,128)S(1)} %get-tuple-element.29), channel_id=1, source_target_pairs={{0,1},{1,0},{2,3},{3,2},{4,5},{5,4},{6,7},{7,6},{8,9},{9,8},{10,11... | collective-permute-start | bytes 196616 | tf_op jit(solution)/shard_map/ppermute | solution.py:503

commit v8 on v7

--- a/solution.py
+++ b/solution.py
@@ -45,8 +45,22 @@
     return [field_half(rows, name, row, h) for h in range(2)]
 
 
+def row_planes(held, span, h):
+    tracer, velocity, slope, kappa, mask = held
+    wide = slice(h * LANES, (h + 1) * LANES)
+    return [
+        tracer[:, span, wide], velocity[0:8, span, wide], velocity[4:12, span, wide], slope[:, span, wide],
+        jnp.concatenate([mask[:, span, wide].astype(F32), kappa[:, span, wide]], axis=0),
+    ]
+
+
+def scaled(groups):
+    c, uv, vw, s, mk = groups
+    return c, uv, vw, s * 0.125, mk * jnp.where(low_of(), 1.0, 0.5)
+
+
 def pack_kernel(*refs):
-    arrays, rows, (to_near, to_far, own, spare), held, sems = refs[:5], refs[5:10], refs[10:14], refs[14:19], refs[19]
+    arrays, held, (to_near, to_far, own, spare), sems = refs[:5], refs[5:10], refs[10:14], refs[14]
     copies = []
     for chunk in range(CHUNKS):
         span = slice(chunk * ROWS // CHUNKS, (chunk + 1) * ROWS // CHUNKS)
@@ -59,33 +73,20 @@
         for copy in copies[-1]:
             copy.start()
     lane, low = lane_of(), low_of()
-    scale = jnp.where(low, 1.0, 0.5)
-    tracer, velocity, slope, kappa, mask = held
+    inside = lax.broadcasted_iota(jnp.int32, (8, 8, LANES), 2) < 64
     first, second = [None] * 8, [None] * 8
     for part in range(8):
         if part * CHUNKS % 8 == 0:
             for copy in copies[part * CHUNKS // 8]:
                 copy.wait()
         span = slice(8 * part, 8 * part + 8)
-        halves = []
-        for h in range(2):
-            wide = slice(h * LANES, (h + 1) * LANES)
-            planes = [
-                tracer[:, span, wide], velocity[0:8, span, wide], velocity[4:12, span, wide], slope[:, span, wide],
-                jnp.concatenate([mask[:, span, wide].astype(F32), kappa[:, span, wide]], axis=0),
-            ]
-            halves.append([jnp.transpose(x, (1, 0, 2)) for x in planes])
+        rims = []
+        for left, right in zip(*[row_planes(held, span, h) for h in range(2)]):
+            rims.append(jnp.transpose(jnp.where(inside, left, right), (1, 0, 2)))
         base = 16 * part
         before, half = lane < base, lane < base + 8
         for g in range(8):
-            rims = []
-            for h in range(2):
-                c, uv, vw, s, mk = [x[g] for x in halves[h]]
-                loaded = (c, uv, vw, s * 0.125, mk * scale)
-                for ref, value in zip(rows, loaded):
-                    ref[8 * part + g, :, h * LANES : (h + 1) * LANES] = value
-                rims.append(loaded)
-            c, uv, vw, s, mk = [jnp.where(lane < 64, a, b) for a, b in zip(*rims)]
+            c, uv, vw, s, mk = scaled([x[g] for x in rims])
             mu = jnp.where(low, mk, pltpu.roll(uv, 4, 0))
             sk = jnp.where(low, s, mk)
             one = jnp.where(half, pltpu.roll(c, (base + 4) % LANES, 1), pltpu.roll(mu, (base + 12) % LANES, 1))
@@ -109,7 +110,13 @@
 
 
 def advect_kernel(*refs):
-    rows, advected = refs[:5], refs[5]
+    held, rows, advected, send_a, send_b = refs[:5], refs[5:10], refs[10], refs[11], refs[12]
+    for part in range(8):
+        for h in range(2):
+            turned = [jnp.transpose(x, (1, 0, 2)) for x in row_planes(held, slice(8 * part, 8 * part + 8), h)]
+            for g in range(8):
+                for ref, value in zip(rows, scaled([x[g] for x in turned])):
+                    ref[8 * part + g, :, h * LANES : (h + 1) * LANES] = value
     get = lambda name, row: field_tiles(rows, name, row)
 
     def advect_block(block, carry):
@@ -120,6 +127,41 @@
         return carry
 
     lax.fori_loop(0, 4, advect_block, 0)
+    put_messages(rows, send_a, send_b)
+
+
+def put_messages(rows, send_a, send_b):
+    lane, low = lane_of(), low_of()
+    lat = lax.axis_index("lat")
+
+    def message(top):
+        row = lambda q: jnp.where(top, ROWS - 1 - q, q)
+        part = lambda name, q, h: field_half(rows, name, row(q), h)
+        pair = lambda n1, q1, n2, q2: [jnp.where(low, part(n1, q1, h), part(n2, q2, h)) for h in range(2)]
+        tiles = [[part("c", q, h) for h in range(2)] for q in range(3)]
+        tiles += [pair("m", 0, "v", 0), pair("m", 1, "v", 1), pair("m", 2, "u", 0), pair("w", 0, "sy", 0)]
+        return tiles + [[part("k", 0, h) for h in range(2)]]
+
+    def store(ref, tiles):
+        for i, tile in enumerate(tiles):
+            for h in range(2):
+                ref[i, :, h * LANES : (h + 1) * LANES] = tile[h]
+
+    even = lat % 2 == 0
+    store(send_a, message(even))
+    folds = lat == lax.axis_size("lat") - 1
+
+    @pl.when(jnp.logical_not(folds))
+    def _():
+        store(send_b, message(jnp.logical_not(even)))
+
+    @pl.when(folds)
+    def _():
+        backward = LANES - 1 - lane
+        flip = lambda x: jnp.take_along_axis(x, backward, axis=1, mode="promise_in_bounds")
+        turned = [[flip(tile[1]), flip(tile[0])] for tile in message(True)]
+        sign = jnp.where(low, 1.0, -1.0)
+        store(send_b, turned[:3] + [[sign * x for x in tile] for tile in turned[3:7]] + turned[7:])
 
 
 def strip_at(g, which, late, from_far, from_near, own, spare):
@@ -137,53 +179,31 @@
 
 
 def edge_kernel(*refs):
-    sources, rows = refs[:4], refs[4:9]
-    send_a, send_b = refs[10:]
+    sources, made, (send_a, send_b) = refs[:4], refs[4:6], refs[6:]
     lane, low = lane_of(), low_of()
     lat = lax.axis_index("lat")
     strips = {(i, g): strip_at(g, i // 2, i % 2, *sources) for i in range(3) for g in (0, 1, 6, 7)}
-
-    def message(top):
-        row = lambda q: jnp.where(top, ROWS - 1 - q, q)
-        part = lambda name, q, h: field_half(rows, name, row(q), h)
-        pair = lambda n1, q1, n2, q2: [jnp.where(low, part(n1, q1, h), part(n2, q2, h)) for h in range(2)]
-        tiles = [[part("c", q, h) for h in range(2)] for q in range(3)]
-        tiles += [pair("m", 0, "v", 0), pair("m", 1, "v", 1), pair("m", 2, "u", 0), pair("w", 0, "sy", 0)]
-        corners = [
-            jnp.where(top, pltpu.roll(strips[i, 7 - q], 16, 1), strips[i, q]) for q in range(2) for i in range(3)
-        ]
-        return tiles, [part("k", 0, h) for h in range(2)], corners
-
-    def store(ref, tiles, kappa, corners):
-        for i, tile in enumerate(tiles):
-            for h in range(2):
-                ref[i, :, h * LANES : (h + 1) * LANES] = tile[h]
+    order = [(q, i) for q in range(2) for i in range(3)]
+    south = [strips[i, q] for q, i in order]
+    north = [pltpu.roll(strips[i, 7 - q], 16, 1) for q, i in order]
+
+    def store(source, ref, corners):
         packed = corners[0]
         for i in range(1, 6):
             packed = jnp.where(lane < 16 * i, packed, pltpu.roll(corners[i], 16 * i, 1))
-        ref[7, :, :LANES] = jnp.where(low, kappa[0], pltpu.roll(packed, 4, 0))
-        ref[7, :, LANES:] = jnp.where(low, kappa[1], packed)
-
-    even = lat % 2 == 0
-    store(send_a, *message(even))
-    folds = lat == lax.axis_size("lat") - 1
-
-    @pl.when(jnp.logical_not(folds))
-    def _():
-        store(send_b, *message(jnp.logical_not(even)))
-
-    @pl.when(folds)
-    def _():
-        tiles, kappa, corners = message(True)
-        backward = LANES - 1 - lane
-        flip = lambda x, index: jnp.take_along_axis(x, index, axis=1, mode="promise_in_bounds")
-        flip_tile = lambda tile: [flip(tile[1], backward), flip(tile[0], backward)]
-        sign = jnp.where(low, 1.0, -1.0)
-        turned = [flip_tile(tile) for tile in tiles]
-        turned = turned[:3] + [[sign * x for x in tile] for tile in turned[3:]]
-        index = jnp.where(lane < 14, 13 - lane, lane)
-        corner_signs = [1.0, sign, -sign]
-        store(send_b, turned, flip_tile(kappa), [corner_signs[i % 3] * flip(x, index) for i, x in enumerate(corners)])
+        ref[7, :, :LANES] = jnp.where(low, source[7, :, :LANES], pltpu.roll(packed, 4, 0))
+        ref[7, :, LANES:] = jnp.where(low, source[7, :, LANES:], packed)
+
+    is_even = jnp.broadcast_to(lat % 2, (8, LANES)) == 0
+    folds = jnp.broadcast_to(lat, (8, LANES)) == lax.axis_size("lat") - 1
+    index = jnp.where(lane < 14, 13 - lane, lane)
+    sign = jnp.where(low, 1.0, -1.0)
+    signs = [1.0, sign, -sign]
+    turned = [
+        signs[i] * jnp.take_along_axis(x, index, axis=1, mode="promise_in_bounds") for (q, i), x in zip(order, north)
+    ]
+    store(made[0], send_a, [jnp.where(is_even, n, s) for n, s in zip(north, south)])
+    store(made[1], send_b, [jnp.where(folds, t, jnp.where(is_even, s, n)) for n, s, t in zip(north, south, turned)])
 
 
 def split_groups(groups):
@@ -401,7 +421,7 @@
 
 
 def rim_kernel(*refs):
-    got_b, got_a = refs[0], refs[1]
+    got_a, got_b = refs[0], refs[1]
     fields = refs[2:7]
     strips, inner, kept, out, edges, sems = refs[7:]
     middle = pltpu.make_async_copy
@@ -507,21 +527,23 @@
         arrays = [plane(tracers), plane(velocity), plane(slopes), diffusivity, sea_mask]
         arrays = [pltpu.with_memory_space_constraint(x, pltpu.HBM) for x in arrays]
         full, side = (ROWS, 8, 2 * LANES), (8, 8, LANES)
-        *rows, to_near, to_far, own, spare = pl.pallas_call(
+        *held, to_near, to_far, own, spare = pl.pallas_call(
             pack_kernel,
-            out_shape=[jax.ShapeDtypeStruct(shape, F32) for shape in [full] * 5 + [(4, 8, LANES)] * 2 + [side] * 2],
+            out_shape=[jax.ShapeDtypeStruct(x.shape, x.dtype) for x in arrays]
+            + [jax.ShapeDtypeStruct(shape, F32) for shape in [(4, 8, LANES)] * 2 + [side] * 2],
             in_specs=[pl.BlockSpec(memory_space=pltpu.HBM)] * 5,
             out_specs=[VMEM] * 9,
-            scratch_shapes=[pltpu.VMEM(x.shape, x.dtype) for x in arrays] + [pltpu.SemaphoreType.DMA((CHUNKS, 5))],
+            scratch_shapes=[pltpu.SemaphoreType.DMA((CHUNKS, 5))],
             compiler_params=pltpu.CompilerParams(vmem_limit_bytes=LIMIT),
         )(*arrays)
         far_got, near_got = move(to_far, far), move(to_near, near)
-        (advected,) = call(
-            advect_kernel, [full], *rows,
+        *rows, advected, made_a, made_b = call(
+            advect_kernel, [full] * 6 + [(8, 8, 2 * LANES)] * 2, *held,
             cost_estimate=pl.CostEstimate(flops=10**7, bytes_accessed=6 * 10**6, transcendentals=0),
         )
         send_a, send_b = call(
-            edge_kernel, [(8, 8, 2 * LANES)] * 2, far_got, near_got, own, spare, *rows, advected
+            edge_kernel, [(8, 8, 2 * LANES)] * 2, far_got, near_got, own, spare, made_a, made_b,
+            input_output_aliases={4: 0, 5: 1},
         )
         got_a, got_b = move(send_a, pair_a), move(send_b, pair_b)
         inner, kept, strips = call(
@@ -536,7 +558,7 @@
             out_specs=pl.BlockSpec(memory_space=pl.ANY),
             scratch_shapes=[pltpu.VMEM((2, 8, 8, 2 * LANES), F32), pltpu.SemaphoreType.DMA((10,))],
             compiler_params=pltpu.CompilerParams(vmem_limit_bytes=LIMIT),
-        )(got_b, got_a, *rows, strips, inner, kept)
+        )(got_a, got_b, *rows, strips, inner, kept)
         return out.reshape(tracers.shape)
 
     return shards

time: 20.3 us -> 20.2 us (level)
  the two profiles are of different devices: /device:TPU:36 before, /device:TPU:6 now
where the time goes in v8:
time: 20.2 us; the launch traced here: 20.1 us
  Pallas kernels  9.06 us (45%)
  starting transfers between devices  8.32 us (41%)
  waiting for transfers between devices  2.66 us (13%)
    ppermute x4, starting transfers between devices, move(): return lax.ppermute(x, ('lon', 'lat'), route)  8.32 us
    pallas_call x3, Pallas kernels, call(): pl.pallas_call(kernel, out_shape=[jax.ShapeDtypeStruct(s, F32) for s in s...  5.68 us
    ppermute x4, waiting for transfers between devices, move(): return lax.ppermute(x, ('lon', 'lat'), route)  2.66 us
    pallas_call x1, Pallas kernels, shards(): pl.pallas_call(pack_kernel, out_shape=[jax.ShapeDtypeStruct(x.shape, x.dt...  2 us
    pallas_call x1, Pallas kernels, shards(): pl.pallas_call(rim_kernel, out_shape=jax.ShapeDtypeStruct((8, ROWS, 2 * L...  1.38 us
  transfers between devices with their start and end apart: 4, of which 1 were waited for; matrix products, arithmetic and copies ran while one was open for 0% of the time, Pallas kernels for 27%

profile of v8, /device:TPU:6, one launch (start us, length us, event | category | flops | bytes accessed | tf_op | source)
XLA Modules:
  0.0 20.1 jit_solution(18393927317329936980)
XLA Ops:
  0.0 2.0 %shard_map.55 = (f32[8,64,256]{2,1,0:T(8,128)S(1)}, f32[12,64,256]{2,1,0:T(8,128)S(1)}, f32[8,64,256]{2,1,0:T(8,128)S(1)}, f32[4,64,256]{2,1,0:T(8,128)S(1)}, s3...) custom-call(f32[8,64,256]{2,1,0:T(8,128)} %bitcast.5, ...), custom_call_target="tpu_custom_call" | custom-call | tf_op jit(solution)/shard_map/pallas_call | solution.py:530
  2.0 5.8 %collective-permute-start = (f32[4,8,128]{2,1,0:T(8,128)S(1)}, f32[4,8,128]{2,1,0:T(8,128)S(1)}, u32[]{:S(2)}, u32[]{:S(2)}) collective-permute-start(f32[4,8,128]{2,1,0:T(8,128)S(1)} %get-tuple-element.27), channel_id=1, source_target_pairs={{0,120},{1,121},{2,122},{3,123},{4,124},{5,125},{6,126},{7,127},{8... | collective-permute-start | bytes 49160 | tf_op jit(solution)/shard_map/ppermute | solution.py:523
  7.9 0.0 collective-permute-start.1
  7.9 2.2 %shard_map.56 = (f32[64,8,256]{2,1,0:T(8,128)S(1)}, f32[64,8,256]{2,1,0:T(8,128)S(1)}, f32[64,8,256]{2,1,0:T(8,128)S(1)}, f32[64,8,256]{2,1,0:T(8,128)S(1)}, f32...) custom-call(f32[8,64,256]{2,1,0:T(8,128)S(1)} %get-tuple-element.31.ref, ...), custom_call_target="tpu_custom_call" | custom-call | flops 10000000 | bytes 6000000 | tf_op jit(solution)/shard_map/pallas_call | solution.py:495
  10.1 0.0 collective-permute-done.refs_0_.refs_6_
  10.1 0.0 collective-permute-done.1.refs_1_.refs_7_
  10.1 0.3 %shard_map.57 = (f32[8,8,256]{2,1,0:T(8,128)S(1)}, f32[8,8,256]{2,1,0:T(8,128)S(1)}) custom-call(f32[4,8,128]{2,1,0:T(8,128)S(1)} %collective-permute-done.refs_0_.refs_6_, f32[4,8,128]{2,1,0:T(8,128)S(1)} %collective-permute-done.1.refs_1_.refs_7_, ...), custom_call_target="tpu_custom_call", output_to_operand_aliasing={{0}: (4, {}), {1}: (5, {})} | custom-call | tf_op jit(solution)/shard_map/pallas_call | solution.py:495
  10.4 0.9 %collective-permute-start.2 = (f32[8,8,256]{2,1,0:T(8,128)S(1)}, f32[8,8,256]{2,1,0:T(8,128)S(1)}, u32[]{:S(2)}, u32[]{:S(2)}) collective-permute-start(f32[8,8,256]{2,1,0:T(8,128)S(1)} %get-tuple-element.38), channel_id=1, source_target_pairs={{0,1},{1,0},{2,3},{3,2},{4,5},{5,4},{6,7},{7,6},{8,9},{9,8},{10,11... | collective-permute-start | bytes 196616 | tf_op jit(solution)/shard_map/ppermute | solution.py:523
  11.2 1.6 %collective-permute-start.3 = (f32[8,8,256]{2,1,0:T(8,128)S(1)}, f32[8,8,256]{2,1,0:T(8,128)S(1)}, u32[]{:S(2)}, u32[]{:S(2)}) collective-permute-start(f32[8,8,256]{2,1,0:T(8,128)S(1)} %get-tuple-element.39), channel_id=1, source_target_pairs={{0,8},{1,2},{2,1},{3,4},{4,3},{5,6},{6,5},{7,127},{8,0},{9,10},{10... | collective-permute-start | bytes 196616 | tf_op jit(solution)/shard_map/ppermute | solution.py:523
  12.8 3.2 %shard_map.58 = (f32[64,8,256]{2,1,0:T(8,128)S(1)}, f32[4,8,384]{2,1,0:T(8,128)S(1)}, f32[4,8,8,128]{3,2,1,0:T(8,128)S(1)}) custom-call(f32[64,8,256]{2,1,0:T(8,128)S(1)} %get-tuple-element.40.refs_0_.refs_2_, f32[64,8,256]{2,1,0:T(8,128)S(1)} %get-tuple-element.41.refs_1_.refs_3_, f32[64,8,256]{2,1,0:T(8,128)S(1)} %get-tuple-element.42.refs_2_.refs_4_, ...), custom_call_target="tpu_custom_call" | custom-call | flops 20000000 | bytes 10000000 | tf_op jit(solution)/shard_map/pallas_call | solution.py:495
  16.0 0.0 collective-permute-done.2.refs_0_
  16.1 2.6 %collective-permute-done.3.refs_1_ = f32[8,8,256]{2,1,0:T(8,128)S(1)} collective-permute-done((f32[8,8,256]{2,1,0:T(8,128)S(1)}, f32[8,8,256]{2,1,0:T(8,128)S(1)}, u32[]{:S(2)}, u32[]{:S(2)}) %collective-permute-start.3) | collective-permute-done | bytes 65568 | tf_op jit(solution)/shard_map/ppermute | solution.py:523
  18.7 1.4 %shard_map.59 = f32[8,64,256]{2,1,0:T(8,128)} custom-call(f32[8,8,256]{2,1,0:T(8,128)S(1)} %collective-permute-done.2.refs_0_, f32[8,8,256]{2,1,0:T(8,128)S(1)} %collective-permute-done.3.refs_1_, f32[64,8,256]{2,1,0:T(8,128)S(1)} %get-tuple-element.40.refs_0_.refs_2_, f32[64,8,256]{2,1,0:T(8,128)S(1)} %get-tuple-element.41.refs_1_.refs_3_, ...), custom_call_target="tpu_custom_call" | custom-call | tf_op jit(solution)/shard_map/pallas_call | solution.py:554
Async XLA Ops:
  2.0 8.1 %collective-permute-start = (f32[4,8,128]{2,1,0:T(8,128)S(1)}, f32[4,8,128]{2,1,0:T(8,128)S(1)}, u32[]{:S(2)}, u32[]{:S(2)}) collective-permute-start(f32[4,8,128]{2,1,0:T(8,128)S(1)} %get-tuple-element.27), channel_id=1, source_target_pairs={{0,120},{1,121},{2,122},{3,123},{4,124},{5,125},{6,126},{7,127},{8... | collective-permute-start | bytes 49160 | tf_op jit(solution)/shard_map/ppermute | solution.py:523
  7.9 2.2 %collective-permute-start.1 = (f32[4,8,128]{2,1,0:T(8,128)S(1)}, f32[4,8,128]{2,1,0:T(8,128)S(1)}, u32[]{:S(2)}, u32[]{:S(2)}) collective-permute-start(f32[4,8,128]{2,1,0:T(8,128)S(1)} %get-tuple-element.28), channel_id=1, source_target_pairs={{0,8},{1,9},{2,10},{3,11},{4,12},{5,13},{6,14},{7,15},{8,0},{9,1},... | collective-permute-start | bytes 49160 | tf_op jit(solution)/shard_map/ppermute | solution.py:523
  10.4 5.7 %collective-permute-start.2 = (f32[8,8,256]{2,1,0:T(8,128)S(1)}, f32[8,8,256]{2,1,0:T(8,128)S(1)}, u32[]{:S(2)}, u32[]{:S(2)}) collective-permute-start(f32[8,8,256]{2,1,0:T(8,128)S(1)} %get-tuple-element.38), channel_id=1, source_target_pairs={{0,1},{1,0},{2,3},{3,2},{4,5},{5,4},{6,7},{7,6},{8,9},{9,8},{10,11... | collective-permute-start | bytes 196616 | tf_op jit(solution)/shard_map/ppermute | solution.py:523
  11.2 7.5 %collective-permute-start.3 = (f32[8,8,256]{2,1,0:T(8,128)S(1)}, f32[8,8,256]{2,1,0:T(8,128)S(1)}, u32[]{:S(2)}, u32[]{:S(2)}) collective-permute-start(f32[8,8,256]{2,1,0:T(8,128)S(1)} %get-tuple-element.39), channel_id=1, source_target_pairs={{0,8},{1,2},{2,1},{3,4},{4,3},{5,6},{6,5},{7,127},{8,0},{9,10},{10... | collective-permute-start | bytes 196616 | tf_op jit(solution)/shard_map/ppermute | solution.py:523

commit v9 on v8

--- a/solution.py
+++ b/solution.py
@@ -121,7 +121,7 @@
 
     def advect_block(block, carry):
         first = 2 + 15 * block
-        for j, tiles in enumerate(advect_rows(get, first, 15)):
+        for j, tiles in enumerate(advect_rows(get, first, 15)[0]):
             for t in range(2):
                 advected[first + j, :, t * LANES : (t + 1) * LANES] = tiles[t]
         return carry
@@ -134,13 +134,32 @@
     lane, low = lane_of(), low_of()
     lat = lax.axis_index("lat")
 
+    first, last = lane < 2, lane >= LANES - 2
+
     def message(top):
         row = lambda q: jnp.where(top, ROWS - 1 - q, q)
-        part = lambda name, q, h: field_half(rows, name, row(q), h)
-        pair = lambda n1, q1, n2, q2: [jnp.where(low, part(n1, q1, h), part(n2, q2, h)) for h in range(2)]
-        tiles = [[part("c", q, h) for h in range(2)] for q in range(3)]
-        tiles += [pair("m", 0, "v", 0), pair("m", 1, "v", 1), pair("m", 2, "u", 0), pair("w", 0, "sy", 0)]
-        return tiles + [[part("k", 0, h) for h in range(2)]]
+        part = lambda name, q: field_tiles(rows, name, row(q))
+        outward = jnp.where(jnp.broadcast_to(jnp.where(top, 1, 0), (8, LANES)) == 1, 1.0, -1.0)
+        c, m, v = [part("c", q) for q in range(3)], [part("m", q) for q in range(3)], [part("v", q) for q in range(2)]
+        half = each(lambda x: 0.5 * x, m[1])
+        opened = each(jnp.multiply, half, m[0])
+        step = each(lambda a, b, o: (a - b) * o, c[0], c[1], opened)
+        inner = each(lambda a, b, x, y: (a - b) * (x * y), c[1], c[2], half, m[2])
+        speed = each(lambda a, b, o: (a + b) * o * outward, v[0], v[1], opened)
+        inflow = each(
+            lambda a, b, s, x, y: s * jnp.where(s >= 0.0, a, b)
+            + jnp.where(s >= 0.0, (jnp.abs(s) - s * s) * median(x, y), 0.0),
+            c[1], c[0], speed, step, inner,
+        )
+        rest = each(lambda s: jnp.where(s >= 0.0, 0.0, jnp.abs(s) - s * s), speed)
+        halved = each(lambda x: 0.5 * x, m[0])
+        flux_x = zonal_flux(c[0], m[0], halved, part("u", 0))
+        across = each(lambda f, g: f - g, flux_x, minus(flux_x))
+        across = [jnp.where(first, 0.0, across[0]), jnp.where(last, 0.0, across[1])]
+        down = each(vertical_divergence, c[0], halved, part("w", 0))
+        cell = each(lambda a, x, z, f: a - x - z + f, c[0], across, down, inflow)
+        pair = lambda a, b: each(lambda x, y: jnp.where(low, x, y), a, b)
+        return [cell, step, c[0], pair(m[0], rest), pair(v[0], part("sy", 0)), part("k", 0)]
 
     def store(ref, tiles):
         for i, tile in enumerate(tiles):
@@ -160,8 +179,8 @@
         backward = LANES - 1 - lane
         flip = lambda x: jnp.take_along_axis(x, backward, axis=1, mode="promise_in_bounds")
         turned = [[flip(tile[1]), flip(tile[0])] for tile in message(True)]
-        sign = jnp.where(low, 1.0, -1.0)
-        store(send_b, turned[:3] + [[sign * x for x in tile] for tile in turned[3:7]] + turned[7:])
+        turned[4] = [-x for x in turned[4]]
+        store(send_b, turned)
 
 
 def strip_at(g, which, late, from_far, from_near, own, spare):
@@ -182,28 +201,34 @@
     sources, made, (send_a, send_b) = refs[:4], refs[4:6], refs[6:]
     lane, low = lane_of(), low_of()
     lat = lax.axis_index("lat")
-    strips = {(i, g): strip_at(g, i // 2, i % 2, *sources) for i in range(3) for g in (0, 1, 6, 7)}
-    order = [(q, i) for q in range(2) for i in range(3)]
-    south = [strips[i, q] for q, i in order]
-    north = [pltpu.roll(strips[i, 7 - q], 16, 1) for q, i in order]
-
-    def store(source, ref, corners):
+    strip = lambda i, g: strip_at(g, i // 2, i % 2, *sources)
+
+    def beside(g, inner, turn):
+        c, mu, vw = strip(0, g), strip(1, g), strip(2, g)
+        m = twice_low(mu)
+        flux_x = zonal_flux([c], [m], [0.5 * m], [twice_high(mu)])
+        step = (c - strip(0, inner)) * (0.5 * m * twice_low(strip(1, inner)))
+        values = [flux_x[0] - minus(flux_x)[0], c, step, jnp.where(low, mu, pltpu.roll(vw, 4, 0))]
+        return [pltpu.roll(x, turn, 1) if turn else x for x in values]
+
+    south, north = beside(0, 1, 0), beside(7, 6, 16)
+
+    def store(source, ref, across, *corners):
+        ref[0, :, :LANES] = source[0, :, :LANES] - jnp.where(lane < 2, pltpu.roll(across, LANES - 10, 1), 0.0)
+        ref[0, :, LANES:] = source[0, :, LANES:] - jnp.where(lane >= LANES - 2, pltpu.roll(across, LANES - 4, 1), 0.0)
         packed = corners[0]
-        for i in range(1, 6):
+        for i in range(1, 3):
             packed = jnp.where(lane < 16 * i, packed, pltpu.roll(corners[i], 16 * i, 1))
-        ref[7, :, :LANES] = jnp.where(low, source[7, :, :LANES], pltpu.roll(packed, 4, 0))
-        ref[7, :, LANES:] = jnp.where(low, source[7, :, LANES:], packed)
+        ref[5, :, :LANES] = jnp.where(low, source[5, :, :LANES], pltpu.roll(packed, 4, 0))
+        ref[5, :, LANES:] = jnp.where(low, source[5, :, LANES:], packed)
 
     is_even = jnp.broadcast_to(lat % 2, (8, LANES)) == 0
     folds = jnp.broadcast_to(lat, (8, LANES)) == lax.axis_size("lat") - 1
     index = jnp.where(lane < 14, 13 - lane, lane)
-    sign = jnp.where(low, 1.0, -1.0)
-    signs = [1.0, sign, -sign]
-    turned = [
-        signs[i] * jnp.take_along_axis(x, index, axis=1, mode="promise_in_bounds") for (q, i), x in zip(order, north)
-    ]
-    store(made[0], send_a, [jnp.where(is_even, n, s) for n, s in zip(north, south)])
-    store(made[1], send_b, [jnp.where(folds, t, jnp.where(is_even, s, n)) for n, s, t in zip(north, south, turned)])
+    turned = [jnp.take_along_axis(x, index, axis=1, mode="promise_in_bounds") for x in north]
+    turned[3] = jnp.where(low, turned[3], -turned[3])
+    store(made[0], send_a, *[jnp.where(is_even, n, s) for n, s in zip(north, south)])
+    store(made[1], send_b, *[jnp.where(folds, t, jnp.where(is_even, s, n)) for n, s, t in zip(north, south, turned)])
 
 
 def split_groups(groups):
@@ -218,12 +243,13 @@
     }
 
 
-def third_tile(groups, bases):
-    east = lane_of() < 64
-    tile = lambda x, base: jnp.where(
-        east, pltpu.roll(x, (2 * LANES - 4 - base) % LANES, 1), pltpu.roll(x, (2 * LANES - 10 - base) % LANES, 1)
-    )
-    return split_groups({n: tile(groups[n], bases[n]) for n in GROUPS})
+def third_of(x, base):
+    east, west = pltpu.roll(x, (2 * LANES - 4 - base) % LANES, 1), pltpu.roll(x, (2 * LANES - 10 - base) % LANES, 1)
+    return jnp.where(lane_of() < 64, east, west)
+
+
+def third_tile(groups, base):
+    return split_groups({n: third_of(groups[n], base) for n in GROUPS})
 
 
 def plus(tiles):
@@ -255,12 +281,31 @@
     return pltpu.roll(x, 1, 0)
 
 
+def median(step, upwind):
+    return jnp.minimum(jnp.maximum(upwind, jnp.minimum(step, 0.0)), jnp.maximum(step, 0.0))
+
+
 def face_flux(here, there, speed, back, step, ahead):
     positive = speed >= 0.0
     upwind = jnp.where(positive, back, ahead)
     size = jnp.abs(speed)
-    limited = jnp.minimum(jnp.maximum(upwind, jnp.minimum(step, 0.0)), jnp.maximum(step, 0.0))
-    return speed * jnp.where(positive, here, there) + (size - size * size) * limited
+    return speed * jnp.where(positive, here, there) + (size - size * size) * median(step, upwind)
+
+
+def zonal_flux(c, m, half, u):
+    east = plus(c)
+    opened = each(jnp.multiply, half, plus(m))
+    speed = each(face_speed, u, plus(u), opened)
+    step = each(lambda a, b, o: (b - a) * o, c, east, opened)
+    return each(face_flux, c, east, speed, minus(step), step, plus(step))
+
+
+def vertical_divergence(value, half, down):
+    opened = open_below(half)
+    under = below(value)
+    step = (under - value) * opened
+    flux = face_flux(value, under, face_speed(down, below(down), opened), above(step), step, below(step))
+    return flux - above(flux)
 
 
 def not_bottom():
@@ -275,38 +320,27 @@
     return (one + two) * half_open
 
 
-def advect_rows(get, first, count):
-    c = {j: get("c", first + j) for j in range(-2, count + 2)}
-    m = {j: get("m", first + j) for j in range(-2, count + 2)}
+def advect_rows(get, first, count, known=()):
+    known = dict(known)
+    low, high = (-1 if -2 in known else -2), (count + 1 if count in known else count + 2)
+    c = {j: get("c", first + j) for j in range(low, high)}
+    m = {j: get("m", first + j) for j in range(low, high)}
     v = {j: get("v", first + j) for j in range(-1, count + 1)}
-    half = {j: each(lambda x: 0.5 * x, m[j]) for j in range(-2, count + 2)}
-    opened = {j: each(jnp.multiply, half[j], m[j + 1]) for j in range(-2, count + 1)}
-    step = {j: each(lambda a, b, o: (b - a) * o, c[j], c[j + 1], opened[j]) for j in range(-2, count + 1)}
+    half = {j: each(lambda x: 0.5 * x, m[j]) for j in range(low, high)}
+    opened = {j: each(jnp.multiply, half[j], m[j + 1]) for j in range(low, high - 1)}
+    step = {j: each(lambda a, b, o: (b - a) * o, c[j], c[j + 1], opened[j]) for j in range(low, high - 1)}
+    step.update(known)
     flux = {}
     for j in range(-1, count):
         speed = each(face_speed, v[j], v[j + 1], opened[j])
         flux[j] = each(face_flux, c[j], c[j + 1], speed, step[j - 1], step[j], step[j + 1])
     result = []
     for j in range(count):
-        east = plus(c[j])
-        opened_x = each(jnp.multiply, half[j], plus(m[j]))
-        u = get("u", first + j)
-        speed = each(face_speed, u, plus(u), opened_x)
-        step_x = each(lambda a, b, o: (b - a) * o, c[j], east, opened_x)
-        flux_x = each(face_flux, c[j], east, speed, minus(step_x), step_x, plus(step_x))
+        flux_x = zonal_flux(c[j], m[j], half[j], get("u", first + j))
         total = each(lambda f, g, a, b: (f - g) + (a - b), flux_x, minus(flux_x), flux[j], flux[j - 1])
-        w = get("w", first + j)
-
-        def finish(value, marker, halved, down, across):
-            opened_z = open_below(halved)
-            under = below(value)
-            step_z = (under - value) * opened_z
-            speed_z = face_speed(down, below(down), opened_z)
-            flux_z = face_flux(value, under, speed_z, above(step_z), step_z, below(step_z))
-            return (value - across - (flux_z - above(flux_z))) * marker
-
-        result.append(each(finish, c[j], m[j], half[j], w, total))
-    return result
+        down = each(vertical_divergence, c[j], half[j], get("w", first + j))
+        result.append(each(lambda a, x, z, o: (a - x - z) * o, c[j], total, down, m[j]))
+    return result, flux, step
 
 
 def slope_flux(k1, k2, opened, step, s1, s2, z1, z2):
@@ -383,7 +417,7 @@
         x = full[g % 8][name]
         return [x if 0 <= g < 8 else pltpu.roll(x, 16 if g < 0 else LANES - 16, 1)]
 
-    for g, (a,) in enumerate(advect_rows(get_strip, 0, 8)):
+    for g, (a,) in enumerate(advect_rows(get_strip, 0, 8)[0]):
         part = full[g]
         step_z = (below(a) - a) * open_below(part["m"])
         step, flux = eastward([a], [part["m"]], [part["k"]], [part["sx"]], [above(step_z) + step_z])
@@ -441,43 +475,42 @@
                 return jnp.where(even, a, b)
             return jnp.where(floor, 0.0, jnp.where(even, b, a))
 
-        tiles = [[tile(i, h) for h in range(2)] for i in range(8)]
-        high = lambda i: [twice_high(x) for x in tiles[i]]
-        below_four = lambda i: [twice_low(x) for x in tiles[i]]
-        corner = jnp.where(low, pltpu.roll(tiles[7][0], 4, 0), tiles[7][1])
-        rows = []
-        for q in range(3):
-            bases = {n: 16 * (3 * min(q, 1) + min(i, 2)) for i, n in enumerate(GROUPS)}
-            side = third_tile({n: corner for n in GROUPS}, bases)
-            main = {"c": tiles[q], "m": below_four(3 + q)}
-            if q < 2:
-                main["v"] = high(3 + q)
-            if q == 0:
-                main.update(u=high(5), w=below_four(6), sy=high(6), k=below_four(7))
-                main["sx"] = main["k"]
-            rows.append({n: x + [side[n]] if n in side else x for n, x in main.items()})
-        return rows
+        tiles = [[tile(i, h) for h in range(2)] for i in range(6)]
+        corner = jnp.where(low, pltpu.roll(tiles[5][0], 4, 0), tiles[5][1])
+        c_side, step_side, mv = [third_of(corner, 16 * i) for i in range(3)]
+        row = {
+            "c": tiles[2] + [c_side],
+            "m": each(twice_low, tiles[3]) + [twice_low(mv)],
+            "v": each(twice_low, tiles[4]) + [twice_high(mv)],
+            "sy": each(twice_high, tiles[4]),
+            "k": each(twice_low, tiles[5]),
+        }
+        return row, tiles[0], tiles[1] + [step_side], each(twice_high, tiles[3])
 
     for is_north in (False, True):
-        rows = halo(is_north)
-        start = ROWS - 2 if is_north else -1
+        outer, cell, step_in, rest = halo(is_north)
+        start, beyond = (ROWS - 2, ROWS) if is_north else (0, -1)
         made, sides = {}, {}
         for row in range(*((ROWS - 4, ROWS) if is_north else (0, 4))):
             base = 16 * (row // 8)
-            sides[row] = third_tile({n: strips[i, row % 8] for i, n in enumerate(GROUPS)}, dict.fromkeys(GROUPS, base))
+            sides[row] = third_tile({n: strips[i, row % 8] for i, n in enumerate(GROUPS)}, base)
 
         def get(name, row):
             if name == "a":
                 return made[row] if row in made else tiles_of(kept, KEPT.index(row), 3)
-            if row < 0:
-                return rows[-row - 1][name]
-            if row >= ROWS:
-                return rows[row - ROWS][name]
+            if row == beyond:
+                return outer[name]
             tiles = field_tiles(fields, name, row)
             return tiles if name == "sy" else tiles + [sides[row][name]]
 
-        for j, tiles in enumerate(advect_rows(get, start, 3)):
-            made[start + j] = tiles
+        known = {2: [-x for x in step_in]} if is_north else {-2: step_in}
+        results, flux, step = advect_rows(get, start, 2, known)
+        made.update(zip((start, start + 1), results))
+        face, sign = (1, -1.0) if is_north else (-1, 1.0)
+        made[beyond] = each(
+            lambda q, g, s, t, f, o: (q + g * median(s, sign * t) - sign * f) * o,
+            cell, rest, step_in, step[face], flux[face], outer["m"],
+        )
         final = ROWS - 3 if is_north else 0
         base = ROWS - 8 if is_north else 0
         done = {final + j: x for j, x in enumerate(diffuse_rows(get, final, 3))}
@@ -538,11 +571,11 @@
         )(*arrays)
         far_got, near_got = move(to_far, far), move(to_near, near)
         *rows, advected, made_a, made_b = call(
-            advect_kernel, [full] * 6 + [(8, 8, 2 * LANES)] * 2, *held,
+            advect_kernel, [full] * 6 + [(6, 8, 2 * LANES)] * 2, *held,
             cost_estimate=pl.CostEstimate(flops=10**7, bytes_accessed=6 * 10**6, transcendentals=0),
         )
         send_a, send_b = call(
-            edge_kernel, [(8, 8, 2 * LANES)] * 2, far_got, near_got, own, spare, made_a, made_b,
+            edge_kernel, [(6, 8, 2 * LANES)] * 2, far_got, near_got, own, spare, made_a, made_b,
             input_output_aliases={4: 0, 5: 1},
         )
         got_a, got_b = move(send_a, pair_a), move(send_b, pair_b)

time: 20.2 us -> 20 us (0.990)
  the two profiles are of different devices: /device:TPU:6 before, /device:TPU:39 now
where the time goes in v9:
time: 20 us; the launch traced here: 19.9 us
  Pallas kernels  9.63 us (48%)
  starting transfers between devices  8.63 us (43%)
  waiting for transfers between devices  1.57 us (8%)
    ppermute x4, starting transfers between devices, move(): return lax.ppermute(x, ('lon', 'lat'), route)  8.63 us
    pallas_call x3, Pallas kernels, call(): pl.pallas_call(kernel, out_shape=[jax.ShapeDtypeStruct(s, F32) for s in s...  6.38 us
    pallas_call x1, Pallas kernels, shards(): pl.pallas_call(pack_kernel, out_shape=[jax.ShapeDtypeStruct(x.shape, x.dt...  2 us
    ppermute x4, waiting for transfers between devices, move(): return lax.ppermute(x, ('lon', 'lat'), route)  1.57 us
    pallas_call x1, Pallas kernels, shards(): pl.pallas_call(rim_kernel, out_shape=jax.ShapeDtypeStruct((8, ROWS, 2 * L...  1.26 us
  transfers between devices with their start and end apart: 4, of which 1 were waited for; matrix products, arithmetic and copies ran while one was open for 0% of the time, Pallas kernels for 30%

profile of v9, /device:TPU:39, one launch (start us, length us, event | category | flops | bytes accessed | tf_op | source)
XLA Modules:
  0.0 19.9 jit_solution(7098641242084396266)
XLA Ops:
  0.0 2.0 %shard_map.55 = (f32[8,64,256]{2,1,0:T(8,128)S(1)}, f32[12,64,256]{2,1,0:T(8,128)S(1)}, f32[8,64,256]{2,1,0:T(8,128)S(1)}, f32[4,64,256]{2,1,0:T(8,128)S(1)}, s3...) custom-call(f32[8,64,256]{2,1,0:T(8,128)} %bitcast.5, ...), custom_call_target="tpu_custom_call" | custom-call | tf_op jit(solution)/shard_map/pallas_call | solution.py:563
  2.0 3.3 %collective-permute-start = (f32[4,8,128]{2,1,0:T(8,128)S(1)}, f32[4,8,128]{2,1,0:T(8,128)S(1)}, u32[]{:S(2)}, u32[]{:S(2)}) collective-permute-start(f32[4,8,128]{2,1,0:T(8,128)S(1)} %get-tuple-element.27), channel_id=1, source_target_pairs={{0,120},{1,121},{2,122},{3,123},{4,124},{5,125},{6,126},{7,127},{8... | collective-permute-start | bytes 49160 | tf_op jit(solution)/shard_map/ppermute | solution.py:556
  5.3 2.3 %collective-permute-start.1 = (f32[4,8,128]{2,1,0:T(8,128)S(1)}, f32[4,8,128]{2,1,0:T(8,128)S(1)}, u32[]{:S(2)}, u32[]{:S(2)}) collective-permute-start(f32[4,8,128]{2,1,0:T(8,128)S(1)} %get-tuple-element.28), channel_id=1, source_target_pairs={{0,8},{1,9},{2,10},{3,11},{4,12},{5,13},{6,14},{7,15},{8,0},{9,1},... | collective-permute-start | bytes 49160 | tf_op jit(solution)/shard_map/ppermute | solution.py:556
  7.6 2.7 %shard_map.56 = (f32[64,8,256]{2,1,0:T(8,128)S(1)}, f32[64,8,256]{2,1,0:T(8,128)S(1)}, f32[64,8,256]{2,1,0:T(8,128)S(1)}, f32[64,8,256]{2,1,0:T(8,128)S(1)}, f32...) custom-call(f32[8,64,256]{2,1,0:T(8,128)S(1)} %get-tuple-element.31.ref, ...), custom_call_target="tpu_custom_call" | custom-call | flops 10000000 | bytes 6000000 | tf_op jit(solution)/shard_map/pallas_call | solution.py:528
  10.3 0.0 collective-permute-done.refs_0_.refs_6_
  10.3 0.0 collective-permute-done.1.refs_1_.refs_7_
  10.3 0.5 %shard_map.57 = (f32[6,8,256]{2,1,0:T(8,128)S(1)}, f32[6,8,256]{2,1,0:T(8,128)S(1)}) custom-call(f32[4,8,128]{2,1,0:T(8,128)S(1)} %collective-permute-done.refs_0_.refs_6_, f32[4,8,128]{2,1,0:T(8,128)S(1)} %collective-permute-done.1.refs_1_.refs_7_, ...), custom_call_target="tpu_custom_call", output_to_operand_aliasing={{0}: (4, {}), {1}: (5, {})} | custom-call | tf_op jit(solution)/shard_map/pallas_call | solution.py:528
  10.8 0.5 %collective-permute-start.2 = (f32[6,8,256]{2,1,0:T(8,128)S(1)}, f32[6,8,256]{2,1,0:T(8,128)S(1)}, u32[]{:S(2)}, u32[]{:S(2)}) collective-permute-start(f32[6,8,256]{2,1,0:T(8,128)S(1)} %get-tuple-element.38), channel_id=1, source_target_pairs={{0,1},{1,0},{2,3},{3,2},{4,5},{5,4},{6,7},{7,6},{8,9},{9,8},{10,11... | collective-permute-start | bytes 147464 | tf_op jit(solution)/shard_map/ppermute | solution.py:556
  11.3 2.5 %collective-permute-start.3 = (f32[6,8,256]{2,1,0:T(8,128)S(1)}, f32[6,8,256]{2,1,0:T(8,128)S(1)}, u32[]{:S(2)}, u32[]{:S(2)}) collective-permute-start(f32[6,8,256]{2,1,0:T(8,128)S(1)} %get-tuple-element.39), channel_id=1, source_target_pairs={{0,8},{1,2},{2,1},{3,4},{4,3},{5,6},{6,5},{7,127},{8,0},{9,10},{10... | collective-permute-start | bytes 147464 | tf_op jit(solution)/shard_map/ppermute | solution.py:556
  13.8 3.2 %shard_map.58 = (f32[64,8,256]{2,1,0:T(8,128)S(1)}, f32[4,8,384]{2,1,0:T(8,128)S(1)}, f32[4,8,8,128]{3,2,1,0:T(8,128)S(1)}) custom-call(f32[64,8,256]{2,1,0:T(8,128)S(1)} %get-tuple-element.40.refs_0_.refs_2_, f32[64,8,256]{2,1,0:T(8,128)S(1)} %get-tuple-element.41.refs_1_.refs_3_, f32[64,8,256]{2,1,0:T(8,128)S(1)} %get-tuple-element.42.refs_2_.refs_4_, ...), custom_call_target="tpu_custom_call" | custom-call | flops 20000000 | bytes 10000000 | tf_op jit(solution)/shard_map/pallas_call | solution.py:528
  17.0 0.0 collective-permute-done.2.refs_0_
  17.0 1.6 %collective-permute-done.3.refs_1_ = f32[6,8,256]{2,1,0:T(8,128)S(1)} collective-permute-done((f32[6,8,256]{2,1,0:T(8,128)S(1)}, f32[6,8,256]{2,1,0:T(8,128)S(1)}, u32[]{:S(2)}, u32[]{:S(2)}) %collective-permute-start.3) | collective-permute-done | bytes 49184 | tf_op jit(solution)/shard_map/ppermute | solution.py:556
  18.6 1.3 %shard_map.59 = f32[8,64,256]{2,1,0:T(8,128)} custom-call(f32[6,8,256]{2,1,0:T(8,128)S(1)} %collective-permute-done.2.refs_0_, f32[6,8,256]{2,1,0:T(8,128)S(1)} %collective-permute-done.3.refs_1_, f32[64,8,256]{2,1,0:T(8,128)S(1)} %get-tuple-element.40.refs_0_.refs_2_, f32[64,8,256]{2,1,0:T(8,128)S(1)} %get-tuple-element.41.refs_1_.refs_3_, ...), custom_call_target="tpu_custom_call" | custom-call | tf_op jit(solution)/shard_map/pallas_call | solution.py:587
Async XLA Ops:
  2.0 8.3 %collective-permute-start = (f32[4,8,128]{2,1,0:T(8,128)S(1)}, f32[4,8,128]{2,1,0:T(8,128)S(1)}, u32[]{:S(2)}, u32[]{:S(2)}) collective-permute-start(f32[4,8,128]{2,1,0:T(8,128)S(1)} %get-tuple-element.27), channel_id=1, source_target_pairs={{0,120},{1,121},{2,122},{3,123},{4,124},{5,125},{6,126},{7,127},{8... | collective-permute-start | bytes 49160 | tf_op jit(solution)/shard_map/ppermute | solution.py:556
  5.3 5.0 %collective-permute-start.1 = (f32[4,8,128]{2,1,0:T(8,128)S(1)}, f32[4,8,128]{2,1,0:T(8,128)S(1)}, u32[]{:S(2)}, u32[]{:S(2)}) collective-permute-start(f32[4,8,128]{2,1,0:T(8,128)S(1)} %get-tuple-element.28), channel_id=1, source_target_pairs={{0,8},{1,9},{2,10},{3,11},{4,12},{5,13},{6,14},{7,15},{8,0},{9,1},... | collective-permute-start | bytes 49160 | tf_op jit(solution)/shard_map/ppermute | solution.py:556
  10.8 6.2 %collective-permute-start.2 = (f32[6,8,256]{2,1,0:T(8,128)S(1)}, f32[6,8,256]{2,1,0:T(8,128)S(1)}, u32[]{:S(2)}, u32[]{:S(2)}) collective-permute-start(f32[6,8,256]{2,1,0:T(8,128)S(1)} %get-tuple-element.38), channel_id=1, source_target_pairs={{0,1},{1,0},{2,3},{3,2},{4,5},{5,4},{6,7},{7,6},{8,9},{9,8},{10,11... | collective-permute-start | bytes 147464 | tf_op jit(solution)/shard_map/ppermute | solution.py:556
  11.3 7.2 %collective-permute-start.3 = (f32[6,8,256]{2,1,0:T(8,128)S(1)}, f32[6,8,256]{2,1,0:T(8,128)S(1)}, u32[]{:S(2)}, u32[]{:S(2)}) collective-permute-start(f32[6,8,256]{2,1,0:T(8,128)S(1)} %get-tuple-element.39), channel_id=1, source_target_pairs={{0,8},{1,2},{2,1},{3,4},{4,3},{5,6},{6,5},{7,127},{8,0},{9,10},{10... | collective-permute-start | bytes 147464 | tf_op jit(solution)/shard_map/ppermute | solution.py:556

commit v10 on v9

--- a/solution.py
+++ b/solution.py
@@ -117,6 +117,7 @@
             for g in range(8):
                 for ref, value in zip(rows, scaled([x[g] for x in turned])):
                     ref[8 * part + g, :, h * LANES : (h + 1) * LANES] = value
+    put_messages(rows, send_a, send_b)
     get = lambda name, row: field_tiles(rows, name, row)
 
     def advect_block(block, carry):
@@ -127,7 +128,6 @@
         return carry
 
     lax.fori_loop(0, 4, advect_block, 0)
-    put_messages(rows, send_a, send_b)
 
 
 def put_messages(rows, send_a, send_b):
@@ -137,9 +137,8 @@
     first, last = lane < 2, lane >= LANES - 2
 
     def message(top):
-        row = lambda q: jnp.where(top, ROWS - 1 - q, q)
-        part = lambda name, q: field_tiles(rows, name, row(q))
-        outward = jnp.where(jnp.broadcast_to(jnp.where(top, 1, 0), (8, LANES)) == 1, 1.0, -1.0)
+        part = lambda name, q: field_tiles(rows, name, ROWS - 1 - q if top else q)
+        outward = 1.0 if top else -1.0
         c, m, v = [part("c", q) for q in range(3)], [part("m", q) for q in range(3)], [part("v", q) for q in range(2)]
         half = each(lambda x: 0.5 * x, m[1])
         opened = each(jnp.multiply, half, m[0])
@@ -161,26 +160,19 @@
         pair = lambda a, b: each(lambda x, y: jnp.where(low, x, y), a, b)
         return [cell, step, c[0], pair(m[0], rest), pair(v[0], part("sy", 0)), part("k", 0)]
 
-    def store(ref, tiles):
-        for i, tile in enumerate(tiles):
-            for h in range(2):
-                ref[i, :, h * LANES : (h + 1) * LANES] = tile[h]
-
-    even = lat % 2 == 0
-    store(send_a, message(even))
-    folds = lat == lax.axis_size("lat") - 1
-
-    @pl.when(jnp.logical_not(folds))
-    def _():
-        store(send_b, message(jnp.logical_not(even)))
-
-    @pl.when(folds)
-    def _():
-        backward = LANES - 1 - lane
-        flip = lambda x: jnp.take_along_axis(x, backward, axis=1, mode="promise_in_bounds")
-        turned = [[flip(tile[1]), flip(tile[0])] for tile in message(True)]
-        turned[4] = [-x for x in turned[4]]
-        store(send_b, turned)
+    backward = LANES - 1 - lane
+    flip = lambda x: jnp.take_along_axis(x, backward, axis=1, mode="promise_in_bounds")
+    is_even = jnp.broadcast_to(lat % 2, (8, LANES)) == 0
+    folds = jnp.broadcast_to(lat, (8, LANES)) == lax.axis_size("lat") - 1
+    north, south = message(True), message(False)
+    for i, (top, bottom) in enumerate(zip(north, south)):
+        for h in range(2):
+            wide = slice(h * LANES, (h + 1) * LANES)
+            turned = flip(top[1 - h])
+            if i == 4:
+                turned = -turned
+            send_a[i, :, wide] = jnp.where(is_even, top[h], bottom[h])
+            send_b[i, :, wide] = jnp.where(folds, turned, jnp.where(is_even, bottom[h], top[h]))
 
 
 def strip_at(g, which, late, from_far, from_near, own, spare):

time: 20 us -> 19.7 us (0.985)
  Pallas kernels: 9.63 us -> 9.28 us
  starting transfers between devices: 8.63 us -> 8.97 us
  waiting for transfers between devices: 1.57 us -> 1.3 us
    pallas_call x3, Pallas kernels: 6.38 us -> 6.02 us  [call(): pl.pallas_call(kernel, out_shape=[jax.ShapeDtypeStruct(s, F32) for s in s...]
    ppermute x4, starting transfers between devices: 8.63 us -> 8.97 us  [move(): return lax.ppermute(x, ('lon', 'lat'), route)]
    ppermute x4, waiting for transfers between devices: 1.57 us -> 1.3 us  [move(): return lax.ppermute(x, ('lon', 'lat'), route)]
  transfers between devices with their start and end apart: 4 -> 4, of which waited for: 1 -> 1; matrix products, arithmetic and copies ran while one was open for 0% -> 0% of each run, Pallas kernels for 30% -> 28%
where the time goes in v10:
time: 19.7 us; the launch traced here: 19.6 us
  Pallas kernels  9.28 us (47%)
  starting transfers between devices  8.97 us (46%)
  waiting for transfers between devices  1.3 us (7%)
    ppermute x4, starting transfers between devices, move(): return lax.ppermute(x, ('lon', 'lat'), route)  8.97 us
    pallas_call x3, Pallas kernels, call(): pl.pallas_call(kernel, out_shape=[jax.ShapeDtypeStruct(s, F32) for s in s...  6.02 us
    pallas_call x1, Pallas kernels, shards(): pl.pallas_call(pack_kernel, out_shape=[jax.ShapeDtypeStruct(x.shape, x.dt...  2 us
    ppermute x4, waiting for transfers between devices, move(): return lax.ppermute(x, ('lon', 'lat'), route)  1.3 us
    pallas_call x1, Pallas kernels, shards(): pl.pallas_call(rim_kernel, out_shape=jax.ShapeDtypeStruct((8, ROWS, 2 * L...  1.26 us
  transfers between devices with their start and end apart: 4, of which 1 were waited for; matrix products, arithmetic and copies ran while one was open for 0% of the time, Pallas kernels for 28%

profile of v10, /device:TPU:39, one launch (start us, length us, event | category | flops | bytes accessed | tf_op | source)
XLA Modules:
  0.0 19.6 jit_solution(9963643910701928917)
XLA Ops:
  0.0 2.0 %shard_map.55 = (f32[8,64,256]{2,1,0:T(8,128)S(1)}, f32[12,64,256]{2,1,0:T(8,128)S(1)}, f32[8,64,256]{2,1,0:T(8,128)S(1)}, f32[4,64,256]{2,1,0:T(8,128)S(1)}, s3...) custom-call(f32[8,64,256]{2,1,0:T(8,128)} %bitcast.5, ...), custom_call_target="tpu_custom_call" | custom-call | tf_op jit(solution)/shard_map/pallas_call | solution.py:555
  2.0 3.3 %collective-permute-start = (f32[4,8,128]{2,1,0:T(8,128)S(1)}, f32[4,8,128]{2,1,0:T(8,128)S(1)}, u32[]{:S(2)}, u32[]{:S(2)}) collective-permute-start(f32[4,8,128]{2,1,0:T(8,128)S(1)} %get-tuple-element.27), channel_id=1, source_target_pairs={{0,120},{1,121},{2,122},{3,123},{4,124},{5,125},{6,126},{7,127},{8... | collective-permute-start | bytes 49160 | tf_op jit(solution)/shard_map/ppermute | solution.py:548
  5.3 2.3 %collective-permute-start.1 = (f32[4,8,128]{2,1,0:T(8,128)S(1)}, f32[4,8,128]{2,1,0:T(8,128)S(1)}, u32[]{:S(2)}, u32[]{:S(2)}) collective-permute-start(f32[4,8,128]{2,1,0:T(8,128)S(1)} %get-tuple-element.28), channel_id=1, source_target_pairs={{0,8},{1,9},{2,10},{3,11},{4,12},{5,13},{6,14},{7,15},{8,0},{9,1},... | collective-permute-start | bytes 49160 | tf_op jit(solution)/shard_map/ppermute | solution.py:548
  7.6 2.3 %shard_map.56 = (f32[64,8,256]{2,1,0:T(8,128)S(1)}, f32[64,8,256]{2,1,0:T(8,128)S(1)}, f32[64,8,256]{2,1,0:T(8,128)S(1)}, f32[64,8,256]{2,1,0:T(8,128)S(1)}, f32...) custom-call(f32[8,64,256]{2,1,0:T(8,128)S(1)} %get-tuple-element.31.ref, ...), custom_call_target="tpu_custom_call" | custom-call | flops 10000000 | bytes 6000000 | tf_op jit(solution)/shard_map/pallas_call | solution.py:520
  10.0 0.0 collective-permute-done.refs_0_.refs_6_
  10.0 0.0 collective-permute-done.1.refs_1_.refs_7_
  10.0 0.5 %shard_map.57 = (f32[6,8,256]{2,1,0:T(8,128)S(1)}, f32[6,8,256]{2,1,0:T(8,128)S(1)}) custom-call(f32[4,8,128]{2,1,0:T(8,128)S(1)} %collective-permute-done.refs_0_.refs_6_, f32[4,8,128]{2,1,0:T(8,128)S(1)} %collective-permute-done.1.refs_1_.refs_7_, ...), custom_call_target="tpu_custom_call", output_to_operand_aliasing={{0}: (4, {}), {1}: (5, {})} | custom-call | tf_op jit(solution)/shard_map/pallas_call | solution.py:520
  10.5 0.6 %collective-permute-start.2 = (f32[6,8,256]{2,1,0:T(8,128)S(1)}, f32[6,8,256]{2,1,0:T(8,128)S(1)}, u32[]{:S(2)}, u32[]{:S(2)}) collective-permute-start(f32[6,8,256]{2,1,0:T(8,128)S(1)} %get-tuple-element.38), channel_id=1, source_target_pairs={{0,1},{1,0},{2,3},{3,2},{4,5},{5,4},{6,7},{7,6},{8,9},{9,8},{10,11... | collective-permute-start | bytes 147464 | tf_op jit(solution)/shard_map/ppermute | solution.py:548
  11.1 2.8 %collective-permute-start.3 = (f32[6,8,256]{2,1,0:T(8,128)S(1)}, f32[6,8,256]{2,1,0:T(8,128)S(1)}, u32[]{:S(2)}, u32[]{:S(2)}) collective-permute-start(f32[6,8,256]{2,1,0:T(8,128)S(1)} %get-tuple-element.39), channel_id=1, source_target_pairs={{0,8},{1,2},{2,1},{3,4},{4,3},{5,6},{6,5},{7,127},{8,0},{9,10},{10... | collective-permute-start | bytes 147464 | tf_op jit(solution)/shard_map/ppermute | solution.py:548
  13.8 3.2 %shard_map.58 = (f32[64,8,256]{2,1,0:T(8,128)S(1)}, f32[4,8,384]{2,1,0:T(8,128)S(1)}, f32[4,8,8,128]{3,2,1,0:T(8,128)S(1)}) custom-call(f32[64,8,256]{2,1,0:T(8,128)S(1)} %get-tuple-element.40.refs_0_.refs_2_, f32[64,8,256]{2,1,0:T(8,128)S(1)} %get-tuple-element.41.refs_1_.refs_3_, f32[64,8,256]{2,1,0:T(8,128)S(1)} %get-tuple-element.42.refs_2_.refs_4_, ...), custom_call_target="tpu_custom_call" | custom-call | flops 20000000 | bytes 10000000 | tf_op jit(solution)/shard_map/pallas_call | solution.py:520
  17.0 0.0 collective-permute-done.2.refs_0_
  17.0 1.3 %collective-permute-done.3.refs_1_ = f32[6,8,256]{2,1,0:T(8,128)S(1)} collective-permute-done((f32[6,8,256]{2,1,0:T(8,128)S(1)}, f32[6,8,256]{2,1,0:T(8,128)S(1)}, u32[]{:S(2)}, u32[]{:S(2)}) %collective-permute-start.3) | collective-permute-done | bytes 49184 | tf_op jit(solution)/shard_map/ppermute | solution.py:548
  18.3 1.3 %shard_map.59 = f32[8,64,256]{2,1,0:T(8,128)} custom-call(f32[6,8,256]{2,1,0:T(8,128)S(1)} %collective-permute-done.2.refs_0_, f32[6,8,256]{2,1,0:T(8,128)S(1)} %collective-permute-done.3.refs_1_, f32[64,8,256]{2,1,0:T(8,128)S(1)} %get-tuple-element.40.refs_0_.refs_2_, f32[64,8,256]{2,1,0:T(8,128)S(1)} %get-tuple-element.41.refs_1_.refs_3_, ...), custom_call_target="tpu_custom_call" | custom-call | tf_op jit(solution)/shard_map/pallas_call | solution.py:579
Async XLA Ops:
  2.0 8.0 %collective-permute-start = (f32[4,8,128]{2,1,0:T(8,128)S(1)}, f32[4,8,128]{2,1,0:T(8,128)S(1)}, u32[]{:S(2)}, u32[]{:S(2)}) collective-permute-start(f32[4,8,128]{2,1,0:T(8,128)S(1)} %get-tuple-element.27), channel_id=1, source_target_pairs={{0,120},{1,121},{2,122},{3,123},{4,124},{5,125},{6,126},{7,127},{8... | collective-permute-start | bytes 49160 | tf_op jit(solution)/shard_map/ppermute | solution.py:548
  5.3 4.6 %collective-permute-start.1 = (f32[4,8,128]{2,1,0:T(8,128)S(1)}, f32[4,8,128]{2,1,0:T(8,128)S(1)}, u32[]{:S(2)}, u32[]{:S(2)}) collective-permute-start(f32[4,8,128]{2,1,0:T(8,128)S(1)} %get-tuple-element.28), channel_id=1, source_target_pairs={{0,8},{1,9},{2,10},{3,11},{4,12},{5,13},{6,14},{7,15},{8,0},{9,1},... | collective-permute-start | bytes 49160 | tf_op jit(solution)/shard_map/ppermute | solution.py:548
  10.5 6.5 %collective-permute-start.2 = (f32[6,8,256]{2,1,0:T(8,128)S(1)}, f32[6,8,256]{2,1,0:T(8,128)S(1)}, u32[]{:S(2)}, u32[]{:S(2)}) collective-permute-start(f32[6,8,256]{2,1,0:T(8,128)S(1)} %get-tuple-element.38), channel_id=1, source_target_pairs={{0,1},{1,0},{2,3},{3,2},{4,5},{5,4},{6,7},{7,6},{8,9},{9,8},{10,11... | collective-permute-start | bytes 147464 | tf_op jit(solution)/shard_map/ppermute | solution.py:548
  11.1 7.2 %collective-permute-start.3 = (f32[6,8,256]{2,1,0:T(8,128)S(1)}, f32[6,8,256]{2,1,0:T(8,128)S(1)}, u32[]{:S(2)}, u32[]{:S(2)}) collective-permute-start(f32[6,8,256]{2,1,0:T(8,128)S(1)} %get-tuple-element.39), channel_id=1, source_target_pairs={{0,8},{1,2},{2,1},{3,4},{4,3},{5,6},{6,5},{7,127},{8,0},{9,10},{10... | collective-permute-start | bytes 147464 | tf_op jit(solution)/shard_map/ppermute | solution.py:548

commit v11 on v10

--- a/solution.py
+++ b/solution.py
@@ -45,11 +45,12 @@
     return [field_half(rows, name, row, h) for h in range(2)]
 
 
-def row_planes(held, span, h):
+def row_planes(held, span, h, both=True):
     tracer, velocity, slope, kappa, mask = held
     wide = slice(h * LANES, (h + 1) * LANES)
     return [
-        tracer[:, span, wide], velocity[0:8, span, wide], velocity[4:12, span, wide], slope[:, span, wide],
+        tracer[:, span, wide], velocity[0:8, span, wide], velocity[4:12, span, wide],
+        slope[:, span, wide] if both else jnp.concatenate([slope[0:4, span, wide]] * 2, axis=0),
         jnp.concatenate([mask[:, span, wide].astype(F32), kappa[:, span, wide]], axis=0),
     ]
 
@@ -64,14 +65,18 @@
     copies = []
     for chunk in range(CHUNKS):
         span = slice(chunk * ROWS // CHUNKS, (chunk + 1) * ROWS // CHUNKS)
+        ends = [array.shape[0] for array in arrays]
+        ends[2] = 4
         copies.append(
             [
-                pltpu.make_async_copy(array.at[:, span], hold.at[:, span], sems.at[chunk, i])
-                for i, (array, hold) in enumerate(zip(arrays, held))
+                pltpu.make_async_copy(array.at[:end, span], hold.at[:end, span], sems.at[chunk, i])
+                for i, (array, hold, end) in enumerate(zip(arrays, held, ends))
             ]
         )
         for copy in copies[-1]:
             copy.start()
+    northward = pltpu.make_async_copy(arrays[2].at[4:], held[2].at[4:], sems.at[0, 5])
+    northward.start()
     lane, low = lane_of(), low_of()
     inside = lax.broadcasted_iota(jnp.int32, (8, 8, LANES), 2) < 64
     first, second = [None] * 8, [None] * 8
@@ -81,7 +86,7 @@
                 copy.wait()
         span = slice(8 * part, 8 * part + 8)
         rims = []
-        for left, right in zip(*[row_planes(held, span, h) for h in range(2)]):
+        for left, right in zip(*[row_planes(held, span, h, False) for h in range(2)]):
             rims.append(jnp.transpose(jnp.where(inside, left, right), (1, 0, 2)))
         base = 16 * part
         before, half = lane < base, lane < base + 8
@@ -107,6 +112,7 @@
         western = jnp.where(slot < 4, pltpu.roll(west[0], LANES - 4, 1), west[1])
         to_near[pair] = jnp.where(to_east, eastern, western)
         to_far[pair] = jnp.where(to_east, western, eastern)
+    northward.wait()
 
 
 def advect_kernel(*refs):
@@ -195,30 +201,43 @@
     lat = lax.axis_index("lat")
     strip = lambda i, g: strip_at(g, i // 2, i % 2, *sources)
 
-    def beside(g, inner, turn):
+    def beside(g, inner):
         c, mu, vw = strip(0, g), strip(1, g), strip(2, g)
-        m = twice_low(mu)
-        flux_x = zonal_flux([c], [m], [0.5 * m], [twice_high(mu)])
-        step = (c - strip(0, inner)) * (0.5 * m * twice_low(strip(1, inner)))
-        values = [flux_x[0] - minus(flux_x)[0], c, step, jnp.where(low, mu, pltpu.roll(vw, 4, 0))]
-        return [pltpu.roll(x, turn, 1) if turn else x for x in values]
-
-    south, north = beside(0, 1, 0), beside(7, 6, 16)
-
-    def store(source, ref, across, *corners):
-        ref[0, :, :LANES] = source[0, :, :LANES] - jnp.where(lane < 2, pltpu.roll(across, LANES - 10, 1), 0.0)
-        ref[0, :, LANES:] = source[0, :, LANES:] - jnp.where(lane >= LANES - 2, pltpu.roll(across, LANES - 4, 1), 0.0)
-        packed = corners[0]
-        for i in range(1, 3):
-            packed = jnp.where(lane < 16 * i, packed, pltpu.roll(corners[i], 16 * i, 1))
+        shifts = (1, 0, LANES - 1, LANES - 2)
+        moved = lambda x: [pltpu.roll(x, by, 1) if by else x for by in shifts]
+        cells, pairs = moved(c), moved(mu)
+        m = [twice_low(x) for x in pairs]
+        half = [0.5 * x for x in m]
+        steps = [(cells[n + 1] - cells[n]) * (half[n] * m[n + 1]) for n in range(3)]
+        speed = face_speed(twice_high(pairs[1]), twice_high(pairs[2]), half[1] * m[2])
+        flux = face_flux(cells[1], cells[2], speed, *steps)
+        step = (c - strip(0, inner)) * (half[1] * twice_low(strip(1, inner)))
+        return flux, c, step, jnp.where(low, mu, pltpu.roll(vw, 4, 0))
+
+    def placed(values, base, backward):
+        if backward:
+            take = lambda x, at: jnp.take_along_axis(x, (base + at + LANES - lane) & (LANES - 1), axis=1, mode="promise_in_bounds")
+            places = [(3, 2), (9, 8), 13, 29, 45]
+        else:
+            take = lambda x, at: pltpu.roll(x, (at - base) % LANES, 1) if (at - base) % LANES else x
+            places = [(118, 119), (124, 125), 0, 16, 32]
+        across = [take(values[0], at) - take(values[0], before) for at, before in places[:2]]
+        c, step, mv = [take(x, at) for x, at in zip(values[1:], places[2:])]
+        if backward:
+            mv = jnp.where(low, mv, -mv)
+        return across + [jnp.where(lane < 16, c, jnp.where(lane < 32, step, mv))]
+
+    south, north = beside(0, 1), beside(7, 6)
+    south, north, turned = placed(south, 0, False), placed(north, 112, False), placed(north, 112, True)
+
+    def store(source, ref, left, right, packed):
+        ref[0, :, :LANES] = source[0, :, :LANES] - jnp.where(lane < 2, left, 0.0)
+        ref[0, :, LANES:] = source[0, :, LANES:] - jnp.where(lane >= LANES - 2, right, 0.0)
         ref[5, :, :LANES] = jnp.where(low, source[5, :, :LANES], pltpu.roll(packed, 4, 0))
         ref[5, :, LANES:] = jnp.where(low, source[5, :, LANES:], packed)
 
     is_even = jnp.broadcast_to(lat % 2, (8, LANES)) == 0
     folds = jnp.broadcast_to(lat, (8, LANES)) == lax.axis_size("lat") - 1
-    index = jnp.where(lane < 14, 13 - lane, lane)
-    turned = [jnp.take_along_axis(x, index, axis=1, mode="promise_in_bounds") for x in north]
-    turned[3] = jnp.where(low, turned[3], -turned[3])
     store(made[0], send_a, *[jnp.where(is_even, n, s) for n, s in zip(north, south)])
     store(made[1], send_b, *[jnp.where(folds, t, jnp.where(is_even, s, n)) for n, s, t in zip(north, south, turned)])
 
@@ -558,7 +577,7 @@
             + [jax.ShapeDtypeStruct(shape, F32) for shape in [(4, 8, LANES)] * 2 + [side] * 2],
             in_specs=[pl.BlockSpec(memory_space=pltpu.HBM)] * 5,
             out_specs=[VMEM] * 9,
-            scratch_shapes=[pltpu.SemaphoreType.DMA((CHUNKS, 5))],
+            scratch_shapes=[pltpu.SemaphoreType.DMA((CHUNKS, 6))],
             compiler_params=pltpu.CompilerParams(vmem_limit_bytes=LIMIT),
         )(*arrays)
         far_got, near_got = move(to_far, far), move(to_near, near)

time: 19.7 us -> 19.5 us (0.990)
  Pallas kernels: 9.28 us -> 8.97 us
    pallas_call x3, Pallas kernels: 6.02 us -> 5.79 us  [call(): pl.pallas_call(kernel, out_shape=[jax.ShapeDtypeStruct(s, F32) for s in s...]
  transfers between devices with their start and end apart: 4 -> 4, of which waited for: 1 -> 1; matrix products, arithmetic and copies ran while one was open for 0% -> 0% of each run, Pallas kernels for 28% -> 29%
where the time goes in v11:
time: 19.5 us; the launch traced here: 19.3 us
  starting transfers between devices  9 us (46%)
  Pallas kernels  8.97 us (46%)
  waiting for transfers between devices  1.3 us (7%)
    ppermute x4, starting transfers between devices, move(): return lax.ppermute(x, ('lon', 'lat'), route)  9 us
    pallas_call x3, Pallas kernels, call(): pl.pallas_call(kernel, out_shape=[jax.ShapeDtypeStruct(s, F32) for s in s...  5.79 us
    pallas_call x1, Pallas kernels, shards(): pl.pallas_call(pack_kernel, out_shape=[jax.ShapeDtypeStruct(x.shape, x.dt...  1.92 us
    ppermute x4, waiting for transfers between devices, move(): return lax.ppermute(x, ('lon', 'lat'), route)  1.3 us
    pallas_call x1, Pallas kernels, shards(): pl.pallas_call(rim_kernel, out_shape=jax.ShapeDtypeStruct((8, ROWS, 2 * L...  1.26 us
  transfers between devices with their start and end apart: 4, of which 1 were waited for; matrix products, arithmetic and copies ran while one was open for 0% of the time, Pallas kernels for 29%

profile of v11, /device:TPU:39, one launch (start us, length us, event | category | flops | bytes accessed | tf_op | source)
XLA Modules:
  0.0 19.3 jit_solution(18084161863225162313)
XLA Ops:
  0.0 1.9 %shard_map.55 = (f32[8,64,256]{2,1,0:T(8,128)S(1)}, f32[12,64,256]{2,1,0:T(8,128)S(1)}, f32[8,64,256]{2,1,0:T(8,128)S(1)}, f32[4,64,256]{2,1,0:T(8,128)S(1)}, s3...) custom-call(f32[8,64,256]{2,1,0:T(8,128)} %bitcast.5, ...), custom_call_target="tpu_custom_call" | custom-call | tf_op jit(solution)/shard_map/pallas_call | solution.py:574
  1.9 3.3 %collective-permute-start = (f32[4,8,128]{2,1,0:T(8,128)S(1)}, f32[4,8,128]{2,1,0:T(8,128)S(1)}, u32[]{:S(2)}, u32[]{:S(2)}) collective-permute-start(f32[4,8,128]{2,1,0:T(8,128)S(1)} %get-tuple-element.27), channel_id=1, source_target_pairs={{0,120},{1,121},{2,122},{3,123},{4,124},{5,125},{6,126},{7,127},{8... | collective-permute-start | bytes 49160 | tf_op jit(solution)/shard_map/ppermute | solution.py:567
  5.3 2.3 %collective-permute-start.1 = (f32[4,8,128]{2,1,0:T(8,128)S(1)}, f32[4,8,128]{2,1,0:T(8,128)S(1)}, u32[]{:S(2)}, u32[]{:S(2)}) collective-permute-start(f32[4,8,128]{2,1,0:T(8,128)S(1)} %get-tuple-element.28), channel_id=1, source_target_pairs={{0,8},{1,9},{2,10},{3,11},{4,12},{5,13},{6,14},{7,15},{8,0},{9,1},... | collective-permute-start | bytes 49160 | tf_op jit(solution)/shard_map/ppermute | solution.py:567
  7.6 2.3 %shard_map.56 = (f32[64,8,256]{2,1,0:T(8,128)S(1)}, f32[64,8,256]{2,1,0:T(8,128)S(1)}, f32[64,8,256]{2,1,0:T(8,128)S(1)}, f32[64,8,256]{2,1,0:T(8,128)S(1)}, f32...) custom-call(f32[8,64,256]{2,1,0:T(8,128)S(1)} %get-tuple-element.31.ref, ...), custom_call_target="tpu_custom_call" | custom-call | flops 10000000 | bytes 6000000 | tf_op jit(solution)/shard_map/pallas_call | solution.py:539
  9.9 0.0 collective-permute-done.refs_0_.refs_6_
  9.9 0.0 collective-permute-done.1.refs_1_.refs_7_
  9.9 0.3 %shard_map.57 = (f32[6,8,256]{2,1,0:T(8,128)S(1)}, f32[6,8,256]{2,1,0:T(8,128)S(1)}) custom-call(f32[4,8,128]{2,1,0:T(8,128)S(1)} %collective-permute-done.refs_0_.refs_6_, f32[4,8,128]{2,1,0:T(8,128)S(1)} %collective-permute-done.1.refs_1_.refs_7_, ...), custom_call_target="tpu_custom_call", output_to_operand_aliasing={{0}: (4, {}), {1}: (5, {})} | custom-call | tf_op jit(solution)/shard_map/pallas_call | solution.py:539
  10.2 0.6 %collective-permute-start.2 = (f32[6,8,256]{2,1,0:T(8,128)S(1)}, f32[6,8,256]{2,1,0:T(8,128)S(1)}, u32[]{:S(2)}, u32[]{:S(2)}) collective-permute-start(f32[6,8,256]{2,1,0:T(8,128)S(1)} %get-tuple-element.38), channel_id=1, source_target_pairs={{0,1},{1,0},{2,3},{3,2},{4,5},{5,4},{6,7},{7,6},{8,9},{9,8},{10,11... | collective-permute-start | bytes 147464 | tf_op jit(solution)/shard_map/ppermute | solution.py:567
  10.8 2.8 %collective-permute-start.3 = (f32[6,8,256]{2,1,0:T(8,128)S(1)}, f32[6,8,256]{2,1,0:T(8,128)S(1)}, u32[]{:S(2)}, u32[]{:S(2)}) collective-permute-start(f32[6,8,256]{2,1,0:T(8,128)S(1)} %get-tuple-element.39), channel_id=1, source_target_pairs={{0,8},{1,2},{2,1},{3,4},{4,3},{5,6},{6,5},{7,127},{8,0},{9,10},{10... | collective-permute-start | bytes 147464 | tf_op jit(solution)/shard_map/ppermute | solution.py:567
  13.6 3.2 %shard_map.58 = (f32[64,8,256]{2,1,0:T(8,128)S(1)}, f32[4,8,384]{2,1,0:T(8,128)S(1)}, f32[4,8,8,128]{3,2,1,0:T(8,128)S(1)}) custom-call(f32[64,8,256]{2,1,0:T(8,128)S(1)} %get-tuple-element.40.refs_0_.refs_2_, f32[64,8,256]{2,1,0:T(8,128)S(1)} %get-tuple-element.41.refs_1_.refs_3_, f32[64,8,256]{2,1,0:T(8,128)S(1)} %get-tuple-element.42.refs_2_.refs_4_, ...), custom_call_target="tpu_custom_call" | custom-call | flops 20000000 | bytes 10000000 | tf_op jit(solution)/shard_map/pallas_call | solution.py:539
  16.8 0.0 collective-permute-done.2.refs_0_
  16.8 1.3 %collective-permute-done.3.refs_1_ = f32[6,8,256]{2,1,0:T(8,128)S(1)} collective-permute-done((f32[6,8,256]{2,1,0:T(8,128)S(1)}, f32[6,8,256]{2,1,0:T(8,128)S(1)}, u32[]{:S(2)}, u32[]{:S(2)}) %collective-permute-start.3) | collective-permute-done | bytes 49184 | tf_op jit(solution)/shard_map/ppermute | solution.py:567
  18.1 1.3 %shard_map.59 = f32[8,64,256]{2,1,0:T(8,128)} custom-call(f32[6,8,256]{2,1,0:T(8,128)S(1)} %collective-permute-done.2.refs_0_, f32[6,8,256]{2,1,0:T(8,128)S(1)} %collective-permute-done.3.refs_1_, f32[64,8,256]{2,1,0:T(8,128)S(1)} %get-tuple-element.40.refs_0_.refs_2_, f32[64,8,256]{2,1,0:T(8,128)S(1)} %get-tuple-element.41.refs_1_.refs_3_, ...), custom_call_target="tpu_custom_call" | custom-call | tf_op jit(solution)/shard_map/pallas_call | solution.py:598
Async XLA Ops:
  1.9 8.0 %collective-permute-start = (f32[4,8,128]{2,1,0:T(8,128)S(1)}, f32[4,8,128]{2,1,0:T(8,128)S(1)}, u32[]{:S(2)}, u32[]{:S(2)}) collective-permute-start(f32[4,8,128]{2,1,0:T(8,128)S(1)} %get-tuple-element.27), channel_id=1, source_target_pairs={{0,120},{1,121},{2,122},{3,123},{4,124},{5,125},{6,126},{7,127},{8... | collective-permute-start | bytes 49160 | tf_op jit(solution)/shard_map/ppermute | solution.py:567
  5.3 4.6 %collective-permute-start.1 = (f32[4,8,128]{2,1,0:T(8,128)S(1)}, f32[4,8,128]{2,1,0:T(8,128)S(1)}, u32[]{:S(2)}, u32[]{:S(2)}) collective-permute-start(f32[4,8,128]{2,1,0:T(8,128)S(1)} %get-tuple-element.28), channel_id=1, source_target_pairs={{0,8},{1,9},{2,10},{3,11},{4,12},{5,13},{6,14},{7,15},{8,0},{9,1},... | collective-permute-start | bytes 49160 | tf_op jit(solution)/shard_map/ppermute | solution.py:567
  10.2 6.6 %collective-permute-start.2 = (f32[6,8,256]{2,1,0:T(8,128)S(1)}, f32[6,8,256]{2,1,0:T(8,128)S(1)}, u32[]{:S(2)}, u32[]{:S(2)}) collective-permute-start(f32[6,8,256]{2,1,0:T(8,128)S(1)} %get-tuple-element.38), channel_id=1, source_target_pairs={{0,1},{1,0},{2,3},{3,2},{4,5},{5,4},{6,7},{7,6},{8,9},{9,8},{10,11... | collective-permute-start | bytes 147464 | tf_op jit(solution)/shard_map/ppermute | solution.py:567
  10.8 7.2 %collective-permute-start.3 = (f32[6,8,256]{2,1,0:T(8,128)S(1)}, f32[6,8,256]{2,1,0:T(8,128)S(1)}, u32[]{:S(2)}, u32[]{:S(2)}) collective-permute-start(f32[6,8,256]{2,1,0:T(8,128)S(1)} %get-tuple-element.39), channel_id=1, source_target_pairs={{0,8},{1,2},{2,1},{3,4},{4,3},{5,6},{6,5},{7,127},{8,0},{9,10},{10... | collective-permute-start | bytes 147464 | tf_op jit(solution)/shard_map/ppermute | solution.py:567

commit v12 on v11

--- a/solution.py
+++ b/solution.py
@@ -365,25 +365,11 @@
 
 
 def diffuse_rows(get, first, count, beside=None):
-    a = {j: get("a", first + j) for j in range(-1, count + 1)}
-    m = {j: get("m", first + j) for j in range(-1, count + 1)}
-    k = {j: get("k", first + j) for j in range(-1, count + 1)}
-    sy = {j: get("sy", first + j) for j in range(-1, count + 1)}
-    step_z, twice_z = {}, {}
-    for j in range(-1, count + 1):
-        wide = 3 if 0 <= j < count else 2
-        step_z[j] = each(lambda x, o: (below(x) - x) * open_below(o), a[j][:wide], m[j])
-        twice_z[j] = each(lambda x: above(x) + x, step_z[j])
-    step_y, flux_y = {}, {}
-    for j in range(-1, count):
-        opened = each(jnp.multiply, m[j][:2], m[j + 1][:2])
-        step_y[j] = each(lambda x, y, o: (y - x) * o, a[j][:2], a[j + 1][:2], opened)
-        flux_y[j] = each(
-            slope_flux, k[j], k[j + 1], opened, step_y[j], sy[j], sy[j + 1], twice_z[j], twice_z[j + 1]
-        )
+    a, m, k, sy, step_z, twice_z, step_y, flux_y = [{} for _ in range(8)]
     result = []
     last = lane_of() == LANES - 1
-    for j in range(count):
+
+    def row_result(j):
         sx = get("sx", first + j)
         step_x, flux_x = eastward(a[j], m[j], k[j], sx, twice_z[j])
         west = [None, None]
@@ -404,6 +390,20 @@
             return (value + across + (flux_z - above(flux_z))) * marker
 
         result.append(each(finish, a[j][:2], m[j], k[j], sx, sy[j], twice_x, twice_y, step_z[j], total))
+
+    for j in range(-1, count + 1):
+        a[j], m[j], k[j], sy[j] = [get(name, first + j) for name in ("a", "m", "k", "sy")]
+        wide = 3 if 0 <= j < count else 2
+        step_z[j] = each(lambda x, o: (below(x) - x) * open_below(o), a[j][:wide], m[j])
+        twice_z[j] = each(lambda x: above(x) + x, step_z[j])
+        if j >= 0:
+            opened = each(jnp.multiply, m[j - 1][:2], m[j][:2])
+            step_y[j - 1] = each(lambda x, y, o: (y - x) * o, a[j - 1][:2], a[j][:2], opened)
+            flux_y[j - 1] = each(
+                slope_flux, k[j - 1], k[j], opened, step_y[j - 1], sy[j - 1], sy[j], twice_z[j - 1], twice_z[j]
+            )
+        if j >= 1:
+            row_result(j - 1)
     return result
 
 

time: 19.5 us -> 19.5 us (level)
  Pallas kernels: 8.97 us -> 8.69 us
  waiting for transfers between devices: 1.3 us -> 1.58 us
    ppermute x4, waiting for transfers between devices: 1.3 us -> 1.58 us  [move(): return lax.ppermute(x, ('lon', 'lat'), route)]
    pallas_call x3, Pallas kernels: 5.79 us -> 5.51 us  [call(): pl.pallas_call(kernel, out_shape=[jax.ShapeDtypeStruct(s, F32) for s in s...]
  transfers between devices with their start and end apart: 4 -> 4, of which waited for: 1 -> 1; matrix products, arithmetic and copies ran while one was open for 0% -> 0% of each run, Pallas kernels for 29% -> 27%
where the time goes in v12:
time: 19.5 us; the launch traced here: 19.3 us
  starting transfers between devices  9 us (46%)
  Pallas kernels  8.69 us (45%)
  waiting for transfers between devices  1.58 us (8%)
    ppermute x4, starting transfers between devices, move(): return lax.ppermute(x, ('lon', 'lat'), route)  9 us
    pallas_call x3, Pallas kernels, call(): pl.pallas_call(kernel, out_shape=[jax.ShapeDtypeStruct(s, F32) for s in s...  5.51 us
    pallas_call x1, Pallas kernels, shards(): pl.pallas_call(pack_kernel, out_shape=[jax.ShapeDtypeStruct(x.shape, x.dt...  1.92 us
    ppermute x4, waiting for transfers between devices, move(): return lax.ppermute(x, ('lon', 'lat'), route)  1.58 us
    pallas_call x1, Pallas kernels, shards(): pl.pallas_call(rim_kernel, out_shape=jax.ShapeDtypeStruct((8, ROWS, 2 * L...  1.26 us
  transfers between devices with their start and end apart: 4, of which 1 were waited for; matrix products, arithmetic and copies ran while one was open for 0% of the time, Pallas kernels for 27%

profile of v12, /device:TPU:39, one launch (start us, length us, event | category | flops | bytes accessed | tf_op | source)
XLA Modules:
  0.0 19.3 jit_solution(12624659990265001211)
XLA Ops:
  0.0 1.9 %shard_map.55 = (f32[8,64,256]{2,1,0:T(8,128)S(1)}, f32[12,64,256]{2,1,0:T(8,128)S(1)}, f32[8,64,256]{2,1,0:T(8,128)S(1)}, f32[4,64,256]{2,1,0:T(8,128)S(1)}, s3...) custom-call(f32[8,64,256]{2,1,0:T(8,128)} %bitcast.5, ...), custom_call_target="tpu_custom_call" | custom-call | tf_op jit(solution)/shard_map/pallas_call | solution.py:574
  1.9 3.3 %collective-permute-start = (f32[4,8,128]{2,1,0:T(8,128)S(1)}, f32[4,8,128]{2,1,0:T(8,128)S(1)}, u32[]{:S(2)}, u32[]{:S(2)}) collective-permute-start(f32[4,8,128]{2,1,0:T(8,128)S(1)} %get-tuple-element.27), channel_id=1, source_target_pairs={{0,120},{1,121},{2,122},{3,123},{4,124},{5,125},{6,126},{7,127},{8... | collective-permute-start | bytes 49160 | tf_op jit(solution)/shard_map/ppermute | solution.py:567
  5.3 2.3 %collective-permute-start.1 = (f32[4,8,128]{2,1,0:T(8,128)S(1)}, f32[4,8,128]{2,1,0:T(8,128)S(1)}, u32[]{:S(2)}, u32[]{:S(2)}) collective-permute-start(f32[4,8,128]{2,1,0:T(8,128)S(1)} %get-tuple-element.28), channel_id=1, source_target_pairs={{0,8},{1,9},{2,10},{3,11},{4,12},{5,13},{6,14},{7,15},{8,0},{9,1},... | collective-permute-start | bytes 49160 | tf_op jit(solution)/shard_map/ppermute | solution.py:567
  7.6 2.3 %shard_map.56 = (f32[64,8,256]{2,1,0:T(8,128)S(1)}, f32[64,8,256]{2,1,0:T(8,128)S(1)}, f32[64,8,256]{2,1,0:T(8,128)S(1)}, f32[64,8,256]{2,1,0:T(8,128)S(1)}, f32...) custom-call(f32[8,64,256]{2,1,0:T(8,128)S(1)} %get-tuple-element.31.ref, ...), custom_call_target="tpu_custom_call" | custom-call | flops 10000000 | bytes 6000000 | tf_op jit(solution)/shard_map/pallas_call | solution.py:539
  9.9 0.0 collective-permute-done.refs_0_.refs_6_
  9.9 0.0 collective-permute-done.1.refs_1_.refs_7_
  9.9 0.3 %shard_map.57 = (f32[6,8,256]{2,1,0:T(8,128)S(1)}, f32[6,8,256]{2,1,0:T(8,128)S(1)}) custom-call(f32[4,8,128]{2,1,0:T(8,128)S(1)} %collective-permute-done.refs_0_.refs_6_, f32[4,8,128]{2,1,0:T(8,128)S(1)} %collective-permute-done.1.refs_1_.refs_7_, ...), custom_call_target="tpu_custom_call", output_to_operand_aliasing={{0}: (4, {}), {1}: (5, {})} | custom-call | tf_op jit(solution)/shard_map/pallas_call | solution.py:539
  10.2 0.6 %collective-permute-start.2 = (f32[6,8,256]{2,1,0:T(8,128)S(1)}, f32[6,8,256]{2,1,0:T(8,128)S(1)}, u32[]{:S(2)}, u32[]{:S(2)}) collective-permute-start(f32[6,8,256]{2,1,0:T(8,128)S(1)} %get-tuple-element.38), channel_id=1, source_target_pairs={{0,1},{1,0},{2,3},{3,2},{4,5},{5,4},{6,7},{7,6},{8,9},{9,8},{10,11... | collective-permute-start | bytes 147464 | tf_op jit(solution)/shard_map/ppermute | solution.py:567
  10.8 2.8 %collective-permute-start.3 = (f32[6,8,256]{2,1,0:T(8,128)S(1)}, f32[6,8,256]{2,1,0:T(8,128)S(1)}, u32[]{:S(2)}, u32[]{:S(2)}) collective-permute-start(f32[6,8,256]{2,1,0:T(8,128)S(1)} %get-tuple-element.39), channel_id=1, source_target_pairs={{0,8},{1,2},{2,1},{3,4},{4,3},{5,6},{6,5},{7,127},{8,0},{9,10},{10... | collective-permute-start | bytes 147464 | tf_op jit(solution)/shard_map/ppermute | solution.py:567
  13.6 2.9 %shard_map.58 = (f32[64,8,256]{2,1,0:T(8,128)S(1)}, f32[4,8,384]{2,1,0:T(8,128)S(1)}, f32[4,8,8,128]{3,2,1,0:T(8,128)S(1)}) custom-call(f32[64,8,256]{2,1,0:T(8,128)S(1)} %get-tuple-element.40.refs_0_.refs_2_, f32[64,8,256]{2,1,0:T(8,128)S(1)} %get-tuple-element.41.refs_1_.refs_3_, f32[64,8,256]{2,1,0:T(8,128)S(1)} %get-tuple-element.42.refs_2_.refs_4_, ...), custom_call_target="tpu_custom_call" | custom-call | flops 20000000 | bytes 10000000 | tf_op jit(solution)/shard_map/pallas_call | solution.py:539
  16.5 0.0 collective-permute-done.2.refs_0_
  16.5 1.6 %collective-permute-done.3.refs_1_ = f32[6,8,256]{2,1,0:T(8,128)S(1)} collective-permute-done((f32[6,8,256]{2,1,0:T(8,128)S(1)}, f32[6,8,256]{2,1,0:T(8,128)S(1)}, u32[]{:S(2)}, u32[]{:S(2)}) %collective-permute-start.3) | collective-permute-done | bytes 49184 | tf_op jit(solution)/shard_map/ppermute | solution.py:567
  18.1 1.3 %shard_map.59 = f32[8,64,256]{2,1,0:T(8,128)} custom-call(f32[6,8,256]{2,1,0:T(8,128)S(1)} %collective-permute-done.2.refs_0_, f32[6,8,256]{2,1,0:T(8,128)S(1)} %collective-permute-done.3.refs_1_, f32[64,8,256]{2,1,0:T(8,128)S(1)} %get-tuple-element.40.refs_0_.refs_2_, f32[64,8,256]{2,1,0:T(8,128)S(1)} %get-tuple-element.41.refs_1_.refs_3_, ...), custom_call_target="tpu_custom_call" | custom-call | tf_op jit(solution)/shard_map/pallas_call | solution.py:598
Async XLA Ops:
  1.9 8.0 %collective-permute-start = (f32[4,8,128]{2,1,0:T(8,128)S(1)}, f32[4,8,128]{2,1,0:T(8,128)S(1)}, u32[]{:S(2)}, u32[]{:S(2)}) collective-permute-start(f32[4,8,128]{2,1,0:T(8,128)S(1)} %get-tuple-element.27), channel_id=1, source_target_pairs={{0,120},{1,121},{2,122},{3,123},{4,124},{5,125},{6,126},{7,127},{8... | collective-permute-start | bytes 49160 | tf_op jit(solution)/shard_map/ppermute | solution.py:567
  5.3 4.6 %collective-permute-start.1 = (f32[4,8,128]{2,1,0:T(8,128)S(1)}, f32[4,8,128]{2,1,0:T(8,128)S(1)}, u32[]{:S(2)}, u32[]{:S(2)}) collective-permute-start(f32[4,8,128]{2,1,0:T(8,128)S(1)} %get-tuple-element.28), channel_id=1, source_target_pairs={{0,8},{1,9},{2,10},{3,11},{4,12},{5,13},{6,14},{7,15},{8,0},{9,1},... | collective-permute-start | bytes 49160 | tf_op jit(solution)/shard_map/ppermute | solution.py:567
  10.2 6.3 %collective-permute-start.2 = (f32[6,8,256]{2,1,0:T(8,128)S(1)}, f32[6,8,256]{2,1,0:T(8,128)S(1)}, u32[]{:S(2)}, u32[]{:S(2)}) collective-permute-start(f32[6,8,256]{2,1,0:T(8,128)S(1)} %get-tuple-element.38), channel_id=1, source_target_pairs={{0,1},{1,0},{2,3},{3,2},{4,5},{5,4},{6,7},{7,6},{8,9},{9,8},{10,11... | collective-permute-start | bytes 147464 | tf_op jit(solution)/shard_map/ppermute | solution.py:567
  10.8 7.2 %collective-permute-start.3 = (f32[6,8,256]{2,1,0:T(8,128)S(1)}, f32[6,8,256]{2,1,0:T(8,128)S(1)}, u32[]{:S(2)}, u32[]{:S(2)}) collective-permute-start(f32[6,8,256]{2,1,0:T(8,128)S(1)} %get-tuple-element.39), channel_id=1, source_target_pairs={{0,8},{1,2},{2,1},{3,4},{4,3},{5,6},{6,5},{7,127},{8,0},{9,10},{10... | collective-permute-start | bytes 147464 | tf_op jit(solution)/shard_map/ppermute | solution.py:567

commit v13 on v12

--- a/solution.py
+++ b/solution.py
@@ -121,8 +121,9 @@
         for h in range(2):
             turned = [jnp.transpose(x, (1, 0, 2)) for x in row_planes(held, slice(8 * part, 8 * part + 8), h)]
             for g in range(8):
-                for ref, value in zip(rows, scaled([x[g] for x in turned])):
-                    ref[8 * part + g, :, h * LANES : (h + 1) * LANES] = value
+                for i, (ref, value) in enumerate(zip(rows, scaled([x[g] for x in turned]))):
+                    if i != 3 or part in (0, 7):
+                        ref[8 * part + g, :, h * LANES : (h + 1) * LANES] = value
     put_messages(rows, send_a, send_b)
     get = lambda name, row: field_tiles(rows, name, row)
 
@@ -412,8 +413,14 @@
 
 
 def interior_kernel(*refs):
-    rows, advected, sources = refs[:5], refs[5], refs[6:10]
-    out, kept, strips, narrow = refs[10:]
+    rows, advected, sources, slope = refs[:5], refs[5], refs[6:10], refs[10]
+    out, kept, strips, slope_rows, narrow = refs[11:]
+    rows = rows[:3] + (slope_rows,) + rows[4:]
+    for part in range(8):
+        for h in range(2):
+            wide = slice(h * LANES, (h + 1) * LANES)
+            turned = jnp.transpose(slope[:, 8 * part : 8 * part + 8, wide], (1, 0, 2))
+            slope_rows[8 * part : 8 * part + 8, :, wide] = turned * 0.125
     lane = lane_of()
     near_east, near_west = lane >= LANES - 2, lane < 2
 
@@ -590,8 +597,9 @@
             input_output_aliases={4: 0, 5: 1},
         )
         got_a, got_b = move(send_a, pair_a), move(send_b, pair_b)
-        inner, kept, strips = call(
-            interior_kernel, [full, (4, 8, 3 * LANES), (4,) + side], *rows, advected, far_got, near_got, own, spare,
+        inner, kept, strips, rows[3] = call(
+            interior_kernel, [full, (4, 8, 3 * LANES), (4,) + side, full],
+            *rows, advected, far_got, near_got, own, spare, held[2],
             scratch_shapes=[pltpu.VMEM((3,) + side, F32)],
             cost_estimate=pl.CostEstimate(flops=2 * 10**7, bytes_accessed=10**7, transcendentals=0),
         )

time: 19.5 us -> 19.3 us (0.990)
  no operation moved by 1% of the time
where the time goes in v13:
time: 19.3 us; the launch traced here: 19.2 us
  starting transfers between devices  9.15 us (47%)
  Pallas kernels  8.54 us (44%)
  waiting for transfers between devices  1.42 us (7%)
    ppermute x4, starting transfers between devices, move(): return lax.ppermute(x, ('lon', 'lat'), route)  9.15 us
    pallas_call x3, Pallas kernels, call(): pl.pallas_call(kernel, out_shape=[jax.ShapeDtypeStruct(s, F32) for s in s...  5.36 us
    pallas_call x1, Pallas kernels, shards(): pl.pallas_call(pack_kernel, out_shape=[jax.ShapeDtypeStruct(x.shape, x.dt...  1.92 us
    ppermute x4, waiting for transfers between devices, move(): return lax.ppermute(x, ('lon', 'lat'), route)  1.42 us
    pallas_call x1, Pallas kernels, shards(): pl.pallas_call(rim_kernel, out_shape=jax.ShapeDtypeStruct((8, ROWS, 2 * L...  1.26 us
  transfers between devices with their start and end apart: 4, of which 1 were waited for; matrix products, arithmetic and copies ran while one was open for 0% of the time, Pallas kernels for 27%

profile of v13, /device:TPU:39, one launch (start us, length us, event | category | flops | bytes accessed | tf_op | source)
XLA Modules:
  0.0 19.2 jit_solution(17438945619090662381)
XLA Ops:
  0.0 1.9 %shard_map.55 = (f32[8,64,256]{2,1,0:T(8,128)S(1)}, f32[12,64,256]{2,1,0:T(8,128)S(1)}, f32[8,64,256]{2,1,0:T(8,128)S(1)}, f32[4,64,256]{2,1,0:T(8,128)S(1)}, s3...) custom-call(f32[8,64,256]{2,1,0:T(8,128)} %bitcast.5, ...), custom_call_target="tpu_custom_call" | custom-call | tf_op jit(solution)/shard_map/pallas_call | solution.py:581
  1.9 3.3 %collective-permute-start = (f32[4,8,128]{2,1,0:T(8,128)S(1)}, f32[4,8,128]{2,1,0:T(8,128)S(1)}, u32[]{:S(2)}, u32[]{:S(2)}) collective-permute-start(f32[4,8,128]{2,1,0:T(8,128)S(1)} %get-tuple-element.28), channel_id=1, source_target_pairs={{0,120},{1,121},{2,122},{3,123},{4,124},{5,125},{6,126},{7,127},{8... | collective-permute-start | bytes 49160 | tf_op jit(solution)/shard_map/ppermute | solution.py:574
  5.3 2.3 %collective-permute-start.1 = (f32[4,8,128]{2,1,0:T(8,128)S(1)}, f32[4,8,128]{2,1,0:T(8,128)S(1)}, u32[]{:S(2)}, u32[]{:S(2)}) collective-permute-start(f32[4,8,128]{2,1,0:T(8,128)S(1)} %get-tuple-element.29), channel_id=1, source_target_pairs={{0,8},{1,9},{2,10},{3,11},{4,12},{5,13},{6,14},{7,15},{8,0},{9,1},... | collective-permute-start | bytes 49160 | tf_op jit(solution)/shard_map/ppermute | solution.py:574
  7.6 2.2 %shard_map.56 = (f32[64,8,256]{2,1,0:T(8,128)S(1)}, f32[64,8,256]{2,1,0:T(8,128)S(1)}, f32[64,8,256]{2,1,0:T(8,128)S(1)}, f32[64,8,256]{2,1,0:T(8,128)S(1)}, f32...) custom-call(f32[8,64,256]{2,1,0:T(8,128)S(1)} %get-tuple-element.32.ref, ...), custom_call_target="tpu_custom_call" | custom-call | flops 10000000 | bytes 6000000 | tf_op jit(solution)/shard_map/pallas_call | solution.py:546
  9.7 0.0 collective-permute-done.refs_0_.refs_6_
  9.7 0.0 collective-permute-done.1.refs_1_.refs_7_
  9.8 0.3 %shard_map.57 = (f32[6,8,256]{2,1,0:T(8,128)S(1)}, f32[6,8,256]{2,1,0:T(8,128)S(1)}) custom-call(f32[4,8,128]{2,1,0:T(8,128)S(1)} %collective-permute-done.refs_0_.refs_6_, f32[4,8,128]{2,1,0:T(8,128)S(1)} %collective-permute-done.1.refs_1_.refs_7_, ...), custom_call_target="tpu_custom_call", output_to_operand_aliasing={{0}: (4, {}), {1}: (5, {})} | custom-call | tf_op jit(solution)/shard_map/pallas_call | solution.py:546
  10.0 0.6 %collective-permute-start.2 = (f32[6,8,256]{2,1,0:T(8,128)S(1)}, f32[6,8,256]{2,1,0:T(8,128)S(1)}, u32[]{:S(2)}, u32[]{:S(2)}) collective-permute-start(f32[6,8,256]{2,1,0:T(8,128)S(1)} %get-tuple-element.39), channel_id=1, source_target_pairs={{0,1},{1,0},{2,3},{3,2},{4,5},{5,4},{6,7},{7,6},{8,9},{9,8},{10,11... | collective-permute-start | bytes 147464 | tf_op jit(solution)/shard_map/ppermute | solution.py:574
  10.7 2.9 %collective-permute-start.3 = (f32[6,8,256]{2,1,0:T(8,128)S(1)}, f32[6,8,256]{2,1,0:T(8,128)S(1)}, u32[]{:S(2)}, u32[]{:S(2)}) collective-permute-start(f32[6,8,256]{2,1,0:T(8,128)S(1)} %get-tuple-element.40), channel_id=1, source_target_pairs={{0,8},{1,2},{2,1},{3,4},{4,3},{5,6},{6,5},{7,127},{8,0},{9,10},{10... | collective-permute-start | bytes 147464 | tf_op jit(solution)/shard_map/ppermute | solution.py:574
  13.6 2.9 %shard_map.58 = (f32[64,8,256]{2,1,0:T(8,128)S(1)}, f32[4,8,384]{2,1,0:T(8,128)S(1)}, f32[4,8,8,128]{3,2,1,0:T(8,128)S(1)}, f32[64,8,256]{2,1,0:T(8,128)S(1)}) custom-call(f32[64,8,256]{2,1,0:T(8,128)S(1)} %get-tuple-element.41.refs_0_.refs_2_, f32[64,8,256]{2,1,0:T(8,128)S(1)} %get-tuple-element.42.refs_1_.refs_3_, ...), custom_call_target="tpu_custom_call" | custom-call | flops 20000000 | bytes 10000000 | tf_op jit(solution)/shard_map/pallas_call | solution.py:546
  16.5 0.0 collective-permute-done.2.refs_0_
  16.5 1.4 %collective-permute-done.3.refs_1_ = f32[6,8,256]{2,1,0:T(8,128)S(1)} collective-permute-done((f32[6,8,256]{2,1,0:T(8,128)S(1)}, f32[6,8,256]{2,1,0:T(8,128)S(1)}, u32[]{:S(2)}, u32[]{:S(2)}) %collective-permute-start.3) | collective-permute-done | bytes 49184 | tf_op jit(solution)/shard_map/ppermute | solution.py:574
  17.9 1.3 %shard_map.59 = f32[8,64,256]{2,1,0:T(8,128)} custom-call(f32[6,8,256]{2,1,0:T(8,128)S(1)} %collective-permute-done.2.refs_0_, f32[6,8,256]{2,1,0:T(8,128)S(1)} %collective-permute-done.3.refs_1_, f32[64,8,256]{2,1,0:T(8,128)S(1)} %get-tuple-element.41.refs_0_.refs_2_, f32[64,8,256]{2,1,0:T(8,128)S(1)} %get-tuple-element.42.refs_1_.refs_3_, ...), custom_call_target="tpu_custom_call" | custom-call | tf_op jit(solution)/shard_map/pallas_call | solution.py:606
Async XLA Ops:
  1.9 7.8 %collective-permute-start = (f32[4,8,128]{2,1,0:T(8,128)S(1)}, f32[4,8,128]{2,1,0:T(8,128)S(1)}, u32[]{:S(2)}, u32[]{:S(2)}) collective-permute-start(f32[4,8,128]{2,1,0:T(8,128)S(1)} %get-tuple-element.28), channel_id=1, source_target_pairs={{0,120},{1,121},{2,122},{3,123},{4,124},{5,125},{6,126},{7,127},{8... | collective-permute-start | bytes 49160 | tf_op jit(solution)/shard_map/ppermute | solution.py:574
  5.3 4.5 %collective-permute-start.1 = (f32[4,8,128]{2,1,0:T(8,128)S(1)}, f32[4,8,128]{2,1,0:T(8,128)S(1)}, u32[]{:S(2)}, u32[]{:S(2)}) collective-permute-start(f32[4,8,128]{2,1,0:T(8,128)S(1)} %get-tuple-element.29), channel_id=1, source_target_pairs={{0,8},{1,9},{2,10},{3,11},{4,12},{5,13},{6,14},{7,15},{8,0},{9,1},... | collective-permute-start | bytes 49160 | tf_op jit(solution)/shard_map/ppermute | solution.py:574
  10.0 6.5 %collective-permute-start.2 = (f32[6,8,256]{2,1,0:T(8,128)S(1)}, f32[6,8,256]{2,1,0:T(8,128)S(1)}, u32[]{:S(2)}, u32[]{:S(2)}) collective-permute-start(f32[6,8,256]{2,1,0:T(8,128)S(1)} %get-tuple-element.39), channel_id=1, source_target_pairs={{0,1},{1,0},{2,3},{3,2},{4,5},{5,4},{6,7},{7,6},{8,9},{9,8},{10,11... | collective-permute-start | bytes 147464 | tf_op jit(solution)/shard_map/ppermute | solution.py:574
  10.7 7.2 %collective-permute-start.3 = (f32[6,8,256]{2,1,0:T(8,128)S(1)}, f32[6,8,256]{2,1,0:T(8,128)S(1)}, u32[]{:S(2)}, u32[]{:S(2)}) collective-permute-start(f32[6,8,256]{2,1,0:T(8,128)S(1)} %get-tuple-element.40), channel_id=1, source_target_pairs={{0,8},{1,2},{2,1},{3,4},{4,3},{5,6},{6,5},{7,127},{8,0},{9,10},{10... | collective-permute-start | bytes 147464 | tf_op jit(solution)/shard_map/ppermute | solution.py:574

commit v14 on v12

--- a/solution.py
+++ b/solution.py
@@ -34,8 +34,8 @@
 
 def field_half(rows, name, row, h):
     which, turn = {
-        "u": (1, twice_low), "v": (1, twice_high), "w": (2, twice_high),
-        "sx": (3, twice_low), "sy": (3, twice_high), "m": (4, twice_low), "k": (4, twice_high),
+        "u": (1, twice_low), "v": (1, twice_high), "w": (2, twice_low),
+        "sx": (3, twice_low), "sy": (3, twice_high), "m": (2, twice_high), "k": (4, None),
     }.get(name, (0, None))
     value = rows[which][row, :, h * LANES : (h + 1) * LANES]
     return turn(value) if turn else value
@@ -115,14 +115,24 @@
     northward.wait()
 
 
+def field_planes(held, span, h):
+    tracer, velocity, slope, kappa, mask = held
+    wide = slice(h * LANES, (h + 1) * LANES)
+    return [
+        tracer[:, span, wide], velocity[0:8, span, wide],
+        jnp.concatenate([velocity[8:12, span, wide], mask[:, span, wide].astype(F32)], axis=0),
+        slope[:, span, wide] * 0.125, jnp.concatenate([kappa[:, span, wide] * 0.5] * 2, axis=0),
+    ]
+
+
 def advect_kernel(*refs):
     held, rows, advected, send_a, send_b = refs[:5], refs[5:10], refs[10], refs[11], refs[12]
     for part in range(8):
         for h in range(2):
-            turned = [jnp.transpose(x, (1, 0, 2)) for x in row_planes(held, slice(8 * part, 8 * part + 8), h)]
-            for g in range(8):
-                for ref, value in zip(rows, scaled([x[g] for x in turned])):
-                    ref[8 * part + g, :, h * LANES : (h + 1) * LANES] = value
+            span = slice(8 * part, 8 * part + 8)
+            for i, x in enumerate(field_planes(held, span, h)):
+                if i < 3 or part in (0, 7):
+                    rows[i][span, :, h * LANES : (h + 1) * LANES] = jnp.transpose(x, (1, 0, 2))
     put_messages(rows, send_a, send_b)
     get = lambda name, row: field_tiles(rows, name, row)
 
@@ -412,8 +422,15 @@
 
 
 def interior_kernel(*refs):
-    rows, advected, sources = refs[:5], refs[5], refs[6:10]
-    out, kept, strips, narrow = refs[10:]
+    rows, advected, sources, slope, kappa = refs[:5], refs[5], refs[6:10], refs[10], refs[11]
+    out, kept, strips, slope_rows, kappa_rows, narrow = refs[12:]
+    rows = rows[:3] + (slope_rows, kappa_rows)
+    for part in range(8):
+        for h in range(2):
+            span, wide = slice(8 * part, 8 * part + 8), slice(h * LANES, (h + 1) * LANES)
+            slope_rows[span, :, wide] = jnp.transpose(slope[:, span, wide] * 0.125, (1, 0, 2))
+            twice = jnp.concatenate([kappa[:, span, wide] * 0.5] * 2, axis=0)
+            kappa_rows[span, :, wide] = jnp.transpose(twice, (1, 0, 2))
     lane = lane_of()
     near_east, near_west = lane >= LANES - 2, lane < 2
 
@@ -590,8 +607,9 @@
             input_output_aliases={4: 0, 5: 1},
         )
         got_a, got_b = move(send_a, pair_a), move(send_b, pair_b)
-        inner, kept, strips = call(
-            interior_kernel, [full, (4, 8, 3 * LANES), (4,) + side], *rows, advected, far_got, near_got, own, spare,
+        inner, kept, strips, rows[3], rows[4] = call(
+            interior_kernel, [full, (4, 8, 3 * LANES), (4,) + side, full, full],
+            *rows, advected, far_got, near_got, own, spare, held[2], held[3],
             scratch_shapes=[pltpu.VMEM((3,) + side, F32)],
             cost_estimate=pl.CostEstimate(flops=2 * 10**7, bytes_accessed=10**7, transcendentals=0),
         )

time: 19.5 us -> 19.3 us (0.990)
  waiting for transfers between devices: 1.58 us -> 1.3 us
  starting transfers between devices: 9 us -> 9.21 us
    ppermute x4, waiting for transfers between devices: 1.58 us -> 1.3 us  [move(): return lax.ppermute(x, ('lon', 'lat'), route)]
    ppermute x4, starting transfers between devices: 9 us -> 9.21 us  [move(): return lax.ppermute(x, ('lon', 'lat'), route)]
where the time goes in v14:
time: 19.3 us; the launch traced here: 19.1 us
  starting transfers between devices  9.21 us (48%)
  Pallas kernels  8.55 us (44%)
  waiting for transfers between devices  1.3 us (7%)
    ppermute x4, starting transfers between devices, move(): return lax.ppermute(x, ('lon', 'lat'), route)  9.21 us
    pallas_call x3, Pallas kernels, call(): pl.pallas_call(kernel, out_shape=[jax.ShapeDtypeStruct(s, F32) for s in s...  5.37 us
    pallas_call x1, Pallas kernels, shards(): pl.pallas_call(pack_kernel, out_shape=[jax.ShapeDtypeStruct(x.shape, x.dt...  1.92 us
    ppermute x4, waiting for transfers between devices, move(): return lax.ppermute(x, ('lon', 'lat'), route)  1.3 us
    pallas_call x1, Pallas kernels, shards(): pl.pallas_call(rim_kernel, out_shape=jax.ShapeDtypeStruct((8, ROWS, 2 * L...  1.26 us
  transfers between devices with their start and end apart: 4, of which 1 were waited for; matrix products, arithmetic and copies ran while one was open for 0% of the time, Pallas kernels for 27%

profile of v14, /device:TPU:39, one launch (start us, length us, event | category | flops | bytes accessed | tf_op | source)
XLA Modules:
  0.0 19.1 jit_solution(12658547801588010023)
XLA Ops:
  0.0 1.9 %shard_map.55 = (f32[8,64,256]{2,1,0:T(8,128)S(1)}, f32[12,64,256]{2,1,0:T(8,128)S(1)}, f32[8,64,256]{2,1,0:T(8,128)S(1)}, f32[4,64,256]{2,1,0:T(8,128)S(1)}, s3...) custom-call(f32[8,64,256]{2,1,0:T(8,128)} %bitcast.5, ...), custom_call_target="tpu_custom_call" | custom-call | tf_op jit(solution)/shard_map/pallas_call | solution.py:591
  1.9 3.3 %collective-permute-start = (f32[4,8,128]{2,1,0:T(8,128)S(1)}, f32[4,8,128]{2,1,0:T(8,128)S(1)}, u32[]{:S(2)}, u32[]{:S(2)}) collective-permute-start(f32[4,8,128]{2,1,0:T(8,128)S(1)} %get-tuple-element.29), channel_id=1, source_target_pairs={{0,120},{1,121},{2,122},{3,123},{4,124},{5,125},{6,126},{7,127},{8... | collective-permute-start | bytes 49160 | tf_op jit(solution)/shard_map/ppermute | solution.py:584
  5.3 2.3 %collective-permute-start.1 = (f32[4,8,128]{2,1,0:T(8,128)S(1)}, f32[4,8,128]{2,1,0:T(8,128)S(1)}, u32[]{:S(2)}, u32[]{:S(2)}) collective-permute-start(f32[4,8,128]{2,1,0:T(8,128)S(1)} %get-tuple-element.30), channel_id=1, source_target_pairs={{0,8},{1,9},{2,10},{3,11},{4,12},{5,13},{6,14},{7,15},{8,0},{9,1},... | collective-permute-start | bytes 49160 | tf_op jit(solution)/shard_map/ppermute | solution.py:584
  7.6 2.1 %shard_map.56 = (f32[64,8,256]{2,1,0:T(8,128)S(1)}, f32[64,8,256]{2,1,0:T(8,128)S(1)}, f32[64,8,256]{2,1,0:T(8,128)S(1)}, f32[64,8,256]{2,1,0:T(8,128)S(1)}, f32...) custom-call(f32[8,64,256]{2,1,0:T(8,128)S(1)} %get-tuple-element.33.ref, ...), custom_call_target="tpu_custom_call" | custom-call | flops 10000000 | bytes 6000000 | tf_op jit(solution)/shard_map/pallas_call | solution.py:556
  9.7 0.0 collective-permute-done.refs_0_.refs_6_
  9.7 0.0 collective-permute-done.1.refs_1_.refs_7_
  9.7 0.3 %shard_map.57 = (f32[6,8,256]{2,1,0:T(8,128)S(1)}, f32[6,8,256]{2,1,0:T(8,128)S(1)}) custom-call(f32[4,8,128]{2,1,0:T(8,128)S(1)} %collective-permute-done.refs_0_.refs_6_, f32[4,8,128]{2,1,0:T(8,128)S(1)} %collective-permute-done.1.refs_1_.refs_7_, ...), custom_call_target="tpu_custom_call", output_to_operand_aliasing={{0}: (4, {}), {1}: (5, {})} | custom-call | tf_op jit(solution)/shard_map/pallas_call | solution.py:556
  10.0 0.6 %collective-permute-start.2 = (f32[6,8,256]{2,1,0:T(8,128)S(1)}, f32[6,8,256]{2,1,0:T(8,128)S(1)}, u32[]{:S(2)}, u32[]{:S(2)}) collective-permute-start(f32[6,8,256]{2,1,0:T(8,128)S(1)} %get-tuple-element.40), channel_id=1, source_target_pairs={{0,1},{1,0},{2,3},{3,2},{4,5},{5,4},{6,7},{7,6},{8,9},{9,8},{10,11... | collective-permute-start | bytes 147464 | tf_op jit(solution)/shard_map/ppermute | solution.py:584
  10.6 3.0 %collective-permute-start.3 = (f32[6,8,256]{2,1,0:T(8,128)S(1)}, f32[6,8,256]{2,1,0:T(8,128)S(1)}, u32[]{:S(2)}, u32[]{:S(2)}) collective-permute-start(f32[6,8,256]{2,1,0:T(8,128)S(1)} %get-tuple-element.41), channel_id=1, source_target_pairs={{0,8},{1,2},{2,1},{3,4},{4,3},{5,6},{6,5},{7,127},{8,0},{9,10},{10... | collective-permute-start | bytes 147464 | tf_op jit(solution)/shard_map/ppermute | solution.py:584
  13.6 3.0 %shard_map.58 = (f32[64,8,256]{2,1,0:T(8,128)S(1)}, f32[4,8,384]{2,1,0:T(8,128)S(1)}, f32[4,8,8,128]{3,2,1,0:T(8,128)S(1)}, f32[64,8,256]{2,1,0:T(8,128)S(1)}, f32[64,8,256]{2,1,0:T(8,128)S(1)}) custom-call(f32[64,8,256]{2,1,0:T(8,128)S(1)} %get-tuple-element.42.refs_0_.refs_2_, f32[64,8,256]{2,1,0:T(8,128)S(1)} %get-tuple-element.43.refs_1_.refs_3_, ...), custom_call_target="tpu_custom_call" | custom-call | flops 20000000 | bytes 10000000 | tf_op jit(solution)/shard_map/pallas_call | solution.py:556
  16.6 0.0 collective-permute-done.2.refs_0_
  16.6 1.3 %collective-permute-done.3.refs_1_ = f32[6,8,256]{2,1,0:T(8,128)S(1)} collective-permute-done((f32[6,8,256]{2,1,0:T(8,128)S(1)}, f32[6,8,256]{2,1,0:T(8,128)S(1)}, u32[]{:S(2)}, u32[]{:S(2)}) %collective-permute-start.3) | collective-permute-done | bytes 49184 | tf_op jit(solution)/shard_map/ppermute | solution.py:584
  17.9 1.3 %shard_map.59 = f32[8,64,256]{2,1,0:T(8,128)} custom-call(f32[6,8,256]{2,1,0:T(8,128)S(1)} %collective-permute-done.2.refs_0_, f32[6,8,256]{2,1,0:T(8,128)S(1)} %collective-permute-done.3.refs_1_, f32[64,8,256]{2,1,0:T(8,128)S(1)} %get-tuple-element.42.refs_0_.refs_2_, f32[64,8,256]{2,1,0:T(8,128)S(1)} %get-tuple-element.43.refs_1_.refs_3_, ...), custom_call_target="tpu_custom_call" | custom-call | tf_op jit(solution)/shard_map/pallas_call | solution.py:616
Async XLA Ops:
  1.9 7.8 %collective-permute-start = (f32[4,8,128]{2,1,0:T(8,128)S(1)}, f32[4,8,128]{2,1,0:T(8,128)S(1)}, u32[]{:S(2)}, u32[]{:S(2)}) collective-permute-start(f32[4,8,128]{2,1,0:T(8,128)S(1)} %get-tuple-element.29), channel_id=1, source_target_pairs={{0,120},{1,121},{2,122},{3,123},{4,124},{5,125},{6,126},{7,127},{8... | collective-permute-start | bytes 49160 | tf_op jit(solution)/shard_map/ppermute | solution.py:584
  5.3 4.4 %collective-permute-start.1 = (f32[4,8,128]{2,1,0:T(8,128)S(1)}, f32[4,8,128]{2,1,0:T(8,128)S(1)}, u32[]{:S(2)}, u32[]{:S(2)}) collective-permute-start(f32[4,8,128]{2,1,0:T(8,128)S(1)} %get-tuple-element.30), channel_id=1, source_target_pairs={{0,8},{1,9},{2,10},{3,11},{4,12},{5,13},{6,14},{7,15},{8,0},{9,1},... | collective-permute-start | bytes 49160 | tf_op jit(solution)/shard_map/ppermute | solution.py:584
  10.0 6.6 %collective-permute-start.2 = (f32[6,8,256]{2,1,0:T(8,128)S(1)}, f32[6,8,256]{2,1,0:T(8,128)S(1)}, u32[]{:S(2)}, u32[]{:S(2)}) collective-permute-start(f32[6,8,256]{2,1,0:T(8,128)S(1)} %get-tuple-element.40), channel_id=1, source_target_pairs={{0,1},{1,0},{2,3},{3,2},{4,5},{5,4},{6,7},{7,6},{8,9},{9,8},{10,11... | collective-permute-start | bytes 147464 | tf_op jit(solution)/shard_map/ppermute | solution.py:584
  10.6 7.2 %collective-permute-start.3 = (f32[6,8,256]{2,1,0:T(8,128)S(1)}, f32[6,8,256]{2,1,0:T(8,128)S(1)}, u32[]{:S(2)}, u32[]{:S(2)}) collective-permute-start(f32[6,8,256]{2,1,0:T(8,128)S(1)} %get-tuple-element.41), channel_id=1, source_target_pairs={{0,8},{1,2},{2,1},{3,4},{4,3},{5,6},{6,5},{7,127},{8,0},{9,10},{10... | collective-permute-start | bytes 147464 | tf_op jit(solution)/shard_map/ppermute | solution.py:584

commit v15 on v13

--- a/solution.py
+++ b/solution.py
@@ -11,7 +11,7 @@
 F32 = jnp.float32
 VMEM = pl.BlockSpec(memory_space=pltpu.VMEM)
 LIMIT = 16 * 1024 * 1024
-CHUNKS = 2
+CHUNKS = 1
 GROUPS = ("c", "mu", "vw", "sk")
 KEPT = (2, 3, ROWS - 4, ROWS - 3)
 
@@ -367,7 +367,6 @@
 
 def diffuse_rows(get, first, count, beside=None):
     a, m, k, sy, step_z, twice_z, step_y, flux_y = [{} for _ in range(8)]
-    result = []
     last = lane_of() == LANES - 1
 
     def row_result(j):
@@ -390,7 +389,7 @@
             )
             return (value + across + (flux_z - above(flux_z))) * marker
 
-        result.append(each(finish, a[j][:2], m[j], k[j], sx, sy[j], twice_x, twice_y, step_z[j], total))
+        return each(finish, a[j][:2], m[j], k[j], sx, sy[j], twice_x, twice_y, step_z[j], total)
 
     for j in range(-1, count + 1):
         a[j], m[j], k[j], sy[j] = [get(name, first + j) for name in ("a", "m", "k", "sy")]
@@ -404,8 +403,7 @@
                 slope_flux, k[j - 1], k[j], opened, step_y[j - 1], sy[j - 1], sy[j], twice_z[j - 1], twice_z[j]
             )
         if j >= 1:
-            row_result(j - 1)
-    return result
+            yield row_result(j - 1)
 
 
 def tiles_of(ref, row, count):
@@ -463,13 +461,13 @@
             kept[i, :, t * LANES : (t + 1) * LANES] = tile
 
     def diffuse_block(block, carry):
-        first = jnp.minimum(3 + 10 * block, ROWS - 3 - 10)
-        for j, tiles in enumerate(diffuse_rows(get, first, 10, beside)):
+        first = jnp.minimum(3 + 12 * block, ROWS - 3 - 12)
+        for j, tiles in enumerate(diffuse_rows(get, first, 12, beside)):
             for t in range(2):
                 out[first + j, :, t * LANES : (t + 1) * LANES] = tiles[t]
         return carry
 
-    lax.fori_loop(0, 6, diffuse_block, 0)
+    lax.fori_loop(0, 5, diffuse_block, 0)
 
 
 def rim_kernel(*refs):

time: 19.3 us -> 19.4 us (level)
  transfers between devices with their start and end apart: 4 -> 4, of which waited for: 1 -> 1; matrix products, arithmetic and copies ran while one was open for 0% -> 0% of each run, Pallas kernels for 27% -> 26%
where the time goes in v15:
time: 19.4 us; the launch traced here: 19.3 us
  starting transfers between devices  9.15 us (47%)
  Pallas kernels  8.63 us (44%)
  waiting for transfers between devices  1.44 us (7%)
    ppermute x4, starting transfers between devices, move(): return lax.ppermute(x, ('lon', 'lat'), route)  9.15 us
    pallas_call x3, Pallas kernels, call(): pl.pallas_call(kernel, out_shape=[jax.ShapeDtypeStruct(s, F32) for s in s...  5.34 us
    pallas_call x1, Pallas kernels, shards(): pl.pallas_call(pack_kernel, out_shape=[jax.ShapeDtypeStruct(x.shape, x.dt...  2.02 us
    ppermute x4, waiting for transfers between devices, move(): return lax.ppermute(x, ('lon', 'lat'), route)  1.44 us
    pallas_call x1, Pallas kernels, shards(): pl.pallas_call(rim_kernel, out_shape=jax.ShapeDtypeStruct((8, ROWS, 2 * L...  1.26 us
  transfers between devices with their start and end apart: 4, of which 1 were waited for; matrix products, arithmetic and copies ran while one was open for 0% of the time, Pallas kernels for 26%

profile of v15, /device:TPU:39, one launch (start us, length us, event | category | flops | bytes accessed | tf_op | source)
XLA Modules:
  0.0 19.3 jit_solution(8985500272199057718)
XLA Ops:
  0.0 2.0 %shard_map.55 = (f32[8,64,256]{2,1,0:T(8,128)S(1)}, f32[12,64,256]{2,1,0:T(8,128)S(1)}, f32[8,64,256]{2,1,0:T(8,128)S(1)}, f32[4,64,256]{2,1,0:T(8,128)S(1)}, s3...) custom-call(f32[8,64,256]{2,1,0:T(8,128)} %bitcast.5, ...), custom_call_target="tpu_custom_call" | custom-call | tf_op jit(solution)/shard_map/pallas_call | solution.py:579
  2.0 3.3 %collective-permute-start = (f32[4,8,128]{2,1,0:T(8,128)S(1)}, f32[4,8,128]{2,1,0:T(8,128)S(1)}, u32[]{:S(2)}, u32[]{:S(2)}) collective-permute-start(f32[4,8,128]{2,1,0:T(8,128)S(1)} %get-tuple-element.28), channel_id=1, source_target_pairs={{0,120},{1,121},{2,122},{3,123},{4,124},{5,125},{6,126},{7,127},{8... | collective-permute-start | bytes 49160 | tf_op jit(solution)/shard_map/ppermute | solution.py:572
  5.4 2.3 %collective-permute-start.1 = (f32[4,8,128]{2,1,0:T(8,128)S(1)}, f32[4,8,128]{2,1,0:T(8,128)S(1)}, u32[]{:S(2)}, u32[]{:S(2)}) collective-permute-start(f32[4,8,128]{2,1,0:T(8,128)S(1)} %get-tuple-element.29), channel_id=1, source_target_pairs={{0,8},{1,9},{2,10},{3,11},{4,12},{5,13},{6,14},{7,15},{8,0},{9,1},... | collective-permute-start | bytes 49160 | tf_op jit(solution)/shard_map/ppermute | solution.py:572
  7.7 2.2 %shard_map.56 = (f32[64,8,256]{2,1,0:T(8,128)S(1)}, f32[64,8,256]{2,1,0:T(8,128)S(1)}, f32[64,8,256]{2,1,0:T(8,128)S(1)}, f32[64,8,256]{2,1,0:T(8,128)S(1)}, f32...) custom-call(f32[8,64,256]{2,1,0:T(8,128)S(1)} %get-tuple-element.32.ref, ...), custom_call_target="tpu_custom_call" | custom-call | flops 10000000 | bytes 6000000 | tf_op jit(solution)/shard_map/pallas_call | solution.py:544
  9.8 0.0 collective-permute-done.refs_0_.refs_6_
  9.9 0.0 collective-permute-done.1.refs_1_.refs_7_
  9.9 0.3 %shard_map.57 = (f32[6,8,256]{2,1,0:T(8,128)S(1)}, f32[6,8,256]{2,1,0:T(8,128)S(1)}) custom-call(f32[4,8,128]{2,1,0:T(8,128)S(1)} %collective-permute-done.refs_0_.refs_6_, f32[4,8,128]{2,1,0:T(8,128)S(1)} %collective-permute-done.1.refs_1_.refs_7_, ...), custom_call_target="tpu_custom_call", output_to_operand_aliasing={{0}: (4, {}), {1}: (5, {})} | custom-call | tf_op jit(solution)/shard_map/pallas_call | solution.py:544
  10.1 0.6 %collective-permute-start.2 = (f32[6,8,256]{2,1,0:T(8,128)S(1)}, f32[6,8,256]{2,1,0:T(8,128)S(1)}, u32[]{:S(2)}, u32[]{:S(2)}) collective-permute-start(f32[6,8,256]{2,1,0:T(8,128)S(1)} %get-tuple-element.39), channel_id=1, source_target_pairs={{0,1},{1,0},{2,3},{3,2},{4,5},{5,4},{6,7},{7,6},{8,9},{9,8},{10,11... | collective-permute-start | bytes 147464 | tf_op jit(solution)/shard_map/ppermute | solution.py:572
  10.8 2.9 %collective-permute-start.3 = (f32[6,8,256]{2,1,0:T(8,128)S(1)}, f32[6,8,256]{2,1,0:T(8,128)S(1)}, u32[]{:S(2)}, u32[]{:S(2)}) collective-permute-start(f32[6,8,256]{2,1,0:T(8,128)S(1)} %get-tuple-element.40), channel_id=1, source_target_pairs={{0,8},{1,2},{2,1},{3,4},{4,3},{5,6},{6,5},{7,127},{8,0},{9,10},{10... | collective-permute-start | bytes 147464 | tf_op jit(solution)/shard_map/ppermute | solution.py:572
  13.7 2.9 %shard_map.58 = (f32[64,8,256]{2,1,0:T(8,128)S(1)}, f32[4,8,384]{2,1,0:T(8,128)S(1)}, f32[4,8,8,128]{3,2,1,0:T(8,128)S(1)}, f32[64,8,256]{2,1,0:T(8,128)S(1)}) custom-call(f32[64,8,256]{2,1,0:T(8,128)S(1)} %get-tuple-element.41.refs_0_.refs_2_, f32[64,8,256]{2,1,0:T(8,128)S(1)} %get-tuple-element.42.refs_1_.refs_3_, ...), custom_call_target="tpu_custom_call" | custom-call | flops 20000000 | bytes 10000000 | tf_op jit(solution)/shard_map/pallas_call | solution.py:544
  16.6 0.0 collective-permute-done.2.refs_0_
  16.6 1.4 %collective-permute-done.3.refs_1_ = f32[6,8,256]{2,1,0:T(8,128)S(1)} collective-permute-done((f32[6,8,256]{2,1,0:T(8,128)S(1)}, f32[6,8,256]{2,1,0:T(8,128)S(1)}, u32[]{:S(2)}, u32[]{:S(2)}) %collective-permute-start.3) | collective-permute-done | bytes 49184 | tf_op jit(solution)/shard_map/ppermute | solution.py:572
  18.0 1.3 %shard_map.59 = f32[8,64,256]{2,1,0:T(8,128)} custom-call(f32[6,8,256]{2,1,0:T(8,128)S(1)} %collective-permute-done.2.refs_0_, f32[6,8,256]{2,1,0:T(8,128)S(1)} %collective-permute-done.3.refs_1_, f32[64,8,256]{2,1,0:T(8,128)S(1)} %get-tuple-element.41.refs_0_.refs_2_, f32[64,8,256]{2,1,0:T(8,128)S(1)} %get-tuple-element.42.refs_1_.refs_3_, ...), custom_call_target="tpu_custom_call" | custom-call | tf_op jit(solution)/shard_map/pallas_call | solution.py:604
Async XLA Ops:
  2.0 7.8 %collective-permute-start = (f32[4,8,128]{2,1,0:T(8,128)S(1)}, f32[4,8,128]{2,1,0:T(8,128)S(1)}, u32[]{:S(2)}, u32[]{:S(2)}) collective-permute-start(f32[4,8,128]{2,1,0:T(8,128)S(1)} %get-tuple-element.28), channel_id=1, source_target_pairs={{0,120},{1,121},{2,122},{3,123},{4,124},{5,125},{6,126},{7,127},{8... | collective-permute-start | bytes 49160 | tf_op jit(solution)/shard_map/ppermute | solution.py:572
  5.4 4.5 %collective-permute-start.1 = (f32[4,8,128]{2,1,0:T(8,128)S(1)}, f32[4,8,128]{2,1,0:T(8,128)S(1)}, u32[]{:S(2)}, u32[]{:S(2)}) collective-permute-start(f32[4,8,128]{2,1,0:T(8,128)S(1)} %get-tuple-element.29), channel_id=1, source_target_pairs={{0,8},{1,9},{2,10},{3,11},{4,12},{5,13},{6,14},{7,15},{8,0},{9,1},... | collective-permute-start | bytes 49160 | tf_op jit(solution)/shard_map/ppermute | solution.py:572
  10.1 6.4 %collective-permute-start.2 = (f32[6,8,256]{2,1,0:T(8,128)S(1)}, f32[6,8,256]{2,1,0:T(8,128)S(1)}, u32[]{:S(2)}, u32[]{:S(2)}) collective-permute-start(f32[6,8,256]{2,1,0:T(8,128)S(1)} %get-tuple-element.39), channel_id=1, source_target_pairs={{0,1},{1,0},{2,3},{3,2},{4,5},{5,4},{6,7},{7,6},{8,9},{9,8},{10,11... | collective-permute-start | bytes 147464 | tf_op jit(solution)/shard_map/ppermute | solution.py:572
  10.8 7.2 %collective-permute-start.3 = (f32[6,8,256]{2,1,0:T(8,128)S(1)}, f32[6,8,256]{2,1,0:T(8,128)S(1)}, u32[]{:S(2)}, u32[]{:S(2)}) collective-permute-start(f32[6,8,256]{2,1,0:T(8,128)S(1)} %get-tuple-element.40), channel_id=1, source_target_pairs={{0,8},{1,2},{2,1},{3,4},{4,3},{5,6},{6,5},{7,127},{8,0},{9,10},{10... | collective-permute-start | bytes 147464 | tf_op jit(solution)/shard_map/ppermute | solution.py:572

commit v16 on v13

--- a/solution.py
+++ b/solution.py
@@ -473,7 +473,7 @@
 
 
 def rim_kernel(*refs):
-    got_a, got_b = refs[0], refs[1]
+    got_b, got_a = refs[0], refs[1]
     fields = refs[2:7]
     strips, inner, kept, out, edges, sems = refs[7:]
     middle = pltpu.make_async_copy
@@ -610,7 +610,7 @@
             out_specs=pl.BlockSpec(memory_space=pl.ANY),
             scratch_shapes=[pltpu.VMEM((2, 8, 8, 2 * LANES), F32), pltpu.SemaphoreType.DMA((10,))],
             compiler_params=pltpu.CompilerParams(vmem_limit_bytes=LIMIT),
-        )(got_a, got_b, *rows, strips, inner, kept)
+        )(got_b, got_a, *rows, strips, inner, kept)
         return out.reshape(tracers.shape)
 
     return shards

time: 19.3 us -> 19.6 us (1.016)
  the two profiles are of different devices: /device:TPU:39 before, /device:TPU:36 now
where the time goes in v16:
time: 19.6 us; the launch traced here: 19.5 us
  starting transfers between devices  10.8 us (55%)
  Pallas kernels  8.59 us (44%)
    ppermute x4, starting transfers between devices, move(): return lax.ppermute(x, ('lon', 'lat'), route)  10.8 us
    pallas_call x3, Pallas kernels, call(): pl.pallas_call(kernel, out_shape=[jax.ShapeDtypeStruct(s, F32) for s in s...  5.36 us
    pallas_call x1, Pallas kernels, shards(): pl.pallas_call(pack_kernel, out_shape=[jax.ShapeDtypeStruct(x.shape, x.dt...  1.92 us
    pallas_call x1, Pallas kernels, shards(): pl.pallas_call(rim_kernel, out_shape=jax.ShapeDtypeStruct((8, ROWS, 2 * L...  1.31 us
  transfers between devices with their start and end apart: 4, of which 0 were waited for; matrix products, arithmetic and copies ran while one was open for 0% of the time, Pallas kernels for 26%

profile of v16, /device:TPU:36, one launch (start us, length us, event | category | flops | bytes accessed | tf_op | source)
XLA Modules:
  0.0 19.5 jit_solution(4772765980715733491)
XLA Ops:
  0.0 1.9 %shard_map.55 = (f32[8,64,256]{2,1,0:T(8,128)S(1)}, f32[12,64,256]{2,1,0:T(8,128)S(1)}, f32[8,64,256]{2,1,0:T(8,128)S(1)}, f32[4,64,256]{2,1,0:T(8,128)S(1)}, s3...) custom-call(f32[8,64,256]{2,1,0:T(8,128)} %bitcast.5, ...), custom_call_target="tpu_custom_call" | custom-call | tf_op jit(solution)/shard_map/pallas_call | solution.py:581
  1.9 4.9 %collective-permute-start = (f32[4,8,128]{2,1,0:T(8,128)S(1)}, f32[4,8,128]{2,1,0:T(8,128)S(1)}, u32[]{:S(2)}, u32[]{:S(2)}) collective-permute-start(f32[4,8,128]{2,1,0:T(8,128)S(1)} %get-tuple-element.28), channel_id=1, source_target_pairs={{0,120},{1,121},{2,122},{3,123},{4,124},{5,125},{6,126},{7,127},{8... | collective-permute-start | bytes 49160 | tf_op jit(solution)/shard_map/ppermute | solution.py:574
  6.9 0.0 collective-permute-start.1
  6.9 2.2 %shard_map.56 = (f32[64,8,256]{2,1,0:T(8,128)S(1)}, f32[64,8,256]{2,1,0:T(8,128)S(1)}, f32[64,8,256]{2,1,0:T(8,128)S(1)}, f32[64,8,256]{2,1,0:T(8,128)S(1)}, f32...) custom-call(f32[8,64,256]{2,1,0:T(8,128)S(1)} %get-tuple-element.32.ref, ...), custom_call_target="tpu_custom_call" | custom-call | flops 10000000 | bytes 6000000 | tf_op jit(solution)/shard_map/pallas_call | solution.py:546
  9.1 0.0 collective-permute-done.refs_0_.refs_6_
  9.1 0.0 collective-permute-done.1.refs_1_.refs_7_
  9.1 0.3 %shard_map.57 = (f32[6,8,256]{2,1,0:T(8,128)S(1)}, f32[6,8,256]{2,1,0:T(8,128)S(1)}) custom-call(f32[4,8,128]{2,1,0:T(8,128)S(1)} %collective-permute-done.refs_0_.refs_6_, f32[4,8,128]{2,1,0:T(8,128)S(1)} %collective-permute-done.1.refs_1_.refs_7_, ...), custom_call_target="tpu_custom_call", output_to_operand_aliasing={{0}: (4, {}), {1}: (5, {})} | custom-call | tf_op jit(solution)/shard_map/pallas_call | solution.py:546
  9.4 0.6 %collective-permute-start.2 = (f32[6,8,256]{2,1,0:T(8,128)S(1)}, f32[6,8,256]{2,1,0:T(8,128)S(1)}, u32[]{:S(2)}, u32[]{:S(2)}) collective-permute-start(f32[6,8,256]{2,1,0:T(8,128)S(1)} %get-tuple-element.39), channel_id=1, source_target_pairs={{0,8},{1,2},{2,1},{3,4},{4,3},{5,6},{6,5},{7,127},{8,0},{9,10},{10... | collective-permute-start | bytes 147464 | tf_op jit(solution)/shard_map/ppermute | solution.py:574
  10.0 5.2 %collective-permute-start.3 = (f32[6,8,256]{2,1,0:T(8,128)S(1)}, f32[6,8,256]{2,1,0:T(8,128)S(1)}, u32[]{:S(2)}, u32[]{:S(2)}) collective-permute-start(f32[6,8,256]{2,1,0:T(8,128)S(1)} %get-tuple-element.40), channel_id=1, source_target_pairs={{0,1},{1,0},{2,3},{3,2},{4,5},{5,4},{6,7},{7,6},{8,9},{9,8},{10,11... | collective-permute-start | bytes 147464 | tf_op jit(solution)/shard_map/ppermute | solution.py:574
  15.2 2.9 %shard_map.58 = (f32[64,8,256]{2,1,0:T(8,128)S(1)}, f32[4,8,384]{2,1,0:T(8,128)S(1)}, f32[4,8,8,128]{3,2,1,0:T(8,128)S(1)}, f32[64,8,256]{2,1,0:T(8,128)S(1)}) custom-call(f32[64,8,256]{2,1,0:T(8,128)S(1)} %get-tuple-element.41.refs_0_.refs_2_, f32[64,8,256]{2,1,0:T(8,128)S(1)} %get-tuple-element.42.refs_1_.refs_3_, ...), custom_call_target="tpu_custom_call" | custom-call | flops 20000000 | bytes 10000000 | tf_op jit(solution)/shard_map/pallas_call | solution.py:546
  18.1 0.0 collective-permute-done.2.refs_0_
  18.1 0.0 collective-permute-done.3.refs_1_
  18.1 1.3 %shard_map.59 = f32[8,64,256]{2,1,0:T(8,128)} custom-call(f32[6,8,256]{2,1,0:T(8,128)S(1)} %collective-permute-done.2.refs_0_, f32[6,8,256]{2,1,0:T(8,128)S(1)} %collective-permute-done.3.refs_1_, f32[64,8,256]{2,1,0:T(8,128)S(1)} %get-tuple-element.41.refs_0_.refs_2_, f32[64,8,256]{2,1,0:T(8,128)S(1)} %get-tuple-element.42.refs_1_.refs_3_, ...), custom_call_target="tpu_custom_call" | custom-call | tf_op jit(solution)/shard_map/pallas_call | solution.py:606
Async XLA Ops:
  1.9 7.1 %collective-permute-start = (f32[4,8,128]{2,1,0:T(8,128)S(1)}, f32[4,8,128]{2,1,0:T(8,128)S(1)}, u32[]{:S(2)}, u32[]{:S(2)}) collective-permute-start(f32[4,8,128]{2,1,0:T(8,128)S(1)} %get-tuple-element.28), channel_id=1, source_target_pairs={{0,120},{1,121},{2,122},{3,123},{4,124},{5,125},{6,126},{7,127},{8... | collective-permute-start | bytes 49160 | tf_op jit(solution)/shard_map/ppermute | solution.py:574
  6.9 2.2 %collective-permute-start.1 = (f32[4,8,128]{2,1,0:T(8,128)S(1)}, f32[4,8,128]{2,1,0:T(8,128)S(1)}, u32[]{:S(2)}, u32[]{:S(2)}) collective-permute-start(f32[4,8,128]{2,1,0:T(8,128)S(1)} %get-tuple-element.29), channel_id=1, source_target_pairs={{0,8},{1,9},{2,10},{3,11},{4,12},{5,13},{6,14},{7,15},{8,0},{9,1},... | collective-permute-start | bytes 49160 | tf_op jit(solution)/shard_map/ppermute | solution.py:574
  9.4 8.8 %collective-permute-start.2 = (f32[6,8,256]{2,1,0:T(8,128)S(1)}, f32[6,8,256]{2,1,0:T(8,128)S(1)}, u32[]{:S(2)}, u32[]{:S(2)}) collective-permute-start(f32[6,8,256]{2,1,0:T(8,128)S(1)} %get-tuple-element.39), channel_id=1, source_target_pairs={{0,8},{1,2},{2,1},{3,4},{4,3},{5,6},{6,5},{7,127},{8,0},{9,10},{10... | collective-permute-start | bytes 147464 | tf_op jit(solution)/shard_map/ppermute | solution.py:574
  10.0 8.2 %collective-permute-start.3 = (f32[6,8,256]{2,1,0:T(8,128)S(1)}, f32[6,8,256]{2,1,0:T(8,128)S(1)}, u32[]{:S(2)}, u32[]{:S(2)}) collective-permute-start(f32[6,8,256]{2,1,0:T(8,128)S(1)} %get-tuple-element.40), channel_id=1, source_target_pairs={{0,1},{1,0},{2,3},{3,2},{4,5},{5,4},{6,7},{7,6},{8,9},{9,8},{10,11... | collective-permute-start | bytes 147464 | tf_op jit(solution)/shard_map/ppermute | solution.py:574
